TPU v7x, 32 devices: a whole 2x2x4 slice. The times are simulated.
32 devices in a mesh: view: 2 (over y), seq: 16 (over z, x, core).
Axes of the slice: x: 2, y: 2, z: 4, core: 2. Of those that a mesh axis runs over, the one named last changes fastest.
Arguments:
- queries: bfloat16 [4, 2, 2048, 2048], P(None, 'view', 'seq'), may hold values from -6 to 6
- key_rows: bfloat16 [4, 2, 2048, 2048], P(None, 'view', 'seq'), may hold values from -6 to 6
- value_rows: bfloat16 [4, 2, 2048, 2048], P(None, 'view', 'seq'), may hold values from -6 to 6
- view_queries: bfloat16 [4, 2, 2048, 2048], P(None, 'view', 'seq'), may hold values from -6 to 6
Outputs:
- spatial: bfloat16 [4, 2, 2048, 2048], P(None, 'view', 'seq')
- joined: bfloat16 [4, 2, 2048, 2048], P(None, 'view', 'seq')
All inputs are finite; a program needn't handle non-finite values.
Results may differ from a plain program's by a relative error of at most 0.0064.
Values may be sent and summed in bfloat16 or wider, within the bound.
No kernel may reach another device: no remote copies, remote signals or barrier semaphores. Data moves between devices by JAX's collectives and lax.ppermute only.
A program may use at most 128 MiB of HBM per device.

v0:
```python
import jax
import jax.numpy as jnp
from jax import lax
from jax.sharding import PartitionSpec as P

HEADS = 32


def split_heads(tokens):
    batch_size, single, local_len, model_width = tokens.shape
    shaped = tokens.reshape(batch_size, local_len, HEADS, model_width // HEADS)
    return shaped.transpose(1, 0, 2, 3).reshape(local_len, batch_size * HEADS, model_width // HEADS)


def merge_heads(pairs, batch_size):
    local_len, pair_count, head_width = pairs.shape
    shaped = pairs.reshape(local_len, batch_size, pair_count // batch_size, head_width)
    return shaped.transpose(1, 0, 2, 3).reshape(
        batch_size, 1, local_len, pair_count // batch_size * head_width
    )


def attend(query_pairs, key_pairs, value_pairs):
    length, pair_count, head_width = query_pairs.shape
    block_rows = min(512, length)
    score_scale = head_width ** (-0.5)

    def one_block(query_block):
        scores = (
            jnp.einsum("qpe,kpe->pqk", query_block, key_pairs, preferred_element_type=jnp.float32)
            * score_scale
        )
        scores = scores - jnp.max(scores, axis=-1, keepdims=True)
        expo = jnp.exp(scores)
        weights = (expo / jnp.sum(expo, axis=-1, keepdims=True)).astype(jnp.bfloat16)
        result = jnp.einsum(
            "pqk,kpe->qpe", weights, value_pairs, preferred_element_type=jnp.float32
        )
        return result.astype(jnp.bfloat16)

    blocks = query_pairs.reshape(length // block_rows, block_rows, pair_count, head_width)
    return lax.map(one_block, blocks).reshape(length, pair_count, head_width)


def view_weights(cross_query, key_part):
    batch_size, view_count, few_rows, model_width = cross_query.shape
    head_width = model_width // HEADS
    split_shape = (batch_size, view_count, few_rows, HEADS, head_width)
    score_scale = head_width ** (-0.5)
    scores = (
        jnp.einsum(
            "bvngd,bwngd->bngvw",
            cross_query.reshape(split_shape),
            key_part.reshape(split_shape),
            preferred_element_type=jnp.float32,
        )
        * score_scale
    )
    scores = scores - jnp.max(scores, axis=-1, keepdims=True)
    expo = jnp.exp(scores)
    return (expo / jnp.sum(expo, axis=-1, keepdims=True)).astype(jnp.bfloat16)


def apply_weights(weights, output_part):
    batch_size, view_count, few_rows, model_width = output_part.shape
    head_width = model_width // HEADS
    split_shape = (batch_size, view_count, few_rows, HEADS, head_width)
    result = jnp.einsum(
        "bngvw,bwngd->bvngd",
        weights,
        output_part.reshape(split_shape),
        preferred_element_type=jnp.float32,
    )
    return result.astype(jnp.bfloat16).reshape(batch_size, view_count, few_rows, model_width)


def local(queries, key_rows, value_rows, view_queries):
    batch_size = queries.shape[0]
    query_pairs, key_pairs, value_pairs = (
        lax.all_to_all(split_heads(queries), "seq", split_axis=1, concat_axis=0, tiled=True),
        lax.all_to_all(split_heads(key_rows), "seq", split_axis=1, concat_axis=0, tiled=True),
        lax.all_to_all(split_heads(value_rows), "seq", split_axis=1, concat_axis=0, tiled=True),
    )
    output_pairs = attend(query_pairs, key_pairs, value_pairs)
    returned = lax.all_to_all(output_pairs, "seq", split_axis=0, concat_axis=1, tiled=True)
    spatial = merge_heads(returned, batch_size)
    cross_query, key_views, output_views = (
        lax.all_to_all(view_queries, "view", split_axis=2, concat_axis=1, tiled=True),
        lax.all_to_all(key_rows, "view", split_axis=2, concat_axis=1, tiled=True),
        lax.all_to_all(spatial, "view", split_axis=2, concat_axis=1, tiled=True),
    )
    mixing = view_weights(cross_query, key_views)
    combined = apply_weights(mixing, output_views)
    joined = lax.all_to_all(combined, "view", split_axis=1, concat_axis=2, tiled=True)
    return (spatial, joined)


def solution(mesh):
    placed = (
        P(None, "view", "seq", None),
        P(None, "view", "seq", None),
        P(None, "view", "seq", None),
        P(None, "view", "seq", None),
    )
    return jax.shard_map(
        local,
        mesh=mesh,
        in_specs=placed,
        out_specs=(P(None, "view", "seq", None), P(None, "view", "seq", None)),
        check_vma=False,
    )
```

profile of v0, /device:TPU:0, one launch (start us, length us, event | category | flops | bytes accessed | tf_op | source)
XLA Modules:
  0.0 500.0 jit_solution(14389359778924005395)
XLA Ops:
  0.6 3.9 copy.87
  4.6 7.4 %all-to-all-start = ((bf16[128,128,64]{0,2,1:T(8,128)(2,1)}), bf16[128,128,64]{0,2,1:T(8,128)(2,1)}, u32[]{:S(2)}, u32[]{:S(2)}) async-start(bf16[128,128,64]{0,2,1:T(8,128)(2,1)} %bitcast.5), calls=%async_computation | async-start | bytes 4194304 | tf_op jit(solution)/shard_map/all_to_all | solution.py:80
  12.0 0.0 copy-start.2
  12.0 4.1 copy.91
  16.1 37.1 %all-to-all-done = bf16[128,128,64]{0,2,1:T(8,128)(2,1)} async-done(((bf16[128,128,64]{0,2,1:T(8,128)(2,1)}), bf16[128,128,64]{0,2,1:T(8,128)(2,1)}, u32[]{:S(2)}, u32[]{:S(2)}) %all-to-all-start) | async-done | bytes 2097184 | tf_op jit(solution)/shard_map/all_to_all | solution.py:80
  53.1 11.3 %all-to-all-start.2 = ((bf16[128,128,64]{0,2,1:T(8,128)(2,1)}), bf16[128,128,64]{0,2,1:T(8,128)(2,1)}, u32[]{:S(2)}, u32[]{:S(2)}) async-start(bf16[128,128,64]{0,2,1:T(8,128)(2,1)} %bitcast.98), calls=%async_computation.2 | async-start | bytes 4194304 | tf_op jit(solution)/shard_map/all_to_all | solution.py:82
  64.4 0.0 copy-done.2
  64.4 2.5 copy.89
  66.9 38.7 %all-to-all-done.2 = bf16[128,128,64]{0,2,1:T(8,128)(2,1)} async-done(((bf16[128,128,64]{0,2,1:T(8,128)(2,1)}), bf16[128,128,64]{0,2,1:T(8,128)(2,1)}, u32[]{:S(2)}, u32[]{:S(2)}) %all-to-all-start.2) | async-done | bytes 2097184 | tf_op jit(solution)/shard_map/all_to_all | solution.py:82
  105.6 11.2 %all-to-all-start.1 = ((bf16[128,128,64]{0,2,1:T(8,128)(2,1)}), bf16[128,128,64]{0,2,1:T(8,128)(2,1)S(1)}, u32[]{:S(2)}, u32[]{:S(2)}) async-start(bf16[128,128,64]{0,2,1:T(8,128)(2,1)} %bitcast.99), calls=%async_computation.1 | async-start | bytes 4194304 | tf_op jit(solution)/shard_map/all_to_all | solution.py:81
  116.8 4.6 copy.100
  121.4 36.5 %all-to-all-done.1 = bf16[128,128,64]{0,2,1:T(8,128)(2,1)S(1)} async-done(((bf16[128,128,64]{0,2,1:T(8,128)(2,1)}), bf16[128,128,64]{0,2,1:T(8,128)(2,1)S(1)}, u32[]{:S(2)}, u32[]{:S(2)}) %all-to-all-start.1) | async-done | bytes 2097184 | tf_op jit(solution)/shard_map/all_to_all | solution.py:81
  157.9 0.0 copy-start.3
  157.9 1.3 copy-done.3
  159.2 3.8 all-to-all-start.5
  163.0 4.5 copy.102
  167.6 4.3 copy.144
  171.8 4.1 reshape.69
  176.0 0.0 copy-start.4
  176.0 3.5 copy.93
  179.5 3.5 copy.142
  183.0 0.0 copy-done.4
  183.0 1.9 copy.143
  184.9 4.1 all-to-all-done.5
  189.0 0.0 copy-start
  189.0 5.0 all-to-all-start.6
  194.0 0.0 copy-done
  194.0 125.6 %while.10 = (s32[]{:T(128)}, bf16[4,512,8,64]{1,3,2,0:T(8,128)(2,1)}, bf16[4,512,8,64]{1,3,2,0:T(8,128)(2,1)}, bf16[2048,8,64]{0,2,1:T(8,128)(2,1)}, bf16[2048,8,64]{0,2,1:T(8,128)(2,1)}, /*index=5*/s32[]{:T(128)}) while((s32[]{:T(128)}, bf16[4,512,8,64]{1,3,2,0:T(8,128)(2,1)}, bf16[4,512,8,64]{1,3,2,0:T(8,128)(2,1)}, ...), condition=%wide.region_3.4_spmd, body=%wide.region_0.3_spmd.sunk | while | flops 2189690880 | bytes 72385608 | solution.py:42
  194.1 16.7 %fusion.54 = (f32[8,512]{1,0:T(8,128)S(1)}, f32[8,512,2048]{2,1,0:T(8,128)}) fusion(bf16[2048,8,64]{0,2,1:T(8,128)(2,1)} %get-tuple-element.129, bf16[4,512,8,64]{1,3,2,0:T(8,128)(2,1)} %get-tuple-element.128, s32[]{:T(128)} %get-tuple-element.120), kind=kOutput, calls=%fused_computation.31.clone.1 | convolution fusion | flops 1098909696 | bytes 36192768 | tf_op jit(solution)/shard_map/while/body/eval_jaxpr/sub | solution.py:33
  210.8 14.7 %fusion.55 = bf16[4,512,8,64]{1,3,2,0:T(8,128)(2,1)} fusion(bf16[4,512,8,64]{1,3,2,0:T(8,128)(2,1)} %get-tuple-element.121, s32[]{:T(128)} %get-tuple-element.120, bf16[2048,8,64]{0,2,1:T(8,128)(2,1)} %get-tuple-element.130, f32[8,512,2048]{2,1,0:T(8,128)} %get-tuple-element.112, f32[8,512]{1,0:T(8,128)S(1)} %get-tuple-element.113), kind=kOutput, calls=%fused_computation.10.clone.1 | convolution fusion | flops 1090781184 | bytes 36192768 | tf_op jit(solution)/shard_map/while/body/eval_jaxpr/pqk,kpe->qpe/dot_general | solution.py:36
  225.5 16.7 %fusion.54 = (f32[8,512]{1,0:T(8,128)S(1)}, f32[8,512,2048]{2,1,0:T(8,128)}) fusion(bf16[2048,8,64]{0,2,1:T(8,128)(2,1)} %get-tuple-element.129, bf16[4,512,8,64]{1,3,2,0:T(8,128)(2,1)} %get-tuple-element.128, s32[]{:T(128)} %get-tuple-element.120), kind=kOutput, calls=%fused_computation.31.clone.1 | convolution fusion | flops 1098909696 | bytes 36192768 | tf_op jit(solution)/shard_map/while/body/eval_jaxpr/sub | solution.py:33
  242.2 14.7 %fusion.55 = bf16[4,512,8,64]{1,3,2,0:T(8,128)(2,1)} fusion(bf16[4,512,8,64]{1,3,2,0:T(8,128)(2,1)} %get-tuple-element.121, s32[]{:T(128)} %get-tuple-element.120, bf16[2048,8,64]{0,2,1:T(8,128)(2,1)} %get-tuple-element.130, f32[8,512,2048]{2,1,0:T(8,128)} %get-tuple-element.112, f32[8,512]{1,0:T(8,128)S(1)} %get-tuple-element.113), kind=kOutput, calls=%fused_computation.10.clone.1 | convolution fusion | flops 1090781184 | bytes 36192768 | tf_op jit(solution)/shard_map/while/body/eval_jaxpr/pqk,kpe->qpe/dot_general | solution.py:36
  256.9 16.7 %fusion.54 = (f32[8,512]{1,0:T(8,128)S(1)}, f32[8,512,2048]{2,1,0:T(8,128)}) fusion(bf16[2048,8,64]{0,2,1:T(8,128)(2,1)} %get-tuple-element.129, bf16[4,512,8,64]{1,3,2,0:T(8,128)(2,1)} %get-tuple-element.128, s32[]{:T(128)} %get-tuple-element.120), kind=kOutput, calls=%fused_computation.31.clone.1 | convolution fusion | flops 1098909696 | bytes 36192768 | tf_op jit(solution)/shard_map/while/body/eval_jaxpr/sub | solution.py:33
  273.6 14.7 %fusion.55 = bf16[4,512,8,64]{1,3,2,0:T(8,128)(2,1)} fusion(bf16[4,512,8,64]{1,3,2,0:T(8,128)(2,1)} %get-tuple-element.121, s32[]{:T(128)} %get-tuple-element.120, bf16[2048,8,64]{0,2,1:T(8,128)(2,1)} %get-tuple-element.130, f32[8,512,2048]{2,1,0:T(8,128)} %get-tuple-element.112, f32[8,512]{1,0:T(8,128)S(1)} %get-tuple-element.113), kind=kOutput, calls=%fused_computation.10.clone.1 | convolution fusion | flops 1090781184 | bytes 36192768 | tf_op jit(solution)/shard_map/while/body/eval_jaxpr/pqk,kpe->qpe/dot_general | solution.py:36
  288.3 16.7 %fusion.54 = (f32[8,512]{1,0:T(8,128)S(1)}, f32[8,512,2048]{2,1,0:T(8,128)}) fusion(bf16[2048,8,64]{0,2,1:T(8,128)(2,1)} %get-tuple-element.129, bf16[4,512,8,64]{1,3,2,0:T(8,128)(2,1)} %get-tuple-element.128, s32[]{:T(128)} %get-tuple-element.120), kind=kOutput, calls=%fused_computation.31.clone.1 | convolution fusion | flops 1098909696 | bytes 36192768 | tf_op jit(solution)/shard_map/while/body/eval_jaxpr/sub | solution.py:33
  305.0 14.7 %fusion.55 = bf16[4,512,8,64]{1,3,2,0:T(8,128)(2,1)} fusion(bf16[4,512,8,64]{1,3,2,0:T(8,128)(2,1)} %get-tuple-element.121, s32[]{:T(128)} %get-tuple-element.120, bf16[2048,8,64]{0,2,1:T(8,128)(2,1)} %get-tuple-element.130, f32[8,512,2048]{2,1,0:T(8,128)} %get-tuple-element.112, f32[8,512]{1,0:T(8,128)S(1)} %get-tuple-element.113), kind=kOutput, calls=%fused_computation.10.clone.1 | convolution fusion | flops 1090781184 | bytes 36192768 | tf_op jit(solution)/shard_map/while/body/eval_jaxpr/pqk,kpe->qpe/dot_general | solution.py:36
  319.7 5.7 %copy.114 = bf16[4,512,8,64]{3,2,1,0:T(8,128)(2,1)} copy(bf16[4,512,8,64]{1,3,2,0:T(8,128)(2,1)} %get-tuple-element.29) | data formatting | bytes 4194304 | tf_op jit(solution)/shard_map/reshape | solution.py:42
  325.3 0.0 copy-start.1
  325.3 7.7 %reshape.85 = bf16[16,2,32768]{2,1,0:T(2,128)(2,1)} reshape(bf16[2048,8,64]{2,1,0:T(8,128)(2,1)} %bitcast.95) | data formatting | bytes 4194304
  333.0 0.0 all-to-all-done.6
  333.0 10.8 %all-to-all-start.3 = ((bf16[16,2,32768]{2,1,0:T(2,128)(2,1)}), bf16[16,2,32768]{2,1,0:T(2,128)(2,1)}, u32[]{:S(2)}, u32[]{:S(2)}) async-start(bf16[16,2,32768]{2,1,0:T(2,128)(2,1)} %reshape.85), calls=%async_computation.3 | async-start | bytes 4194304 | tf_op jit(solution)/shard_map/all_to_all | solution.py:85
  343.8 0.0 copy-done.1
  343.8 4.6 reshape.82
  348.4 7.0 %reshape.83 = bf16[4,2,64,32,64]{4,3,0,2,1:T(8,128)(2,1)} reshape(bf16[4,1,128,2048]{3,0,1,2:T(4,128)(2,1)} %all-to-all-done.6) | data formatting | bytes 4194304 | tf_op jit(solution)/shard_map/reshape | solution.py:54
  355.4 29.6 %all-to-all-done.3 = bf16[16,2,32768]{2,1,0:T(2,128)(2,1)} async-done(((bf16[16,2,32768]{2,1,0:T(2,128)(2,1)}), bf16[16,2,32768]{2,1,0:T(2,128)(2,1)}, u32[]{:S(2)}, u32[]{:S(2)}) %all-to-all-start.3) | async-done | bytes 2097184 | tf_op jit(solution)/shard_map/all_to_all | solution.py:85
  385.0 7.4 %reshape.86 = bf16[2048,8,64]{2,1,0:T(8,128)(2,1)} reshape(bf16[16,2,32768]{2,1,0:T(2,128)(2,1)} %all-to-all-done.3) | data formatting | bytes 4194304
  392.4 4.1 copy.97
  396.5 2.9 copy.98
  399.4 5.0 %all-to-all-start.4 = ((bf16[4,1,128,2048]{3,0,1,2:T(4,128)(2,1)}), bf16[4,1,128,2048]{3,0,1,2:T(4,128)(2,1)}, u32[]{:S(2)}, u32[]{:S(2)}) async-start(bf16[4,1,128,2048]{3,0,1,2:T(4,128)(2,1)} %copy.98), calls=%async_computation.4 | async-start | bytes 4194304 | tf_op jit(solution)/shard_map/all_to_all | solution.py:90
  404.4 31.7 %fusion.37 = (f32[4,64,32,2]{3,2,1,0:T(8,128)}, f32[4,64,32,2,2]{3,4,2,1,0:T(2,128)}) fusion(bf16[4,2,64,32,64]{4,3,0,2,1:T(8,128)(2,1)} %reshape.83, bf16[4,2,64,32,64]{4,3,0,2,1:T(8,128)(2,1)} %reshape.82), kind=kOutput, calls=%fused_computation.32 | convolution fusion | flops 4292609 | bytes 4390912 | tf_op jit(solution)/shard_map/sub | solution.py:59
  436.1 0.0 all-to-all-done.4
  436.1 7.0 %reshape.81 = bf16[4,2,64,32,64]{4,3,0,2,1:T(8,128)(2,1)} reshape(bf16[4,1,128,2048]{3,0,1,2:T(4,128)(2,1)} %all-to-all-done.4) | data formatting | bytes 4194304 | tf_op jit(solution)/shard_map/reshape | solution.py:71
  443.2 13.2 %fusion.28 = bf16[4,2,64,32,64]{4,1,3,2,0:T(2,128)(2,1)S(1)} fusion(f32[4,64,32,2,2]{3,4,2,1,0:T(2,128)} %get-tuple-element.78, f32[4,64,32,2]{3,2,1,0:T(8,128)} %get-tuple-element.77, bf16[4,2,64,32,64]{4,3,0,2,1:T(8,128)(2,1)} %reshape.81), kind=kOutput, calls=%fused_computation.24 | convolution fusion | flops 5308416 | bytes 4390912 | tf_op jit(solution)/shard_map/bngvw,bwngd->bvngd/dot_general | solution.py:68
  456.3 2.7 copy.123
  459.0 6.7 %reshape.84 = bf16[4,2,64,2048]{3,2,0,1:T(8,128)(2,1)} reshape(bf16[4,2,64,32,64]{4,3,2,0,1:T(8,128)(2,1)} %copy.123) | data formatting | bytes 4194304 | tf_op jit(solution)/shard_map/reshape | solution.py:74
  465.8 4.8 all-to-all-start.7
  470.6 2.6 copy.111
  473.2 23.6 %all-to-all-done.7 = bf16[4,2,64,2048]{3,2,0,1:T(8,128)(2,1)} async-done(((bf16[4,2,64,2048]{3,2,0,1:T(8,128)(2,1)}), bf16[4,2,64,2048]{3,2,0,1:T(8,128)(2,1)}, u32[]{:S(2)}, u32[]{:S(2)}) %all-to-all-start.7) | async-done | bytes 2097184 | tf_op jit(solution)/shard_map/all_to_all | solution.py:94
  496.8 3.2 copy.110
  (1 shorter events, 0.0 us)
Async XLA Ops:
  4.6 48.6 %all-to-all-start = ((bf16[128,128,64]{0,2,1:T(8,128)(2,1)}), bf16[128,128,64]{0,2,1:T(8,128)(2,1)}, u32[]{:S(2)}, u32[]{:S(2)}) async-start(bf16[128,128,64]{0,2,1:T(8,128)(2,1)} %bitcast.5), calls=%async_computation | async-start | bytes 4194304 | tf_op jit(solution)/shard_map/all_to_all | solution.py:80
  12.0 52.4 %copy-start.2 = (bf16[4,1,128,2048]{3,2,1,0:T(8,128)(2,1)S(1)}, bf16[4,1,128,2048]{3,2,1,0:T(8,128)(2,1)}, u32[]{:S(2)}) copy-start(bf16[4,1,128,2048]{3,2,1,0:T(8,128)(2,1)} %param.7) | copy-start | bytes 6291460
  53.1 52.4 %all-to-all-start.2 = ((bf16[128,128,64]{0,2,1:T(8,128)(2,1)}), bf16[128,128,64]{0,2,1:T(8,128)(2,1)}, u32[]{:S(2)}, u32[]{:S(2)}) async-start(bf16[128,128,64]{0,2,1:T(8,128)(2,1)} %bitcast.98), calls=%async_computation.2 | async-start | bytes 4194304 | tf_op jit(solution)/shard_map/all_to_all | solution.py:82
  105.6 52.3 %all-to-all-start.1 = ((bf16[128,128,64]{0,2,1:T(8,128)(2,1)}), bf16[128,128,64]{0,2,1:T(8,128)(2,1)S(1)}, u32[]{:S(2)}, u32[]{:S(2)}) async-start(bf16[128,128,64]{0,2,1:T(8,128)(2,1)} %bitcast.99), calls=%async_computation.1 | async-start | bytes 4194304 | tf_op jit(solution)/shard_map/all_to_all | solution.py:81
  157.9 1.3 copy-start.3
  159.2 29.8 %all-to-all-start.5 = ((bf16[4,1,128,2048]{3,0,1,2:T(4,128)(2,1)}), bf16[4,1,128,2048]{3,0,1,2:T(4,128)(2,1)S(1)}, u32[]{:S(2)}, u32[]{:S(2)}) async-start(bf16[4,1,128,2048]{3,0,1,2:T(4,128)(2,1)} %copy.100), calls=%async_computation.5 | async-start | bytes 4194304 | tf_op jit(solution)/shard_map/all_to_all | solution.py:88
  176.0 7.0 %copy-start.4 = (bf16[128,128,64]{0,2,1:T(8,128)(2,1)S(1)}, bf16[128,128,64]{0,2,1:T(8,128)(2,1)}, u32[]{:S(2)}) copy-start(bf16[128,128,64]{0,2,1:T(8,128)(2,1)} %copy-done.3) | copy-start | bytes 6291460
  189.0 5.0 copy-start
  189.0 144.0 %all-to-all-start.6 = ((bf16[4,1,128,2048]{3,0,1,2:T(4,128)(2,1)}), bf16[4,1,128,2048]{3,0,1,2:T(4,128)(2,1)}, u32[]{:S(2)}, u32[]{:S(2)}) async-start(bf16[4,1,128,2048]{3,0,1,2:T(4,128)(2,1)} %copy.102), calls=%async_computation.6 | async-start | bytes 4194304 | tf_op jit(solution)/shard_map/all_to_all | solution.py:89
  325.3 18.5 %copy-start.1 = (bf16[4,1,128,2048]{3,0,1,2:T(4,128)(2,1)S(1)}, bf16[4,1,128,2048]{3,0,1,2:T(4,128)(2,1)}, u32[]{:S(2)}) copy-start(bf16[4,1,128,2048]{3,0,1,2:T(4,128)(2,1)} %copy-done) | copy-start | bytes 6291460
  333.0 52.0 %all-to-all-start.3 = ((bf16[16,2,32768]{2,1,0:T(2,128)(2,1)}), bf16[16,2,32768]{2,1,0:T(2,128)(2,1)}, u32[]{:S(2)}, u32[]{:S(2)}) async-start(bf16[16,2,32768]{2,1,0:T(2,128)(2,1)} %reshape.85), calls=%async_computation.3 | async-start | bytes 4194304 | tf_op jit(solution)/shard_map/all_to_all | solution.py:85
  399.4 36.8 %all-to-all-start.4 = ((bf16[4,1,128,2048]{3,0,1,2:T(4,128)(2,1)}), bf16[4,1,128,2048]{3,0,1,2:T(4,128)(2,1)}, u32[]{:S(2)}, u32[]{:S(2)}) async-start(bf16[4,1,128,2048]{3,0,1,2:T(4,128)(2,1)} %copy.98), calls=%async_computation.4 | async-start | bytes 4194304 | tf_op jit(solution)/shard_map/all_to_all | solution.py:90
  465.8 31.0 %all-to-all-start.7 = ((bf16[4,2,64,2048]{3,2,0,1:T(8,128)(2,1)}), bf16[4,2,64,2048]{3,2,0,1:T(8,128)(2,1)}, u32[]{:S(2)}, u32[]{:S(2)}) async-start(bf16[4,2,64,2048]{3,2,0,1:T(8,128)(2,1)} %reshape.84), calls=%async_computation.7 | async-start | bytes 4194304 | tf_op jit(solution)/shard_map/all_to_all | solution.py:94
where the time goes:
time: 506 us; the launch traced here: 500 us
  matrix products  171 us (34%)
  waiting for transfers between devices  170 us (34%)
  local copies, waits for them, and re-layouts  99.9 us (20%)
  starting transfers between devices  59.3 us (12%)
    sub x4, matrix products, one_block(): scores = scores - jnp.max(scores, axis=-1, keepdims=True)  66.9 us
    dot_general x4, matrix products, one_block(): jnp.einsum('pqk,kpe->qpe', weights, value_pairs, preferred_element_type=j...  58.7 us
    unnamed x18, local copies, waits for them, and re-layouts  38.7 us
    all_to_all x1, waiting for transfers between devices, local(): lax.all_to_all(split_heads(value_rows), 'seq', split_axis=1, concat_axis=...  38.7 us
    all_to_all x1, waiting for transfers between devices, local(): lax.all_to_all(split_heads(queries), 'seq', split_axis=1, concat_axis=0,...  37.1 us
    all_to_all x1, waiting for transfers between devices, local(): lax.all_to_all(split_heads(key_rows), 'seq', split_axis=1, concat_axis=0,...  36.5 us
    sub x1, matrix products, view_weights(): scores = scores - jnp.max(scores, axis=-1, keepdims=True)  31.7 us
    all_to_all x1, waiting for transfers between devices, local(): lax.all_to_all(output_pairs, 'seq', split_axis=0, concat_axis=1, tiled=True)  29.6 us
  transfers between devices with their start and end apart: 8, of which 6 were waited for; matrix products, arithmetic and copies ran while one was open for 44% of the time, Pallas kernels for 0%

commit v1 on v0

v1 whole, which is shorter than its diff:
```python
import functools
import math

import jax
import jax.numpy as jnp
from jax import lax
from jax.experimental import pallas as pl
from jax.experimental.pallas import tpu as pltpu
from jax.sharding import PartitionSpec as P

HEADS = 32
LANES = 128
VMEM_LIMIT = 48 * 1024 * 1024


def block_place(me, shift, lane_blocks, per_chunk):
    other = me ^ shift
    video = 0 if per_chunk == 1 else other // lane_blocks
    column = other if per_chunk == 1 else other % lane_blocks
    return video, pl.ds(pl.multiple_of(column * LANES, LANES), LANES)


def source_copies(me, first_batch, per_chunk, sources, targets, sems):
    rows = sources[0].shape[2]
    lane_blocks = sources[0].shape[3] // LANES
    copies = []
    for shift, target in enumerate(targets):
        video, lanes = block_place(me, shift, lane_blocks, per_chunk)
        for which, source in enumerate(sources):
            copies.append(
                pltpu.make_async_copy(
                    source.at[first_batch + video, 0, :, lanes],
                    target.at[pl.ds(which * rows, rows), :],
                    sems.at[len(copies)],
                )
            )
    return copies


def pack_kernel(first_batch, per_chunk, me_ref, q_ref, k_ref, v_ref, *refs):
    targets, sems = refs[:-1], refs[-1]
    copies = source_copies(
        me_ref[0], first_batch, per_chunk, (q_ref, k_ref, v_ref), targets, sems
    )
    for copy in copies:
        copy.start()
    for copy in copies:
        copy.wait()


def pack(me, sources, first_batch, per_chunk, parts):
    rows = sources[0].shape[2]
    dtype = sources[0].dtype
    anywhere = pl.BlockSpec(memory_space=pl.ANY)
    return pl.pallas_call(
        functools.partial(pack_kernel, first_batch, per_chunk),
        in_specs=[pl.BlockSpec(memory_space=pltpu.SMEM)] + [anywhere] * 3,
        out_specs=[anywhere] * parts,
        out_shape=[jax.ShapeDtypeStruct((3 * rows, LANES), dtype)] * parts,
        scratch_shapes=[pltpu.SemaphoreType.DMA((3 * parts,))],
        cost_estimate=pl.CostEstimate(
            flops=0, bytes_accessed=parts * 3 * rows * LANES * 4, transcendentals=0
        ),
        name="pack",
    )(me, *sources)


def attend_kernel(parts, rows, group, next_batch, per_chunk, me_ref, *refs):
    blocks, refs = refs[:parts], refs[parts:]
    sources = ()
    if next_batch is not None:
        sources, refs = refs[:3], refs[3:]
    targets, refs = refs[:parts], refs[parts:]
    query_scr, key_scr, value_scr, out_scr, in_sems, pack_sems, out_sems = refs
    length = parts * rows
    head_width = LANES // 2
    first, second = pl.ds(0, LANES), pl.ds(LANES, LANES)

    loads = []
    for part, block in enumerate(blocks):
        here = pl.ds(part * rows, rows)
        for which, target in (
            (0, query_scr.at[here, :]),
            (1, key_scr.at[here, first]),
            (1, key_scr.at[here, second]),
            (2, value_scr.at[here, first]),
        ):
            loads.append(
                pltpu.make_async_copy(
                    block.at[pl.ds(which * rows, rows), :], target, in_sems.at[len(loads)]
                )
            )
    for copy in loads:
        copy.start()
    packs = []
    if next_batch is not None:
        packs = source_copies(me_ref[0], next_batch, per_chunk, sources, targets, pack_sems)
    for copy in packs:
        copy.start()
    value_scr[:, LANES : 2 * LANES] = jnp.ones((length, LANES), value_scr.dtype)
    for copy in loads:
        copy.wait()

    block_rows = group * rows
    lane = lax.broadcasted_iota(jnp.int32, (block_rows, 2 * LANES), 1) % LANES
    own = lax.broadcasted_iota(jnp.int32, (block_rows, LANES), 1) // head_width

    def one_block(step, carry):
        here = pl.ds(pl.multiple_of(step * block_rows, block_rows), block_rows)
        query = query_scr[here, :].astype(jnp.float32)
        query = query * (head_width ** (-0.5) * math.log2(math.e))
        high = query.astype(jnp.bfloat16)
        low = (query - high.astype(jnp.float32)).astype(jnp.bfloat16)
        pair = jnp.concatenate([high, low], axis=1)
        results = []
        for head in range(2):
            masked = jnp.where((lane // head_width) == head, pair, jnp.zeros_like(pair))
            scores = lax.dot_general(
                masked,
                key_scr[...],
                (((1,), (1,)), ((), ())),
                preferred_element_type=jnp.float32,
            )
            top = jnp.max(scores, axis=-1, keepdims=True)
            weights = jnp.exp2(scores - top).astype(jnp.bfloat16)
            total = jnp.dot(weights, value_scr[...], preferred_element_type=jnp.float32)
            results.append(total[:, 0:LANES] / total[:, LANES : 2 * LANES])
        out_scr[here, :] = jnp.where(own == 0, results[0], results[1]).astype(out_scr.dtype)
        return carry

    lax.fori_loop(0, length // block_rows, one_block, 0)
    offset = 0 if next_batch is None else 3 * rows
    stores = [
        pltpu.make_async_copy(
            out_scr.at[pl.ds(part * rows, rows), :],
            target.at[pl.ds(offset, rows), :],
            out_sems.at[part],
        )
        for part, target in enumerate(targets)
    ]
    for copy in stores:
        copy.start()
    for copy in packs + stores:
        copy.wait()


def attend(me, blocks, rows, sources, next_batch, per_chunk):
    parts = len(blocks)
    length = parts * rows
    dtype = blocks[0].dtype
    group = max(1, 256 // rows)
    extra = () if next_batch is None else tuple(sources)
    out_rows = rows if next_batch is None else 4 * rows
    anywhere = pl.BlockSpec(memory_space=pl.ANY)
    return pl.pallas_call(
        functools.partial(attend_kernel, parts, rows, group, next_batch, per_chunk),
        in_specs=[pl.BlockSpec(memory_space=pltpu.SMEM)] + [anywhere] * (parts + len(extra)),
        out_specs=[anywhere] * parts,
        out_shape=[jax.ShapeDtypeStruct((out_rows, LANES), dtype)] * parts,
        scratch_shapes=[
            pltpu.VMEM((length, LANES), dtype),
            pltpu.VMEM((length, 2 * LANES), dtype),
            pltpu.VMEM((length, 2 * LANES), dtype),
            pltpu.VMEM((length, LANES), dtype),
            pltpu.SemaphoreType.DMA((4 * parts,)),
            pltpu.SemaphoreType.DMA((3 * parts,)),
            pltpu.SemaphoreType.DMA((parts,)),
        ],
        compiler_params=pltpu.CompilerParams(vmem_limit_bytes=VMEM_LIMIT),
        cost_estimate=pl.CostEstimate(
            flops=2 * 2 * 2 * length * length * 256,
            bytes_accessed=parts * rows * LANES * 8,
            transcendentals=2 * length * length,
        ),
        name="attend",
    )(me, *blocks, *extra)


def gather_kernel(first_batch, per_chunk, parts, offset, me_ref, *refs):
    spatial_ref, piece_ref, sems = refs[-3:]
    blocks = refs[:parts]
    rows = piece_ref.shape[1]
    lane_blocks = piece_ref.shape[2] // LANES
    copies = []
    for shift, block in enumerate(blocks):
        video, lanes = block_place(me_ref[0], shift, lane_blocks, per_chunk)
        source = block.at[pl.ds(offset, rows), :]
        for target in (piece_ref.at[video, :, lanes], spatial_ref.at[first_batch + video, 0, :, lanes]):
            copies.append(pltpu.make_async_copy(source, target, sems.at[len(copies)]))
    for copy in copies:
        copy.start()
    for copy in copies:
        copy.wait()


def gather(me, carry, blocks, offset, shape, first_batch, per_chunk):
    parts = len(blocks)
    batch_size, single, rows, width = shape.shape
    anywhere = pl.BlockSpec(memory_space=pl.ANY)
    return pl.pallas_call(
        functools.partial(gather_kernel, first_batch, per_chunk, parts, offset),
        in_specs=[pl.BlockSpec(memory_space=pltpu.SMEM)] + [anywhere] * (parts + len(carry)),
        out_specs=[anywhere] * 2,
        out_shape=[shape, jax.ShapeDtypeStruct((per_chunk, rows, width), shape.dtype)],
        scratch_shapes=[pltpu.SemaphoreType.DMA((2 * parts,))],
        input_output_aliases={1 + parts: 0} if carry else {},
        cost_estimate=pl.CostEstimate(
            flops=0, bytes_accessed=parts * rows * LANES * 8, transcendentals=0
        ),
        name="gather",
    )(me, *blocks, *carry)


def combine_kernel(views, group, carried, *refs):
    refs = refs[carried:]
    query_ref = refs[0]
    key_refs = refs[1 : 1 + views]
    value_refs = refs[1 + views : 1 + 2 * views]
    (joined_ref,) = refs[1 + 2 * views :]
    head_width = LANES // 2
    source = (lax.broadcasted_iota(jnp.int32, (2 * LANES, LANES), 0) % LANES) // head_width
    target = lax.broadcasted_iota(jnp.int32, (2 * LANES, LANES), 1) // head_width
    spread = jnp.where(source == target, 1.0, 0.0).astype(jnp.bfloat16)
    for j in range(group):
        lanes = slice(j * LANES, (j + 1) * LANES)
        query = query_ref[0, 0, :, lanes].astype(jnp.float32)
        scores = []
        for key_ref in key_refs:
            product = query * key_ref[0, 0, :, lanes].astype(jnp.float32)
            high = product.astype(jnp.bfloat16)
            low = (product - high.astype(jnp.float32)).astype(jnp.bfloat16)
            both = jnp.concatenate([high, low], axis=1)
            scores.append(
                jnp.dot(both, spread, preferred_element_type=jnp.float32)
                * (head_width ** (-0.5))
            )
        top = functools.reduce(jnp.maximum, scores)
        expo = [jnp.exp(score - top) for score in scores]
        inverse = 1.0 / functools.reduce(jnp.add, expo)
        joined = None
        for value_ref, part in zip(value_refs, expo):
            weight = (part * inverse).astype(jnp.bfloat16).astype(jnp.float32)
            term = weight * value_ref[0, :, lanes].astype(jnp.float32)
            joined = term if joined is None else joined + term
        joined_ref[0, 0, :, lanes] = joined.astype(joined_ref.dtype)


def combine(carry, view_queries, keys, outputs, first_batch):
    batch_size, single, rows, width = view_queries.shape
    per_chunk = outputs[0].shape[0]
    views = len(keys)
    group = 4
    steps = width // LANES // group

    def place(i):
        return (first_batch + i // steps, 0, 0, i % steps)

    wide = pl.BlockSpec((1, 1, rows, group * LANES), place)
    narrow = pl.BlockSpec((1, rows, group * LANES), lambda i: (i // steps, 0, i % steps))
    shape = jax.ShapeDtypeStruct(view_queries.shape, view_queries.dtype)
    carried = len(carry)
    size = per_chunk * rows * width
    return pl.pallas_call(
        functools.partial(combine_kernel, views, group, carried),
        grid=(per_chunk * steps,),
        in_specs=[pl.BlockSpec(memory_space=pl.ANY)] * carried
        + [wide] * (1 + views)
        + [narrow] * views,
        out_specs=[wide],
        out_shape=[shape],
        input_output_aliases={i: i for i in range(carried)},
        cost_estimate=pl.CostEstimate(
            flops=size * 1024 * views,
            bytes_accessed=size * 2 * (2 * views + 2),
            transcendentals=size * (views + 1),
        ),
        name="combine",
    )(*carry, view_queries, *keys, *outputs)


def across(value, views):
    return [
        lax.ppermute(value, "view", [(i, i ^ shift) for i in range(views)])
        for shift in range(1, views)
    ]


def exchange(blocks):
    parts = len(blocks)
    arrived = [blocks[0]] + [None] * (parts - 1)
    for shift in reversed(range(1, parts)):
        arrived[shift] = lax.ppermute(
            blocks[shift], "seq", [(i, i ^ shift) for i in range(parts)]
        )
    return arrived


def local(seq_size, views, queries, key_rows, value_rows, view_queries):
    batch_size, single, rows, width = queries.shape
    per_chunk = seq_size // (width // LANES)
    chunks = batch_size // per_chunk
    ahead = 2
    me = lax.axis_index("seq").astype(jnp.int32).reshape(1)
    sources = (queries, key_rows, value_rows)
    received = {}
    for c in range(min(ahead, chunks)):
        received[c] = exchange(pack(me, sources, c * per_chunk, per_chunk, seq_size))
    other_keys = across(key_rows, views)
    received[0], other_keys = lax.optimization_barrier((received[0], other_keys))
    keys = [key_rows] + other_keys
    shape = jax.ShapeDtypeStruct(queries.shape, queries.dtype)
    spatial, joined = (), ()
    for c in range(chunks):
        later = c + ahead if c + ahead < chunks else None
        next_batch = None if later is None else later * per_chunk
        returned = exchange(attend(me, received[c], rows, sources, next_batch, per_chunk))
        if later is not None:
            received[later] = returned
        offset = 0 if later is None else 3 * rows
        spatial, piece = gather(me, spatial, returned, offset, shape, c * per_chunk, per_chunk)
        spatial = (spatial,)
        outputs = [piece] + across(piece, views)
        joined = combine(joined, view_queries, keys, outputs, c * per_chunk)
    return spatial[0], joined[0]


def solution(mesh):
    spec = P(None, "view", "seq", None)
    return jax.shard_map(
        functools.partial(local, mesh.shape["seq"], mesh.shape["view"]),
        mesh=mesh,
        in_specs=(spec,) * 4,
        out_specs=(spec, spec),
        check_vma=False,
    )
```

time: 506 us -> 558 us (1.10); the launches traced: 500 us -> 558 us
  Pallas kernels: 0 us -> 326 us
  matrix products: 171 us -> 0 us
  waiting for transfers between devices: 170 us -> 57.7 us
  starting transfers between devices: 59.3 us -> 168 us
  local copies, waits for them, and re-layouts: 99.9 us -> 4.11 us
    pallas_call x0 -> x14, Pallas kernels: none -> 326 us  [the longest x4 133 us: gather(): pl.pallas_call(functools.partial(gather_kernel, first_batch, per_chunk, p...]
    all_to_all x8 -> x0, waiting for transfers between devices: 170 us -> none  [the longest x1 38.7 us: local(): lax.all_to_all(split_heads(value_rows), 'seq', split_axis=1, concat_axis=...]
    ppermute x0 -> x95, starting transfers between devices: none -> 168 us  [the longest x90 162 us: exchange(): lax.ppermute(blocks[shift], 'seq', [(i, i ^ shift) for i in range(parts)])]
    sub x5 -> x0, matrix products: 98.7 us -> none  [the longest x4 66.9 us: one_block(): scores = scores - jnp.max(scores, axis=-1, keepdims=True)]
    dot_general x5 -> x0, matrix products: 71.9 us -> none  [the longest x4 58.7 us: one_block(): jnp.einsum('pqk,kpe->qpe', weights, value_pairs, preferred_element_type=j...]
    all_to_all x8 -> x0, starting transfers between devices: 59.3 us -> none  [the longest x1 11.3 us: local(): lax.all_to_all(split_heads(value_rows), 'seq', split_axis=1, concat_axis=...]
    ppermute x0 -> x95, waiting for transfers between devices: none -> 57.7 us  [the longest x90 57.7 us: exchange(): lax.ppermute(blocks[shift], 'seq', [(i, i ^ shift) for i in range(parts)])]
    reshape x8 -> x0, local copies, waits for them, and re-layouts: 40.7 us -> none  [the longest x2 9.43 us: apply_weights(): result.astype(jnp.bfloat16)]
  transfers between devices with their start and end apart: 8 -> 95, of which waited for: 6 -> 20; matrix products, arithmetic and copies ran while one was open for 44% -> 0% of each run, Pallas kernels for 0% -> 49%
where the time goes in v1:
time: 558 us
  Pallas kernels  326 us (58%)
  starting transfers between devices  168 us (30%)
  waiting for transfers between devices  57.7 us (10%)
    ppermute x90, starting transfers between devices, exchange(): lax.ppermute(blocks[shift], 'seq', [(i, i ^ shift) for i in range(parts)])  162 us
    pallas_call x4, Pallas kernels, gather(): pl.pallas_call(functools.partial(gather_kernel, first_batch, per_chunk, p...  133 us
    pallas_call x2, Pallas kernels, pack(): pl.pallas_call(functools.partial(pack_kernel, first_batch, per_chunk), in...  98.4 us
    pallas_call x4, Pallas kernels, attend(): pl.pallas_call(functools.partial(attend_kernel, parts, rows, group, next_...  77.5 us
    ppermute x90, waiting for transfers between devices, exchange(): lax.ppermute(blocks[shift], 'seq', [(i, i ^ shift) for i in range(parts)])  57.7 us
    pallas_call x4, Pallas kernels, combine(): pl.pallas_call(functools.partial(combine_kernel, views, group, carried),...  17.5 us
  transfers between devices with their start and end apart: 95, of which 20 were waited for; matrix products, arithmetic and copies ran while one was open for 0% of the time, Pallas kernels for 49%

profile of v1, /device:TPU:0, one launch (start us, length us, event | category | flops | bytes accessed | tf_op | source)
XLA Modules:
  0.0 557.8 jit_solution(6123208989477049073)
XLA Ops:
  0.6 49.2 %pack.2 = (bf16[384,128]{1,0:T(8,128)(2,1)}, bf16[384,128]{1,0:T(8,128)(2,1)}, bf16[384,128]{1,0:T(8,128)(2,1)}, bf16[384,128]{1,0:T(8,128)(2,1)}, bf16[384,128]...) custom-call(s32[1]{0:T(128)} %bitcast.me_ref, ...), custom_call_target="tpu_custom_call" | custom-call | bytes 3145728 | tf_op jit(solution)/shard_map/pack/pallas_call | solution.py:55
  50.4 2.6 collective-permute-start.1
  53.0 1.8 collective-permute-start.3
  54.8 2.6 collective-permute-start.5
  58.6 2.6 collective-permute-start.7
  62.1 2.7 collective-permute-start.9
  64.8 2.8 collective-permute-done.5.refs_6_
  67.7 49.2 %pack.3 = (bf16[384,128]{1,0:T(8,128)(2,1)}, bf16[384,128]{1,0:T(8,128)(2,1)}, bf16[384,128]{1,0:T(8,128)(2,1)}, bf16[384,128]{1,0:T(8,128)(2,1)}, bf16[384,128]...) custom-call(s32[1]{0:T(128)} %bitcast.me_ref, ...), custom_call_target="tpu_custom_call" | custom-call | bytes 3145728 | tf_op jit(solution)/shard_map/pack/pallas_call | solution.py:55
  116.9 2.0 collective-permute-start.11
  119.8 2.4 collective-permute-start.13
  122.2 2.7 collective-permute-start.14
  128.2 6.8 %collective-permute-start.48 = (bf16[384,128]{1,0:T(8,128)(2,1)}, bf16[384,128]{1,0:T(8,128)(2,1)S(1)}, u32[]{:S(2)}, u32[]{:S(2)}) collective-permute-start(bf16[384,128]{1,0:T(8,128)(2,1)} %get-tuple-element.175), channel_id=1, source_target_pairs={{0,4},{1,5},{2,6},{3,7},{4,0},{5,1},{6,2},{7,3},{8,12},{9,13},{10,... | collective-permute-start | bytes 294920 | tf_op jit(solution)/shard_map/ppermute | solution.py:292
  135.0 1.9 collective-permute-start.49
  136.9 1.8 collective-permute-start.50
  141.8 2.0 collective-permute-start.53
  143.8 2.4 collective-permute-start.54
  146.3 19.7 %attend.4 = (bf16[512,128]{1,0:T(8,128)(2,1)S(1)}, bf16[512,128]{1,0:T(8,128)(2,1)S(1)}, bf16[512,128]{1,0:T(8,128)(2,1)S(1)}, bf16[512,128]{1,0:T(8,128)(2,1)S(...) custom-call(s32[1]{0:T(128)} %bitcast.me_ref, ...), custom_call_target="tpu_custom_call" | custom-call | flops 8589934592 | bytes 2097152 | tf_op jit(solution)/shard_map/attend/pallas_call | solution.py:155
  169.7 7.0 %collective-permute-done.55.refs_11_ = bf16[384,128]{1,0:T(8,128)(2,1)S(1)} collective-permute-done((bf16[384,128]{1,0:T(8,128)(2,1)S(1)}, bf16[384,128]{1,0:T(8,128)(2,1)S(1)}, u32[]{:S(2)}, u32[]{:S(2)}) %collective-permute-start.55) | collective-permute-done | bytes 98336 | tf_op jit(solution)/shard_map/ppermute | solution.py:292
  181.1 1.9 collective-permute-done.18.refs_4_
  184.2 1.8 collective-permute-start.23
  186.0 7.9 %collective-permute-done.20.refs_6_ = bf16[512,128]{1,0:T(8,128)(2,1)S(1)} collective-permute-done((bf16[512,128]{1,0:T(8,128)(2,1)S(1)}, bf16[512,128]{1,0:T(8,128)(2,1)S(1)}, u32[]{:S(2)}, u32[]{:S(2)}) %collective-permute-start.20) | collective-permute-done | bytes 131104 | tf_op jit(solution)/shard_map/ppermute | solution.py:292
  197.0 11.7 %collective-permute-start.27 = (bf16[512,128]{1,0:T(8,128)(2,1)S(1)}, bf16[512,128]{1,0:T(8,128)(2,1)S(1)}, u32[]{:S(2)}, u32[]{:S(2)}) collective-permute-start(bf16[512,128]{1,0:T(8,128)(2,1)S(1)} %get-tuple-element.152), channel_id=1, source_target_pairs={{0,13},{1,12},{2,15},{3,14},{4,9},{5,8},{6,11},{7,10},{8,5},{9,4},... | collective-permute-start | bytes 393224 | tf_op jit(solution)/shard_map/ppermute | solution.py:292
  208.7 3.6 collective-permute-done.24.refs_10_
  212.3 2.1 collective-permute-start.28
  214.4 5.0 collective-permute-start.29
  219.4 2.0 collective-permute-start.56
  221.5 3.9 collective-permute-start.58
  225.4 2.3 collective-permute-start.59
  227.7 19.0 %attend.5 = (bf16[128,128]{1,0:T(8,128)(2,1)S(1)}, bf16[128,128]{1,0:T(8,128)(2,1)S(1)}, bf16[128,128]{1,0:T(8,128)(2,1)S(1)}, bf16[128,128]{1,0:T(8,128)(2,1)S(...) custom-call(s32[1]{0:T(128)} %bitcast.me_ref, ...), custom_call_target="tpu_custom_call" | custom-call | flops 8589934592 | bytes 2097152 | tf_op jit(solution)/shard_map/attend/pallas_call | solution.py:155
  247.1 2.5 collective-permute-start.31
  249.7 14.5 %collective-permute-start.33 = (bf16[128,128]{1,0:T(8,128)(2,1)S(1)}, bf16[128,128]{1,0:T(8,128)(2,1)S(1)}, u32[]{:S(2)}, u32[]{:S(2)}) collective-permute-start(bf16[128,128]{1,0:T(8,128)(2,1)S(1)} %get-tuple-element.159), channel_id=1, source_target_pairs={{0,4},{1,5},{2,6},{3,7},{4,0},{5,1},{6,2},{7,3},{8,12},{9,13},{10,... | collective-permute-start | bytes 98312 | tf_op jit(solution)/shard_map/ppermute | solution.py:292
  264.3 19.7 %attend.6 = (bf16[512,128]{1,0:T(8,128)(2,1)S(1)}, bf16[512,128]{1,0:T(8,128)(2,1)S(1)}, bf16[512,128]{1,0:T(8,128)(2,1)S(1)}, bf16[512,128]{1,0:T(8,128)(2,1)S(...) custom-call(s32[1]{0:T(128)} %bitcast.me_ref, ...), custom_call_target="tpu_custom_call" | custom-call | flops 8589934592 | bytes 2097152 | tf_op jit(solution)/shard_map/attend/pallas_call | solution.py:155
  288.0 2.2 collective-permute-start.66
  295.4 2.6 collective-permute-start.70
  298.1 6.2 %collective-permute-done.66.refs_6_ = bf16[512,128]{1,0:T(8,128)(2,1)S(1)} collective-permute-done((bf16[512,128]{1,0:T(8,128)(2,1)S(1)}, bf16[512,128]{1,0:T(8,128)(2,1)S(1)}, u32[]{:S(2)}, u32[]{:S(2)}) %collective-permute-start.66) | collective-permute-done | bytes 131104 | tf_op jit(solution)/shard_map/ppermute | solution.py:292
  304.3 2.1 collective-permute-done.67.refs_7_
  311.5 12.6 %collective-permute-done.70.refs_10_ = bf16[512,128]{1,0:T(8,128)(2,1)S(1)} collective-permute-done((bf16[512,128]{1,0:T(8,128)(2,1)S(1)}, bf16[512,128]{1,0:T(8,128)(2,1)S(1)}, u32[]{:S(2)}, u32[]{:S(2)}) %collective-permute-start.70) | collective-permute-done | bytes 131104 | tf_op jit(solution)/shard_map/ppermute | solution.py:292
  324.1 2.0 collective-permute-start.75
  327.7 5.9 %collective-permute-start.36 = (bf16[128,128]{1,0:T(8,128)(2,1)S(1)}, bf16[128,128]{1,0:T(8,128)(2,1)S(1)}, u32[]{:S(2)}, u32[]{:S(2)}) collective-permute-start(bf16[128,128]{1,0:T(8,128)(2,1)S(1)} %get-tuple-element.162), channel_id=1, source_target_pairs={{0,7},{1,6},{2,5},{3,4},{4,3},{5,2},{6,1},{7,0},{8,15},{9,14},{10,... | collective-permute-start | bytes 98312 | tf_op jit(solution)/shard_map/ppermute | solution.py:292
  333.6 3.7 collective-permute-start.37
  337.3 3.2 collective-permute-start.38
  340.5 4.6 collective-permute-start.39
  345.2 19.0 %attend.7 = (bf16[128,128]{1,0:T(8,128)(2,1)S(1)}, bf16[128,128]{1,0:T(8,128)(2,1)S(1)}, bf16[128,128]{1,0:T(8,128)(2,1)S(1)}, bf16[128,128]{1,0:T(8,128)(2,1)S(...) custom-call(s32[1]{0:T(128)} %bitcast.me_ref, ...), custom_call_target="tpu_custom_call" | custom-call | flops 8589934592 | bytes 2097152 | tf_op jit(solution)/shard_map/attend/pallas_call | solution.py:155
  368.8 2.1 collective-permute-start.82
  370.9 33.1 %gather.4 = (bf16[4,1,128,2048]{3,2,1,0:T(8,128)(2,1)}, bf16[1,128,2048]{2,1,0:T(8,128)(2,1)}) custom-call(s32[1]{0:T(128)} %bitcast.me_ref, bf16[512,128]{1,0:T(8,128)(2,1)} %copy-done.17, bf16[512,128]{1,0:T(8,128)(2,1)} %copy-done.18, bf16[512,128]{1,0:T(8,128)(2,1)} %copy-done.19, bf16[512,128]{1,0:T(8,128)(2,1)} %copy-done.20, ...), custom_call_target="tpu_custom_call" | custom-call | bytes 2097152 | tf_op jit(solution)/shard_map/gather/pallas_call | solution.py:200
  404.1 1.7 collective-permute-start.91
  405.8 1.8 collective-permute-start.84
  409.2 2.3 collective-permute-start.86
  411.5 1.7 collective-permute-start.87
  414.7 33.1 %gather.5 = (bf16[4,1,128,2048]{3,2,1,0:T(8,128)(2,1)}, bf16[1,128,2048]{2,1,0:T(8,128)(2,1)}) custom-call(s32[1]{0:T(128)} %bitcast.me_ref, bf16[512,128]{1,0:T(8,128)(2,1)} %copy-done.1, bf16[512,128]{1,0:T(8,128)(2,1)} %copy-done.2, bf16[512,128]{1,0:T(8,128)(2,1)} %copy-done.3, bf16[512,128]{1,0:T(8,128)(2,1)} %copy-done.4, ...), custom_call_target="tpu_custom_call", output_to_operand_aliasing={{0}: (17, {})} | custom-call | bytes 2097152 | tf_op jit(solution)/shard_map/gather/pallas_call | solution.py:200
  449.0 2.1 collective-permute-start.89
  451.1 2.4 collective-permute-start.90
  453.6 2.0 collective-permute-done.89.refs_14_
  457.1 1.9 collective-permute-start.42
  459.0 33.2 %gather.6 = (bf16[4,1,128,2048]{3,2,1,0:T(8,128)(2,1)}, bf16[1,128,2048]{2,1,0:T(8,128)(2,1)}) custom-call(s32[1]{0:T(128)} %bitcast.me_ref, bf16[128,128]{1,0:T(8,128)(2,1)} %copy-done.34, bf16[128,128]{1,0:T(8,128)(2,1)} %copy-done.62, bf16[128,128]{1,0:T(8,128)(2,1)} %copy-done.63, bf16[128,128]{1,0:T(8,128)(2,1)} %copy-done.64, ...), custom_call_target="tpu_custom_call", output_to_operand_aliasing={{0}: (17, {})} | custom-call | bytes 2097152 | tf_op jit(solution)/shard_map/gather/pallas_call | solution.py:200
  493.6 2.5 collective-permute-start.43
  496.2 1.8 collective-permute-start.44
  498.0 2.3 collective-permute-done.43.refs_14_
  500.3 2.2 collective-permute-done.44.refs_15_
  503.1 33.1 %gather.7 = (bf16[4,1,128,2048]{3,2,1,0:T(8,128)(2,1)}, bf16[1,128,2048]{2,1,0:T(8,128)(2,1)}) custom-call(s32[1]{0:T(128)} %bitcast.me_ref, bf16[128,128]{1,0:T(8,128)(2,1)} %copy-done.33, bf16[128,128]{1,0:T(8,128)(2,1)} %copy-done.52, bf16[128,128]{1,0:T(8,128)(2,1)} %copy-done.53, bf16[128,128]{1,0:T(8,128)(2,1)} %copy-done.54, ...), custom_call_target="tpu_custom_call", output_to_operand_aliasing={{0}: (17, {})} | custom-call | bytes 2097152 | tf_op jit(solution)/shard_map/gather/pallas_call | solution.py:200
  537.8 4.4 combine.4.refs_0_
  543.0 4.4 combine.5.refs_0_
  548.2 4.4 combine.6.refs_0_
  553.4 4.4 combine.7
  (318 shorter events, 54.6 us)
Async XLA Ops:
  54.8 12.7 %collective-permute-start.5 = (bf16[384,128]{1,0:T(8,128)(2,1)}, bf16[384,128]{1,0:T(8,128)(2,1)S(1)}, u32[]{:S(2)}, u32[]{:S(2)}) collective-permute-start(bf16[384,128]{1,0:T(8,128)(2,1)} %get-tuple-element.129), channel_id=1, source_target_pairs={{0,6},{1,7},{2,4},{3,5},{4,2},{5,3},{6,0},{7,1},{8,14},{9,15},{10,... | collective-permute-start | bytes 294920 | tf_op jit(solution)/shard_map/ppermute | solution.py:292
  57.4 59.4 %collective-permute-start.6 = (bf16[384,128]{1,0:T(8,128)(2,1)}, bf16[384,128]{1,0:T(8,128)(2,1)S(1)}, u32[]{:S(2)}, u32[]{:S(2)}) collective-permute-start(bf16[384,128]{1,0:T(8,128)(2,1)} %get-tuple-element.130), channel_id=1, source_target_pairs={{0,7},{1,6},{2,5},{3,4},{4,3},{5,2},{6,1},{7,0},{8,15},{9,14},{10,... | collective-permute-start | bytes 294920 | tf_op jit(solution)/shard_map/ppermute | solution.py:292
  58.6 60.4 %collective-permute-start.7 = (bf16[384,128]{1,0:T(8,128)(2,1)}, bf16[384,128]{1,0:T(8,128)(2,1)S(1)}, u32[]{:S(2)}, u32[]{:S(2)}) collective-permute-start(bf16[384,128]{1,0:T(8,128)(2,1)} %get-tuple-element.131), channel_id=1, source_target_pairs={{0,8},{1,9},{2,10},{3,11},{4,12},{5,13},{6,14},{7,15},{8,0},{9,1},... | collective-permute-start | bytes 294920 | tf_op jit(solution)/shard_map/ppermute | solution.py:292
  61.1 58.7 %collective-permute-start.8 = (bf16[384,128]{1,0:T(8,128)(2,1)}, bf16[384,128]{1,0:T(8,128)(2,1)S(1)}, u32[]{:S(2)}, u32[]{:S(2)}) collective-permute-start(bf16[384,128]{1,0:T(8,128)(2,1)} %get-tuple-element.132), channel_id=1, source_target_pairs={{0,9},{1,8},{2,11},{3,10},{4,13},{5,12},{6,15},{7,14},{8,1},{9,0},... | collective-permute-start | bytes 294920 | tf_op jit(solution)/shard_map/ppermute | solution.py:292
  62.1 60.1 %collective-permute-start.9 = (bf16[384,128]{1,0:T(8,128)(2,1)}, bf16[384,128]{1,0:T(8,128)(2,1)S(1)}, u32[]{:S(2)}, u32[]{:S(2)}) collective-permute-start(bf16[384,128]{1,0:T(8,128)(2,1)} %get-tuple-element.133), channel_id=1, source_target_pairs={{0,10},{1,11},{2,8},{3,9},{4,14},{5,15},{6,12},{7,13},{8,2},{9,3},... | collective-permute-start | bytes 294920 | tf_op jit(solution)/shard_map/ppermute | solution.py:292
  67.6 57.4 %collective-permute-start.10 = (bf16[384,128]{1,0:T(8,128)(2,1)}, bf16[384,128]{1,0:T(8,128)(2,1)S(1)}, u32[]{:S(2)}, u32[]{:S(2)}) collective-permute-start(bf16[384,128]{1,0:T(8,128)(2,1)} %get-tuple-element.134), channel_id=1, source_target_pairs={{0,11},{1,10},{2,9},{3,8},{4,15},{5,14},{6,13},{7,12},{8,3},{9,2},... | collective-permute-start | bytes 294920 | tf_op jit(solution)/shard_map/ppermute | solution.py:292
  122.2 12.8 %collective-permute-start.14 = (bf16[384,128]{1,0:T(8,128)(2,1)S(1)}, bf16[384,128]{1,0:T(8,128)(2,1)S(1)}, u32[]{:S(2)}, u32[]{:S(2)}) collective-permute-start(bf16[384,128]{1,0:T(8,128)(2,1)S(1)} %copy-done.87), channel_id=1, source_target_pairs={{0,15},{1,14},{2,13},{3,12},{4,11},{5,10},{6,9},{7,8},{8,7},{9,6},... | collective-permute-start | bytes 294920 | tf_op jit(solution)/shard_map/ppermute | solution.py:292
  125.0 13.7 %collective-permute-start.46 = (bf16[384,128]{1,0:T(8,128)(2,1)}, bf16[384,128]{1,0:T(8,128)(2,1)S(1)}, u32[]{:S(2)}, u32[]{:S(2)}) collective-permute-start(bf16[384,128]{1,0:T(8,128)(2,1)} %get-tuple-element.173), channel_id=1, source_target_pairs={{0,2},{1,3},{2,0},{3,1},{4,6},{5,7},{6,4},{7,5},{8,10},{9,11},{10,... | collective-permute-start | bytes 294920 | tf_op jit(solution)/shard_map/ppermute | solution.py:292
  125.8 14.4 %collective-permute-start.47 = (bf16[384,128]{1,0:T(8,128)(2,1)}, bf16[384,128]{1,0:T(8,128)(2,1)S(1)}, u32[]{:S(2)}, u32[]{:S(2)}) collective-permute-start(bf16[384,128]{1,0:T(8,128)(2,1)} %get-tuple-element.174), channel_id=1, source_target_pairs={{0,3},{1,2},{2,1},{3,0},{4,7},{5,6},{6,5},{7,4},{8,11},{9,10},{10,... | collective-permute-start | bytes 294920 | tf_op jit(solution)/shard_map/ppermute | solution.py:292
  128.2 13.3 %collective-permute-start.48 = (bf16[384,128]{1,0:T(8,128)(2,1)}, bf16[384,128]{1,0:T(8,128)(2,1)S(1)}, u32[]{:S(2)}, u32[]{:S(2)}) collective-permute-start(bf16[384,128]{1,0:T(8,128)(2,1)} %get-tuple-element.175), channel_id=1, source_target_pairs={{0,4},{1,5},{2,6},{3,7},{4,0},{5,1},{6,2},{7,3},{8,12},{9,13},{10,... | collective-permute-start | bytes 294920 | tf_op jit(solution)/shard_map/ppermute | solution.py:292
  138.7 125.5 %collective-permute-start.60 = (bf16[4,1,128,2048]{3,2,1,0:T(8,128)(2,1)}, bf16[4,1,128,2048]{3,2,1,0:T(8,128)(2,1)S(1)}, u32[]{:S(2)}, u32[]{:S(2)}) collective-permute-start(bf16[4,1,128,2048]{3,2,1,0:T(8,128)(2,1)} %refs_2_.5), channel_id=1, source_target_pairs={{0,16},{16,0},{1,17},{17,1},{2,18},{18,2},{3,19},{19,3},{4,20},{20... | collective-permute-start | bytes 6291464 | tf_op jit(solution)/shard_map/ppermute | solution.py:283
  140.2 25.8 %collective-permute-start.51 = (bf16[384,128]{1,0:T(8,128)(2,1)}, bf16[384,128]{1,0:T(8,128)(2,1)S(1)}, u32[]{:S(2)}, u32[]{:S(2)}) collective-permute-start(bf16[384,128]{1,0:T(8,128)(2,1)} %get-tuple-element.178), channel_id=1, source_target_pairs={{0,7},{1,6},{2,5},{3,4},{4,3},{5,2},{6,1},{7,0},{8,15},{9,14},{10,... | collective-permute-start | bytes 294920 | tf_op jit(solution)/shard_map/ppermute | solution.py:292
  141.5 24.6 %collective-permute-start.52 = (bf16[384,128]{1,0:T(8,128)(2,1)}, bf16[384,128]{1,0:T(8,128)(2,1)S(1)}, u32[]{:S(2)}, u32[]{:S(2)}) collective-permute-start(bf16[384,128]{1,0:T(8,128)(2,1)} %get-tuple-element.179), channel_id=1, source_target_pairs={{0,8},{1,9},{2,10},{3,11},{4,12},{5,13},{6,14},{7,15},{8,0},{9,1},... | collective-permute-start | bytes 294920 | tf_op jit(solution)/shard_map/ppermute | solution.py:292
  141.8 25.7 %collective-permute-start.53 = (bf16[384,128]{1,0:T(8,128)(2,1)}, bf16[384,128]{1,0:T(8,128)(2,1)S(1)}, u32[]{:S(2)}, u32[]{:S(2)}) collective-permute-start(bf16[384,128]{1,0:T(8,128)(2,1)} %get-tuple-element.180), channel_id=1, source_target_pairs={{0,9},{1,8},{2,11},{3,10},{4,13},{5,12},{6,15},{7,14},{8,1},{9,0},... | collective-permute-start | bytes 294920 | tf_op jit(solution)/shard_map/ppermute | solution.py:292
  143.8 24.2 %collective-permute-start.54 = (bf16[384,128]{1,0:T(8,128)(2,1)}, bf16[384,128]{1,0:T(8,128)(2,1)S(1)}, u32[]{:S(2)}, u32[]{:S(2)}) collective-permute-start(bf16[384,128]{1,0:T(8,128)(2,1)} %get-tuple-element.181), channel_id=1, source_target_pairs={{0,10},{1,11},{2,8},{3,9},{4,14},{5,15},{6,12},{7,13},{8,2},{9,3},... | collective-permute-start | bytes 294920 | tf_op jit(solution)/shard_map/ppermute | solution.py:292
  167.5 12.2 %collective-permute-start.17 = (bf16[512,128]{1,0:T(8,128)(2,1)S(1)}, bf16[512,128]{1,0:T(8,128)(2,1)S(1)}, u32[]{:S(2)}, u32[]{:S(2)}) collective-permute-start(bf16[512,128]{1,0:T(8,128)(2,1)S(1)} %get-tuple-element.142), channel_id=1, source_target_pairs={{0,3},{1,2},{2,1},{3,0},{4,7},{5,6},{6,5},{7,4},{8,11},{9,10},{10,... | collective-permute-start | bytes 393224 | tf_op jit(solution)/shard_map/ppermute | solution.py:292
  178.2 15.7 %collective-permute-start.20 = (bf16[512,128]{1,0:T(8,128)(2,1)S(1)}, bf16[512,128]{1,0:T(8,128)(2,1)S(1)}, u32[]{:S(2)}, u32[]{:S(2)}) collective-permute-start(bf16[512,128]{1,0:T(8,128)(2,1)S(1)} %get-tuple-element.145), channel_id=1, source_target_pairs={{0,6},{1,7},{2,4},{3,5},{4,2},{5,3},{6,0},{7,1},{8,14},{9,15},{10,... | collective-permute-start | bytes 393224 | tf_op jit(solution)/shard_map/ppermute | solution.py:292
  179.7 15.3 %collective-permute-start.21 = (bf16[512,128]{1,0:T(8,128)(2,1)S(1)}, bf16[512,128]{1,0:T(8,128)(2,1)S(1)}, u32[]{:S(2)}, u32[]{:S(2)}) collective-permute-start(bf16[512,128]{1,0:T(8,128)(2,1)S(1)} %get-tuple-element.146), channel_id=1, source_target_pairs={{0,7},{1,6},{2,5},{3,4},{4,3},{5,2},{6,1},{7,0},{8,15},{9,14},{10,... | collective-permute-start | bytes 393224 | tf_op jit(solution)/shard_map/ppermute | solution.py:292
  183.0 12.4 %collective-permute-start.22 = (bf16[512,128]{1,0:T(8,128)(2,1)S(1)}, bf16[512,128]{1,0:T(8,128)(2,1)S(1)}, u32[]{:S(2)}, u32[]{:S(2)}) collective-permute-start(bf16[512,128]{1,0:T(8,128)(2,1)S(1)} %get-tuple-element.147), channel_id=1, source_target_pairs={{0,8},{1,9},{2,10},{3,11},{4,12},{5,13},{6,14},{7,15},{8,0},{9,1},... | collective-permute-start | bytes 393224 | tf_op jit(solution)/shard_map/ppermute | solution.py:292
  184.2 12.8 %collective-permute-start.23 = (bf16[512,128]{1,0:T(8,128)(2,1)S(1)}, bf16[512,128]{1,0:T(8,128)(2,1)S(1)}, u32[]{:S(2)}, u32[]{:S(2)}) collective-permute-start(bf16[512,128]{1,0:T(8,128)(2,1)S(1)} %get-tuple-element.148), channel_id=1, source_target_pairs={{0,9},{1,8},{2,11},{3,10},{4,13},{5,12},{6,15},{7,14},{8,1},{9,0},... | collective-permute-start | bytes 393224 | tf_op jit(solution)/shard_map/ppermute | solution.py:292
  193.9 18.5 %collective-permute-start.24 = (bf16[512,128]{1,0:T(8,128)(2,1)S(1)}, bf16[512,128]{1,0:T(8,128)(2,1)S(1)}, u32[]{:S(2)}, u32[]{:S(2)}) collective-permute-start(bf16[512,128]{1,0:T(8,128)(2,1)S(1)} %get-tuple-element.149), channel_id=1, source_target_pairs={{0,10},{1,11},{2,8},{3,9},{4,14},{5,15},{6,12},{7,13},{8,2},{9,3},... | collective-permute-start | bytes 393224 | tf_op jit(solution)/shard_map/ppermute | solution.py:292
  195.0 19.4 %collective-permute-start.25 = (bf16[512,128]{1,0:T(8,128)(2,1)S(1)}, bf16[512,128]{1,0:T(8,128)(2,1)S(1)}, u32[]{:S(2)}, u32[]{:S(2)}) collective-permute-start(bf16[512,128]{1,0:T(8,128)(2,1)S(1)} %get-tuple-element.150), channel_id=1, source_target_pairs={{0,11},{1,10},{2,9},{3,8},{4,15},{5,14},{6,13},{7,12},{8,3},{9,2},... | collective-permute-start | bytes 393224 | tf_op jit(solution)/shard_map/ppermute | solution.py:292
  195.4 24.1 %collective-permute-start.26 = (bf16[512,128]{1,0:T(8,128)(2,1)S(1)}, bf16[512,128]{1,0:T(8,128)(2,1)S(1)}, u32[]{:S(2)}, u32[]{:S(2)}) collective-permute-start(bf16[512,128]{1,0:T(8,128)(2,1)S(1)} %get-tuple-element.151), channel_id=1, source_target_pairs={{0,12},{1,13},{2,14},{3,15},{4,8},{5,9},{6,10},{7,11},{8,4},{9,5},... | collective-permute-start | bytes 393224 | tf_op jit(solution)/shard_map/ppermute | solution.py:292
  197.0 24.4 %collective-permute-start.27 = (bf16[512,128]{1,0:T(8,128)(2,1)S(1)}, bf16[512,128]{1,0:T(8,128)(2,1)S(1)}, u32[]{:S(2)}, u32[]{:S(2)}) collective-permute-start(bf16[512,128]{1,0:T(8,128)(2,1)S(1)} %get-tuple-element.152), channel_id=1, source_target_pairs={{0,13},{1,12},{2,15},{3,14},{4,9},{5,8},{6,11},{7,10},{8,5},{9,4},... | collective-permute-start | bytes 393224 | tf_op jit(solution)/shard_map/ppermute | solution.py:292
  219.4 27.5 %collective-permute-start.56 = (bf16[384,128]{1,0:T(8,128)(2,1)S(1)}, bf16[384,128]{1,0:T(8,128)(2,1)S(1)}, u32[]{:S(2)}, u32[]{:S(2)}) collective-permute-start(bf16[384,128]{1,0:T(8,128)(2,1)S(1)} %copy-done.85), channel_id=1, source_target_pairs={{0,12},{1,13},{2,14},{3,15},{4,8},{5,9},{6,10},{7,11},{8,4},{9,5},... | collective-permute-start | bytes 294920 | tf_op jit(solution)/shard_map/ppermute | solution.py:292
  221.4 25.6 %collective-permute-start.57 = (bf16[384,128]{1,0:T(8,128)(2,1)S(1)}, bf16[384,128]{1,0:T(8,128)(2,1)S(1)}, u32[]{:S(2)}, u32[]{:S(2)}) collective-permute-start(bf16[384,128]{1,0:T(8,128)(2,1)S(1)} %copy-done.84), channel_id=1, source_target_pairs={{0,13},{1,12},{2,15},{3,14},{4,9},{5,8},{6,11},{7,10},{8,5},{9,4},... | collective-permute-start | bytes 294920 | tf_op jit(solution)/shard_map/ppermute | solution.py:292
  221.5 28.1 %collective-permute-start.58 = (bf16[384,128]{1,0:T(8,128)(2,1)S(1)}, bf16[384,128]{1,0:T(8,128)(2,1)S(1)}, u32[]{:S(2)}, u32[]{:S(2)}) collective-permute-start(bf16[384,128]{1,0:T(8,128)(2,1)S(1)} %copy-done.83), channel_id=1, source_target_pairs={{0,14},{1,15},{2,12},{3,13},{4,10},{5,11},{6,8},{7,9},{8,6},{9,7},... | collective-permute-start | bytes 294920 | tf_op jit(solution)/shard_map/ppermute | solution.py:292
  225.4 24.3 %collective-permute-start.59 = (bf16[384,128]{1,0:T(8,128)(2,1)S(1)}, bf16[384,128]{1,0:T(8,128)(2,1)S(1)}, u32[]{:S(2)}, u32[]{:S(2)}) collective-permute-start(bf16[384,128]{1,0:T(8,128)(2,1)S(1)} %copy-done.82), channel_id=1, source_target_pairs={{0,15},{1,14},{2,13},{3,12},{4,11},{5,10},{6,9},{7,8},{8,7},{9,6},... | collective-permute-start | bytes 294920 | tf_op jit(solution)/shard_map/ppermute | solution.py:292
  247.0 37.1 %collective-permute-start.30 = (bf16[128,128]{1,0:T(8,128)(2,1)S(1)}, bf16[128,128]{1,0:T(8,128)(2,1)S(1)}, u32[]{:S(2)}, u32[]{:S(2)}) collective-permute-start(bf16[128,128]{1,0:T(8,128)(2,1)S(1)} %get-tuple-element.156), channel_id=1, source_target_pairs={{0,1},{1,0},{2,3},{3,2},{4,5},{5,4},{6,7},{7,6},{8,9},{9,8},{10,11... | collective-permute-start | bytes 98312 | tf_op jit(solution)/shard_map/ppermute | solution.py:292
  247.1 37.2 %collective-permute-start.31 = (bf16[128,128]{1,0:T(8,128)(2,1)S(1)}, bf16[128,128]{1,0:T(8,128)(2,1)S(1)}, u32[]{:S(2)}, u32[]{:S(2)}) collective-permute-start(bf16[128,128]{1,0:T(8,128)(2,1)S(1)} %get-tuple-element.157), channel_id=1, source_target_pairs={{0,2},{1,3},{2,0},{3,1},{4,6},{5,7},{6,4},{7,5},{8,10},{9,11},{10,... | collective-permute-start | bytes 98312 | tf_op jit(solution)/shard_map/ppermute | solution.py:292
  249.6 35.7 %collective-permute-start.32 = (bf16[128,128]{1,0:T(8,128)(2,1)S(1)}, bf16[128,128]{1,0:T(8,128)(2,1)S(1)}, u32[]{:S(2)}, u32[]{:S(2)}) collective-permute-start(bf16[128,128]{1,0:T(8,128)(2,1)S(1)} %get-tuple-element.158), channel_id=1, source_target_pairs={{0,3},{1,2},{2,1},{3,0},{4,7},{5,6},{6,5},{7,4},{8,11},{9,10},{10,... | collective-permute-start | bytes 98312 | tf_op jit(solution)/shard_map/ppermute | solution.py:292
  249.7 36.3 %collective-permute-start.33 = (bf16[128,128]{1,0:T(8,128)(2,1)S(1)}, bf16[128,128]{1,0:T(8,128)(2,1)S(1)}, u32[]{:S(2)}, u32[]{:S(2)}) collective-permute-start(bf16[128,128]{1,0:T(8,128)(2,1)S(1)} %get-tuple-element.159), channel_id=1, source_target_pairs={{0,4},{1,5},{2,6},{3,7},{4,0},{5,1},{6,2},{7,3},{8,12},{9,13},{10,... | collective-permute-start | bytes 98312 | tf_op jit(solution)/shard_map/ppermute | solution.py:292
  264.2 23.4 %collective-permute-start.34 = (bf16[128,128]{1,0:T(8,128)(2,1)S(1)}, bf16[128,128]{1,0:T(8,128)(2,1)S(1)}, u32[]{:S(2)}, u32[]{:S(2)}) collective-permute-start(bf16[128,128]{1,0:T(8,128)(2,1)S(1)} %get-tuple-element.160), channel_id=1, source_target_pairs={{0,5},{1,4},{2,7},{3,6},{4,1},{5,0},{6,3},{7,2},{8,13},{9,12},{10,... | collective-permute-start | bytes 98312 | tf_op jit(solution)/shard_map/ppermute | solution.py:292
  288.0 16.2 %collective-permute-start.66 = (bf16[512,128]{1,0:T(8,128)(2,1)S(1)}, bf16[512,128]{1,0:T(8,128)(2,1)S(1)}, u32[]{:S(2)}, u32[]{:S(2)}) collective-permute-start(bf16[512,128]{1,0:T(8,128)(2,1)S(1)} %get-tuple-element.209), channel_id=1, source_target_pairs={{0,6},{1,7},{2,4},{3,5},{4,2},{5,3},{6,0},{7,1},{8,14},{9,15},{10,... | collective-permute-start | bytes 393224 | tf_op jit(solution)/shard_map/ppermute | solution.py:292
  290.5 15.9 %collective-permute-start.67 = (bf16[512,128]{1,0:T(8,128)(2,1)S(1)}, bf16[512,128]{1,0:T(8,128)(2,1)S(1)}, u32[]{:S(2)}, u32[]{:S(2)}) collective-permute-start(bf16[512,128]{1,0:T(8,128)(2,1)S(1)} %get-tuple-element.210), channel_id=1, source_target_pairs={{0,7},{1,6},{2,5},{3,4},{4,3},{5,2},{6,1},{7,0},{8,15},{9,14},{10,... | collective-permute-start | bytes 393224 | tf_op jit(solution)/shard_map/ppermute | solution.py:292
  292.4 15.7 %collective-permute-start.68 = (bf16[512,128]{1,0:T(8,128)(2,1)S(1)}, bf16[512,128]{1,0:T(8,128)(2,1)S(1)}, u32[]{:S(2)}, u32[]{:S(2)}) collective-permute-start(bf16[512,128]{1,0:T(8,128)(2,1)S(1)} %get-tuple-element.211), channel_id=1, source_target_pairs={{0,8},{1,9},{2,10},{3,11},{4,12},{5,13},{6,14},{7,15},{8,0},{9,1},... | collective-permute-start | bytes 393224 | tf_op jit(solution)/shard_map/ppermute | solution.py:292
  294.1 15.6 %collective-permute-start.69 = (bf16[512,128]{1,0:T(8,128)(2,1)S(1)}, bf16[512,128]{1,0:T(8,128)(2,1)S(1)}, u32[]{:S(2)}, u32[]{:S(2)}) collective-permute-start(bf16[512,128]{1,0:T(8,128)(2,1)S(1)} %get-tuple-element.212), channel_id=1, source_target_pairs={{0,9},{1,8},{2,11},{3,10},{4,13},{5,12},{6,15},{7,14},{8,1},{9,0},... | collective-permute-start | bytes 393224 | tf_op jit(solution)/shard_map/ppermute | solution.py:292
  295.4 28.7 %collective-permute-start.70 = (bf16[512,128]{1,0:T(8,128)(2,1)S(1)}, bf16[512,128]{1,0:T(8,128)(2,1)S(1)}, u32[]{:S(2)}, u32[]{:S(2)}) collective-permute-start(bf16[512,128]{1,0:T(8,128)(2,1)S(1)} %get-tuple-element.213), channel_id=1, source_target_pairs={{0,10},{1,11},{2,8},{3,9},{4,14},{5,15},{6,12},{7,13},{8,2},{9,3},... | collective-permute-start | bytes 393224 | tf_op jit(solution)/shard_map/ppermute | solution.py:292
  304.3 23.4 %collective-permute-start.71 = (bf16[512,128]{1,0:T(8,128)(2,1)S(1)}, bf16[512,128]{1,0:T(8,128)(2,1)S(1)}, u32[]{:S(2)}, u32[]{:S(2)}) collective-permute-start(bf16[512,128]{1,0:T(8,128)(2,1)S(1)} %get-tuple-element.214), channel_id=1, source_target_pairs={{0,11},{1,10},{2,9},{3,8},{4,15},{5,14},{6,13},{7,12},{8,3},{9,2},... | collective-permute-start | bytes 393224 | tf_op jit(solution)/shard_map/ppermute | solution.py:292
  306.4 21.2 %collective-permute-start.72 = (bf16[512,128]{1,0:T(8,128)(2,1)S(1)}, bf16[512,128]{1,0:T(8,128)(2,1)S(1)}, u32[]{:S(2)}, u32[]{:S(2)}) collective-permute-start(bf16[512,128]{1,0:T(8,128)(2,1)S(1)} %get-tuple-element.215), channel_id=1, source_target_pairs={{0,12},{1,13},{2,14},{3,15},{4,8},{5,9},{6,10},{7,11},{8,4},{9,5},... | collective-permute-start | bytes 393224 | tf_op jit(solution)/shard_map/ppermute | solution.py:292
  308.1 25.4 %collective-permute-start.73 = (bf16[512,128]{1,0:T(8,128)(2,1)S(1)}, bf16[512,128]{1,0:T(8,128)(2,1)S(1)}, u32[]{:S(2)}, u32[]{:S(2)}) collective-permute-start(bf16[512,128]{1,0:T(8,128)(2,1)S(1)} %get-tuple-element.216), channel_id=1, source_target_pairs={{0,13},{1,12},{2,15},{3,14},{4,9},{5,8},{6,11},{7,10},{8,5},{9,4},... | collective-permute-start | bytes 393224 | tf_op jit(solution)/shard_map/ppermute | solution.py:292
  309.7 27.6 %collective-permute-start.74 = (bf16[512,128]{1,0:T(8,128)(2,1)S(1)}, bf16[512,128]{1,0:T(8,128)(2,1)S(1)}, u32[]{:S(2)}, u32[]{:S(2)}) collective-permute-start(bf16[512,128]{1,0:T(8,128)(2,1)S(1)} %get-tuple-element.217), channel_id=1, source_target_pairs={{0,14},{1,15},{2,12},{3,13},{4,10},{5,11},{6,8},{7,9},{8,6},{9,7},... | collective-permute-start | bytes 393224 | tf_op jit(solution)/shard_map/ppermute | solution.py:292
  324.1 16.4 %collective-permute-start.75 = (bf16[512,128]{1,0:T(8,128)(2,1)S(1)}, bf16[512,128]{1,0:T(8,128)(2,1)S(1)}, u32[]{:S(2)}, u32[]{:S(2)}) collective-permute-start(bf16[512,128]{1,0:T(8,128)(2,1)S(1)} %get-tuple-element.218), channel_id=1, source_target_pairs={{0,15},{1,14},{2,13},{3,12},{4,11},{5,10},{6,9},{7,8},{8,7},{9,6},... | collective-permute-start | bytes 393224 | tf_op jit(solution)/shard_map/ppermute | solution.py:292
  327.7 36.8 %collective-permute-start.35 = (bf16[128,128]{1,0:T(8,128)(2,1)S(1)}, bf16[128,128]{1,0:T(8,128)(2,1)S(1)}, u32[]{:S(2)}, u32[]{:S(2)}) collective-permute-start(bf16[128,128]{1,0:T(8,128)(2,1)S(1)} %get-tuple-element.161), channel_id=1, source_target_pairs={{0,6},{1,7},{2,4},{3,5},{4,2},{5,3},{6,0},{7,1},{8,14},{9,15},{10,... | collective-permute-start | bytes 98312 | tf_op jit(solution)/shard_map/ppermute | solution.py:292
  327.7 36.9 %collective-permute-start.36 = (bf16[128,128]{1,0:T(8,128)(2,1)S(1)}, bf16[128,128]{1,0:T(8,128)(2,1)S(1)}, u32[]{:S(2)}, u32[]{:S(2)}) collective-permute-start(bf16[128,128]{1,0:T(8,128)(2,1)S(1)} %get-tuple-element.162), channel_id=1, source_target_pairs={{0,7},{1,6},{2,5},{3,4},{4,3},{5,2},{6,1},{7,0},{8,15},{9,14},{10,... | collective-permute-start | bytes 98312 | tf_op jit(solution)/shard_map/ppermute | solution.py:292
  333.6 31.7 %collective-permute-start.37 = (bf16[128,128]{1,0:T(8,128)(2,1)S(1)}, bf16[128,128]{1,0:T(8,128)(2,1)S(1)}, u32[]{:S(2)}, u32[]{:S(2)}) collective-permute-start(bf16[128,128]{1,0:T(8,128)(2,1)S(1)} %get-tuple-element.163), channel_id=1, source_target_pairs={{0,8},{1,9},{2,10},{3,11},{4,12},{5,13},{6,14},{7,15},{8,0},{9,1},... | collective-permute-start | bytes 98312 | tf_op jit(solution)/shard_map/ppermute | solution.py:292
  337.3 29.1 %collective-permute-start.38 = (bf16[128,128]{1,0:T(8,128)(2,1)S(1)}, bf16[128,128]{1,0:T(8,128)(2,1)S(1)}, u32[]{:S(2)}, u32[]{:S(2)}) collective-permute-start(bf16[128,128]{1,0:T(8,128)(2,1)S(1)} %get-tuple-element.164), channel_id=1, source_target_pairs={{0,9},{1,8},{2,11},{3,10},{4,13},{5,12},{6,15},{7,14},{8,1},{9,0},... | collective-permute-start | bytes 98312 | tf_op jit(solution)/shard_map/ppermute | solution.py:292
  340.5 25.9 %collective-permute-start.39 = (bf16[128,128]{1,0:T(8,128)(2,1)S(1)}, bf16[128,128]{1,0:T(8,128)(2,1)S(1)}, u32[]{:S(2)}, u32[]{:S(2)}) collective-permute-start(bf16[128,128]{1,0:T(8,128)(2,1)S(1)} %get-tuple-element.165), channel_id=1, source_target_pairs={{0,10},{1,11},{2,8},{3,9},{4,14},{5,15},{6,12},{7,13},{8,2},{9,3},... | collective-permute-start | bytes 98312 | tf_op jit(solution)/shard_map/ppermute | solution.py:292
  366.4 37.7 %collective-permute-start.79 = (bf16[128,128]{1,0:T(8,128)(2,1)S(1)}, bf16[128,128]{1,0:T(8,128)(2,1)S(1)}, u32[]{:S(2)}, u32[]{:S(2)}) collective-permute-start(bf16[128,128]{1,0:T(8,128)(2,1)S(1)} %get-tuple-element.223), channel_id=1, source_target_pairs={{0,4},{1,5},{2,6},{3,7},{4,0},{5,1},{6,2},{7,3},{8,12},{9,13},{10,... | collective-permute-start | bytes 98312 | tf_op jit(solution)/shard_map/ppermute | solution.py:292
  366.4 39.4 %collective-permute-start.80 = (bf16[128,128]{1,0:T(8,128)(2,1)S(1)}, bf16[128,128]{1,0:T(8,128)(2,1)S(1)}, u32[]{:S(2)}, u32[]{:S(2)}) collective-permute-start(bf16[128,128]{1,0:T(8,128)(2,1)S(1)} %get-tuple-element.224), channel_id=1, source_target_pairs={{0,5},{1,4},{2,7},{3,6},{4,1},{5,0},{6,3},{7,2},{8,13},{9,12},{10,... | collective-permute-start | bytes 98312 | tf_op jit(solution)/shard_map/ppermute | solution.py:292
  368.1 39.5 %collective-permute-start.81 = (bf16[128,128]{1,0:T(8,128)(2,1)S(1)}, bf16[128,128]{1,0:T(8,128)(2,1)S(1)}, u32[]{:S(2)}, u32[]{:S(2)}) collective-permute-start(bf16[128,128]{1,0:T(8,128)(2,1)S(1)} %get-tuple-element.225), channel_id=1, source_target_pairs={{0,6},{1,7},{2,4},{3,5},{4,2},{5,3},{6,0},{7,1},{8,14},{9,15},{10,... | collective-permute-start | bytes 98312 | tf_op jit(solution)/shard_map/ppermute | solution.py:292
  368.8 40.4 %collective-permute-start.82 = (bf16[128,128]{1,0:T(8,128)(2,1)S(1)}, bf16[128,128]{1,0:T(8,128)(2,1)S(1)}, u32[]{:S(2)}, u32[]{:S(2)}) collective-permute-start(bf16[128,128]{1,0:T(8,128)(2,1)S(1)} %get-tuple-element.226), channel_id=1, source_target_pairs={{0,7},{1,6},{2,5},{3,4},{4,3},{5,2},{6,1},{7,0},{8,15},{9,14},{10,... | collective-permute-start | bytes 98312 | tf_op jit(solution)/shard_map/ppermute | solution.py:292
  370.8 40.6 %collective-permute-start.83 = (bf16[128,128]{1,0:T(8,128)(2,1)S(1)}, bf16[128,128]{1,0:T(8,128)(2,1)S(1)}, u32[]{:S(2)}, u32[]{:S(2)}) collective-permute-start(bf16[128,128]{1,0:T(8,128)(2,1)S(1)} %get-tuple-element.227), channel_id=1, source_target_pairs={{0,8},{1,9},{2,10},{3,11},{4,12},{5,13},{6,14},{7,15},{8,0},{9,1},... | collective-permute-start | bytes 98312 | tf_op jit(solution)/shard_map/ppermute | solution.py:292
  404.1 132.9 %collective-permute-start.91 = (bf16[1,128,2048]{2,1,0:T(8,128)(2,1)}, bf16[1,128,2048]{2,1,0:T(8,128)(2,1)S(1)}, u32[]{:S(2)}, u32[]{:S(2)}) collective-permute-start(bf16[1,128,2048]{2,1,0:T(8,128)(2,1)} %get-tuple-element.240.refs_3_), channel_id=1, source_target_pairs={{0,16},{16,0},{1,17},{17,1},{2,18},{18,2},{3,19},{19,3},{4,20},{20... | collective-permute-start | bytes 1572872 | tf_op jit(solution)/shard_map/ppermute | solution.py:283
  407.6 40.4 %collective-permute-start.85 = (bf16[128,128]{1,0:T(8,128)(2,1)S(1)}, bf16[128,128]{1,0:T(8,128)(2,1)S(1)}, u32[]{:S(2)}, u32[]{:S(2)}) collective-permute-start(bf16[128,128]{1,0:T(8,128)(2,1)S(1)} %get-tuple-element.229), channel_id=1, source_target_pairs={{0,10},{1,11},{2,8},{3,9},{4,14},{5,15},{6,12},{7,13},{8,2},{9,3},... | collective-permute-start | bytes 98312 | tf_op jit(solution)/shard_map/ppermute | solution.py:292
  409.2 39.8 %collective-permute-start.86 = (bf16[128,128]{1,0:T(8,128)(2,1)S(1)}, bf16[128,128]{1,0:T(8,128)(2,1)S(1)}, u32[]{:S(2)}, u32[]{:S(2)}) collective-permute-start(bf16[128,128]{1,0:T(8,128)(2,1)S(1)} %get-tuple-element.230), channel_id=1, source_target_pairs={{0,11},{1,10},{2,9},{3,8},{4,15},{5,14},{6,13},{7,12},{8,3},{9,2},... | collective-permute-start | bytes 98312 | tf_op jit(solution)/shard_map/ppermute | solution.py:292
  411.5 39.6 %collective-permute-start.87 = (bf16[128,128]{1,0:T(8,128)(2,1)S(1)}, bf16[128,128]{1,0:T(8,128)(2,1)S(1)}, u32[]{:S(2)}, u32[]{:S(2)}) collective-permute-start(bf16[128,128]{1,0:T(8,128)(2,1)S(1)} %get-tuple-element.231), channel_id=1, source_target_pairs={{0,12},{1,13},{2,14},{3,15},{4,8},{5,9},{6,10},{7,11},{8,4},{9,5},... | collective-permute-start | bytes 98312 | tf_op jit(solution)/shard_map/ppermute | solution.py:292
  413.2 40.2 %collective-permute-start.88 = (bf16[128,128]{1,0:T(8,128)(2,1)S(1)}, bf16[128,128]{1,0:T(8,128)(2,1)S(1)}, u32[]{:S(2)}, u32[]{:S(2)}) collective-permute-start(bf16[128,128]{1,0:T(8,128)(2,1)S(1)} %get-tuple-element.232), channel_id=1, source_target_pairs={{0,13},{1,12},{2,15},{3,14},{4,9},{5,8},{6,11},{7,10},{8,5},{9,4},... | collective-permute-start | bytes 98312 | tf_op jit(solution)/shard_map/ppermute | solution.py:292
  448.1 94.1 %collective-permute-start.92 = (bf16[1,128,2048]{2,1,0:T(8,128)(2,1)}, bf16[1,128,2048]{2,1,0:T(8,128)(2,1)S(1)}, u32[]{:S(2)}, u32[]{:S(2)}) collective-permute-start(bf16[1,128,2048]{2,1,0:T(8,128)(2,1)} %get-tuple-element.241.refs_4_), channel_id=1, source_target_pairs={{0,16},{16,0},{1,17},{17,1},{2,18},{18,2},{3,19},{19,3},{4,20},{20... | collective-permute-start | bytes 1572872 | tf_op jit(solution)/shard_map/ppermute | solution.py:283
  453.5 38.7 %collective-permute-start.40 = (bf16[128,128]{1,0:T(8,128)(2,1)S(1)}, bf16[128,128]{1,0:T(8,128)(2,1)S(1)}, u32[]{:S(2)}, u32[]{:S(2)}) collective-permute-start(bf16[128,128]{1,0:T(8,128)(2,1)S(1)} %copy-done.46), channel_id=1, source_target_pairs={{0,11},{1,10},{2,9},{3,8},{4,15},{5,14},{6,13},{7,12},{8,3},{9,2},... | collective-permute-start | bytes 98312 | tf_op jit(solution)/shard_map/ppermute | solution.py:292
  455.6 38.0 %collective-permute-start.41 = (bf16[128,128]{1,0:T(8,128)(2,1)S(1)}, bf16[128,128]{1,0:T(8,128)(2,1)S(1)}, u32[]{:S(2)}, u32[]{:S(2)}) collective-permute-start(bf16[128,128]{1,0:T(8,128)(2,1)S(1)} %copy-done.44), channel_id=1, source_target_pairs={{0,12},{1,13},{2,14},{3,15},{4,8},{5,9},{6,10},{7,11},{8,4},{9,5},... | collective-permute-start | bytes 98312 | tf_op jit(solution)/shard_map/ppermute | solution.py:292
  457.1 39.0 %collective-permute-start.42 = (bf16[128,128]{1,0:T(8,128)(2,1)S(1)}, bf16[128,128]{1,0:T(8,128)(2,1)S(1)}, u32[]{:S(2)}, u32[]{:S(2)}) collective-permute-start(bf16[128,128]{1,0:T(8,128)(2,1)S(1)} %copy-done.42), channel_id=1, source_target_pairs={{0,13},{1,12},{2,15},{3,14},{4,9},{5,8},{6,11},{7,10},{8,5},{9,4},... | collective-permute-start | bytes 98312 | tf_op jit(solution)/shard_map/ppermute | solution.py:292
  492.2 55.1 %collective-permute-start.93 = (bf16[1,128,2048]{2,1,0:T(8,128)(2,1)}, bf16[1,128,2048]{2,1,0:T(8,128)(2,1)S(1)}, u32[]{:S(2)}, u32[]{:S(2)}) collective-permute-start(bf16[1,128,2048]{2,1,0:T(8,128)(2,1)} %get-tuple-element.242.refs_4_), channel_id=1, source_target_pairs={{0,16},{16,0},{1,17},{17,1},{2,18},{18,2},{3,19},{19,3},{4,20},{20... | collective-permute-start | bytes 1572872 | tf_op jit(solution)/shard_map/ppermute | solution.py:283
  536.2 16.4 %collective-permute-start.94 = (bf16[1,128,2048]{2,1,0:T(8,128)(2,1)}, bf16[1,128,2048]{2,1,0:T(8,128)(2,1)S(1)}, u32[]{:S(2)}, u32[]{:S(2)}) collective-permute-start(bf16[1,128,2048]{2,1,0:T(8,128)(2,1)} %get-tuple-element.243.refs_4_), channel_id=1, source_target_pairs={{0,16},{16,0},{1,17},{17,1},{2,18},{18,2},{3,19},{19,3},{4,20},{20... | collective-permute-start | bytes 1572872 | tf_op jit(solution)/shard_map/ppermute | solution.py:283
  (120 other events, 4394.9 us)

commit v2 on v0

v2 whole, which is shorter than its diff:
```python
import functools
import math

import jax
import jax.numpy as jnp
from jax import lax
from jax.experimental import pallas as pl
from jax.experimental.pallas import tpu as pltpu
from jax.sharding import PartitionSpec as P

HEADS = 32
LANES = 128
VMEM_LIMIT = 48 * 1024 * 1024


def split_size(parts):
    return 1 << ((parts.bit_length() - 1) // 2)


def distances(me, near, far_first, outer, inner):
    shift_high, shift_low = (outer, inner) if far_first else (inner, outer)
    return (me // near ^ shift_high) * near + (me % near ^ shift_low)


def pack_kernel(near, far_first, per_chunk, rows, ahead, me_ref, *refs):
    sources, out_refs = refs[:3], refs[3 + ahead :]
    lane_blocks = sources[0].shape[3] // LANES
    for outer, out_ref in enumerate(out_refs):
        for inner in range(out_ref.shape[0]):
            block = distances(me_ref[0], near, far_first, outer, inner)
            video = 0 if per_chunk == 1 else block // lane_blocks
            column = block if per_chunk == 1 else block % lane_blocks
            lanes = pl.ds(pl.multiple_of(column * LANES, LANES), LANES)
            for which, source in enumerate(sources):
                here = slice(which * rows, (which + 1) * rows)
                out_ref[inner, here, :] = source[video, 0, :, lanes]


def pack(me, sources, first_batch, per_chunk, parts, far_first, after=()):
    batch_size, single, rows, width = sources[0].shape
    near = split_size(parts)
    count = parts // near if far_first else near
    spec = pl.BlockSpec(
        (per_chunk, 1, rows, width), lambda i: (first_batch // per_chunk, 0, 0, 0)
    )
    shape = (parts // count, 3 * rows, LANES)
    return pl.pallas_call(
        functools.partial(pack_kernel, near, far_first, per_chunk, rows, len(after)),
        grid=(1,),
        in_specs=[pl.BlockSpec(memory_space=pltpu.SMEM)]
        + [spec] * 3
        + [pl.BlockSpec(memory_space=pl.ANY)] * len(after),
        out_specs=[pl.BlockSpec(shape, lambda i: (0, 0, 0))] * count,
        out_shape=[jax.ShapeDtypeStruct(shape, sources[0].dtype)] * count,
        cost_estimate=pl.CostEstimate(
            flops=0, bytes_accessed=parts * 3 * rows * LANES * 4, transcendentals=0
        ),
        name="pack",
    )(me, *sources, *after)


def repack_kernel(count, *refs):
    in_refs, out_refs = refs[:count], refs[count:]
    for outer, out_ref in enumerate(out_refs):
        for inner, in_ref in enumerate(in_refs):
            out_ref[inner] = in_ref[outer]


def repack(blocks):
    count = len(blocks)
    far, rows, lanes = blocks[0].shape
    shape = (count, rows, lanes)
    return pl.pallas_call(
        functools.partial(repack_kernel, count),
        out_shape=[jax.ShapeDtypeStruct(shape, blocks[0].dtype)] * far,
        cost_estimate=pl.CostEstimate(
            flops=0, bytes_accessed=count * far * rows * lanes * 4, transcendentals=0
        ),
        name="repack",
    )(*blocks)


def attend_kernel(group, rows, parts, near, far_first, count, me_ref, *refs):
    in_refs = refs[:count]
    out_ref, query_scr, key_scr, value_scr = refs[-4:]
    step = pl.program_id(0)
    length = parts * rows
    head_width = LANES // 2

    def load(in_ref, index, place):
        here = pl.ds(pl.multiple_of(place * rows, rows), rows)
        query_scr[here, :] = in_ref[index, 0:rows, :]
        keys = in_ref[index, rows : 2 * rows, :]
        key_scr[here, 0:LANES] = keys
        key_scr[here, LANES : 2 * LANES] = keys
        value_scr[here, 0:LANES] = in_ref[index, 2 * rows : 3 * rows, :]

    @pl.when(step == 0)
    def _():
        value_scr[:, LANES : 2 * LANES] = jnp.ones((length, LANES), value_scr.dtype)
        for outer, in_ref in enumerate(in_refs):
            for inner in range(in_ref.shape[0]):
                load(in_ref, inner, distances(me_ref[0], near, far_first, outer, inner))

    block = group * rows
    here = pl.ds(pl.multiple_of(step * block, block), block)
    query = query_scr[here, :].astype(jnp.float32)
    query = query * (head_width ** (-0.5) * math.log2(math.e))
    high = query.astype(jnp.bfloat16)
    low = (query - high.astype(jnp.float32)).astype(jnp.bfloat16)
    pair = jnp.concatenate([high, low], axis=1)
    lane = lax.broadcasted_iota(jnp.int32, (block, 2 * LANES), 1) % LANES
    results = []
    for head in range(2):
        mine = (lane // head_width) == head
        masked = jnp.where(mine, pair, jnp.zeros_like(pair))
        scores = lax.dot_general(
            masked, key_scr[...], (((1,), (1,)), ((), ())), preferred_element_type=jnp.float32
        )
        top = jnp.max(scores, axis=-1, keepdims=True)
        weights = jnp.exp2(scores - top).astype(jnp.bfloat16)
        total = jnp.dot(weights, value_scr[...], preferred_element_type=jnp.float32)
        results.append(total[:, 0:LANES] / total[:, LANES : 2 * LANES])
    own = lax.broadcasted_iota(jnp.int32, (block, LANES), 1) // head_width
    merged = jnp.where(own == 0, results[0], results[1]).astype(out_ref.dtype)
    out_ref[...] = merged.reshape(group, rows, LANES)


def attend(me, arrived, parts, far_first, after=()):
    triple = arrived[0].shape[1]
    rows = triple // 3
    length = parts * rows
    dtype = arrived[0].dtype
    group = max(1, 256 // rows)
    count = len(arrived)
    return pl.pallas_call(
        functools.partial(
            attend_kernel, group, rows, parts, split_size(parts), far_first, count
        ),
        grid=(parts // group,),
        in_specs=[pl.BlockSpec(memory_space=pltpu.SMEM)]
        + [pl.BlockSpec(value.shape, lambda i: (0, 0, 0)) for value in arrived]
        + [pl.BlockSpec(memory_space=pl.ANY)] * len(after),
        out_specs=pl.BlockSpec((group, rows, LANES), lambda i: (i, 0, 0)),
        out_shape=jax.ShapeDtypeStruct((parts, rows, LANES), dtype),
        scratch_shapes=[
            pltpu.VMEM((length, LANES), dtype),
            pltpu.VMEM((length, 2 * LANES), dtype),
            pltpu.VMEM((length, 2 * LANES), dtype),
        ],
        compiler_params=pltpu.CompilerParams(vmem_limit_bytes=VMEM_LIMIT),
        cost_estimate=pl.CostEstimate(
            flops=2 * 2 * 2 * length * length * 256,
            bytes_accessed=parts * rows * LANES * 8,
            transcendentals=2 * length * length,
        ),
        name="attend",
    )(me, *arrived, *after)


def combine_kernel(views, group, carried, view_ref, *refs):
    refs = refs[carried:]
    query_ref = refs[0]
    key_refs = refs[1 : 1 + views]
    value_refs = refs[1 + views : 1 + 2 * views]
    spatial_ref, joined_ref = refs[1 + 2 * views :]
    head_width = LANES // 2
    source = (lax.broadcasted_iota(jnp.int32, (2 * LANES, LANES), 0) % LANES) // head_width
    target = lax.broadcasted_iota(jnp.int32, (2 * LANES, LANES), 1) // head_width
    spread = jnp.where(source == target, 1.0, 0.0).astype(jnp.bfloat16)
    for j in range(group):
        lanes = slice(j * LANES, (j + 1) * LANES)
        query = query_ref[0, 0, :, lanes].astype(jnp.float32)
        scores = []
        for key_ref in key_refs:
            product = query * key_ref[0, 0, 0, :, lanes].astype(jnp.float32)
            high = product.astype(jnp.bfloat16)
            low = (product - high.astype(jnp.float32)).astype(jnp.bfloat16)
            both = jnp.concatenate([high, low], axis=1)
            scores.append(
                jnp.dot(both, spread, preferred_element_type=jnp.float32)
                * (head_width ** (-0.5))
            )
        top = functools.reduce(jnp.maximum, scores)
        expo = [jnp.exp(score - top) for score in scores]
        inverse = 1.0 / functools.reduce(jnp.add, expo)
        joined = None
        for value_ref, part in zip(value_refs, expo):
            weight = (part * inverse).astype(jnp.bfloat16).astype(jnp.float32)
            term = weight * value_ref[j].astype(jnp.float32)
            joined = term if joined is None else joined + term
        joined_ref[0, 0, :, lanes] = joined.astype(joined_ref.dtype)
        spatial_ref[0, 0, :, lanes] = value_refs[0][j]


def combine(view, carry, view_queries, keys, outputs, first_batch):
    batch_size, single, rows, width = view_queries.shape
    parts = outputs[0].shape[0]
    views = len(outputs)
    group = 4
    steps = width // LANES // group

    def place(i, view_ref):
        return (first_batch + i // steps, 0, 0, i % steps)

    def key_place(shift, i, view_ref):
        return (view_ref[0] ^ shift,) + place(i, view_ref)

    wide = pl.BlockSpec((1, 1, rows, group * LANES), place)
    key_specs = [
        pl.BlockSpec((1, 1, 1, rows, group * LANES), functools.partial(key_place, shift))
        for shift in range(views)
    ]
    narrow = pl.BlockSpec((group, rows, LANES), lambda i, view_ref: (i, 0, 0))
    shape = jax.ShapeDtypeStruct(view_queries.shape, view_queries.dtype)
    carried = len(carry)
    return pl.pallas_call(
        functools.partial(combine_kernel, views, group, carried),
        grid_spec=pltpu.PrefetchScalarGridSpec(
            num_scalar_prefetch=1,
            grid=(parts // group,),
            in_specs=[pl.BlockSpec(memory_space=pl.ANY)] * carried
            + [wide]
            + key_specs
            + [narrow] * views,
            out_specs=[wide, wide],
        ),
        out_shape=[shape, shape],
        input_output_aliases={1 + i: i for i in range(carried)},
        cost_estimate=pl.CostEstimate(
            flops=parts * rows * LANES * 1024 * views,
            bytes_accessed=parts * rows * LANES * 2 * (2 * views + 3),
            transcendentals=parts * rows * LANES * (views + 1),
        ),
        name="combine",
    )(view, *carry, view_queries, *[keys] * views, *outputs)


def swap(blocks, axis, size, stride):
    return [blocks[0]] + [
        lax.ppermute(blocks[shift], axis, [(i, i ^ (shift * stride)) for i in range(size)])
        for shift in range(1, len(blocks))
    ]


def local(seq_size, views, queries, key_rows, value_rows, view_queries):
    batch_size, single, rows, width = queries.shape
    per_chunk = seq_size // (width // LANES)
    chunks = batch_size // per_chunk
    near = split_size(seq_size)
    me = lax.axis_index("seq").astype(jnp.int32).reshape(1)
    view = lax.axis_index("view").astype(jnp.int32).reshape(1)
    exchange = functools.partial(
        lax.all_to_all, axis_name="seq", split_axis=0, concat_axis=0, tiled=True
    )
    keys = lax.all_gather(key_rows, "view")
    sources = (queries, key_rows, value_rows)
    received, first_packed, after = [], [], ()
    for c in range(chunks):
        strides = (near, 1) if c == 0 else (1, near)
        packed = pack(me, sources, c * per_chunk, per_chunk, seq_size, c == 0, after)
        first_packed.append(packed[0])
        blocks = repack(swap(packed, "seq", seq_size, strides[0]))
        after = (packed[0],) if c == 0 else (blocks[0],)
        received.append(swap(blocks, "seq", seq_size, strides[1]))
    carry, attended = (), ()
    for c in range(chunks):
        after = attended + tuple(first_packed[c + 2 : c + 3])
        if c == 1:
            after += (keys,)
        attended = (attend(me, received[c], seq_size, c > 0, after),)
        returned = exchange(attended[0])
        outputs = swap([returned] * views, "view", views, 1)
        carry = combine(view, carry, view_queries, keys, outputs, c * per_chunk)
    return tuple(carry)


def solution(mesh):
    spec = P(None, "view", "seq", None)
    return jax.shard_map(
        functools.partial(local, mesh.shape["seq"], mesh.shape["view"]),
        mesh=mesh,
        in_specs=(spec,) * 4,
        out_specs=(spec, spec),
        check_vma=False,
    )
```

time: 506 us -> 323 us (0.64)
  matrix products: 171 us -> 0 us
  Pallas kernels: 0 us -> 108 us
  local copies, waits for them, and re-layouts: 99.9 us -> 8.25 us
  waiting for transfers between devices: 170 us -> 116 us
  starting transfers between devices: 59.3 us -> 76 us
  between operations: 0.77 us -> 14.2 us
    all_to_all x8 -> x4, waiting for transfers between devices: 170 us -> 10.8 us  [local(): returned = exchange(attended[0])]
    pallas_call x0 -> x16, Pallas kernels: none -> 108 us  [the longest x4 67.9 us: attend(): pl.pallas_call(functools.partial(attend_kernel, group, rows, parts, split...]
    ppermute x0 -> x28, waiting for transfers between devices: none -> 104 us  [swap(): lax.ppermute(blocks[shift], axis, [(i, i ^ shift * stride) for i in range...]
    sub x5 -> x0, matrix products: 98.7 us -> none  [the longest x4 66.9 us: one_block(): scores = scores - jnp.max(scores, axis=-1, keepdims=True)]
    dot_general x5 -> x0, matrix products: 71.9 us -> none  [the longest x4 58.7 us: one_block(): jnp.einsum('pqk,kpe->qpe', weights, value_pairs, preferred_element_type=j...]
    reshape x8 -> x0, local copies, waits for them, and re-layouts: 40.7 us -> none  [the longest x2 9.43 us: apply_weights(): result.astype(jnp.bfloat16)]
    ppermute x0 -> x28, starting transfers between devices: none -> 37.1 us  [swap(): lax.ppermute(blocks[shift], axis, [(i, i ^ shift * stride) for i in range...]
    unnamed x18 -> x48, local copies, waits for them, and re-layouts: 38.7 us -> 8.25 us
  transfers between devices with their start and end apart: 8 -> 33, of which waited for: 6 -> 12; matrix products, arithmetic and copies ran while one was open for 44% -> 0% of each run, Pallas kernels for 0% -> 32%
where the time goes in v2:
time: 323 us; the launch traced here: 322 us
  waiting for transfers between devices  116 us (36%)
  Pallas kernels  108 us (33%)
  starting transfers between devices  76 us (24%)
  between operations  14.2 us (4%)
  local copies, waits for them, and re-layouts  8.25 us (3%)
    ppermute x28, waiting for transfers between devices, swap(): lax.ppermute(blocks[shift], axis, [(i, i ^ shift * stride) for i in range...  104 us
    pallas_call x4, Pallas kernels, attend(): pl.pallas_call(functools.partial(attend_kernel, group, rows, parts, split...  67.9 us
    all_to_all x4, starting transfers between devices, local(): returned = exchange(attended[0])  38.9 us
    ppermute x28, starting transfers between devices, swap(): lax.ppermute(blocks[shift], axis, [(i, i ^ shift * stride) for i in range...  37.1 us
    pallas_call x4, Pallas kernels, combine(): pl.pallas_call(functools.partial(combine_kernel, views, group, carried),...  17.7 us
    pallas_call x4, Pallas kernels, pack(): pl.pallas_call(functools.partial(pack_kernel, near, far_first, per_chunk,...  11.8 us
    all_to_all x4, waiting for transfers between devices, local(): returned = exchange(attended[0])  10.8 us
    pallas_call x4, Pallas kernels, repack(): pl.pallas_call(functools.partial(repack_kernel, count), out_shape=[jax.Sh...  10.4 us
  transfers between devices with their start and end apart: 33, of which 12 were waited for; matrix products, arithmetic and copies ran while one was open for 0% of the time, Pallas kernels for 32%

profile of v2, /device:TPU:0, one launch (start us, length us, event | category | flops | bytes accessed | tf_op | source)
XLA Modules:
  0.0 321.7 jit_solution(1773557906464044480)
XLA Ops:
  7.2 0.7 all-gather.3.cloned.1.call-update
  7.9 2.9 pack.4
  10.8 3.0 collective-permute-start
  13.9 2.6 collective-permute-start.1
  16.4 2.9 pack.5
  19.4 1.7 collective-permute-start.7
  21.1 9.7 %collective-permute-done.refs_1_ = bf16[4,384,128]{2,1,0:T(8,128)(2,1)S(1)} collective-permute-done((bf16[4,384,128]{2,1,0:T(8,128)(2,1)}, bf16[4,384,128]{2,1,0:T(8,128)(2,1)S(1)}, u32[]{:S(2)}, u32[]{:S(2)}) %collective-permute-start) | collective-permute-done | bytes 393248 | tf_op jit(solution)/shard_map/ppermute | solution.py:241
  31.2 12.7 %collective-permute-done.1.refs_2_ = bf16[4,384,128]{2,1,0:T(8,128)(2,1)S(1)} collective-permute-done((bf16[4,384,128]{2,1,0:T(8,128)(2,1)}, bf16[4,384,128]{2,1,0:T(8,128)(2,1)S(1)}, u32[]{:S(2)}, u32[]{:S(2)}) %collective-permute-start.1) | collective-permute-done | bytes 393248 | tf_op jit(solution)/shard_map/ppermute | solution.py:241
  43.9 0.8 copy-done.17
  44.7 0.8 copy-done.18
  45.4 2.6 repack.4
  48.0 1.5 collective-permute-start.4
  49.5 0.4 collective-permute-start.5
  49.9 0.4 copy-done.13
  50.3 0.4 copy-done.14
  50.8 2.6 repack.5
  53.4 2.9 pack.6
  56.6 6.8 %collective-permute-start.10 = (bf16[4,384,128]{2,1,0:T(8,128)(2,1)}, bf16[4,384,128]{2,1,0:T(8,128)(2,1)S(1)}, u32[]{:S(2)}, u32[]{:S(2)}) collective-permute-start(bf16[4,384,128]{2,1,0:T(8,128)(2,1)} %get-tuple-element.56), channel_id=1, source_target_pairs={{0,4},{1,5},{2,6},{3,7},{4,0},{5,1},{6,2},{7,3},{8,12},{9,13},{10,... | collective-permute-start | bytes 1179656 | tf_op jit(solution)/shard_map/ppermute | solution.py:241
  63.4 1.0 collective-permute-start.11
  64.4 1.5 collective-permute-start.12
  65.9 1.8 collective-permute-done.5.refs_3_
  67.8 1.5 collective-permute-start.14
  69.3 0.5 collective-permute-start.15
  70.1 1.0 copy-done.1
  71.1 17.0 %attend.4.refs_4_ = bf16[16,128,128]{2,1,0:T(8,128)(2,1)} custom-call(s32[1]{0:T(128)} %bitcast.2.me_ref, bf16[4,384,128]{2,1,0:T(8,128)(2,1)S(1)} %copy-done.4, bf16[4,384,128]{2,1,0:T(8,128)(2,1)S(1)} %collective-permute-done.3.refs_1_, bf16[4,384,128]{2,1,0:T(8,128)(2,1)S(1)} %collective-permute-done.4.refs_2_, ...), custom_call_target="tpu_custom_call" | custom-call | flops 8589934592 | bytes 2097152 | tf_op jit(solution)/shard_map/attend/pallas_call | solution.py:136
  88.0 9.7 %all-to-all-start = ((bf16[16,128,128]{2,1,0:T(8,128)(2,1)}), bf16[16,128,128]{2,1,0:T(8,128)(2,1)S(1)}, u32[]{:S(2)}, u32[]{:S(2)}) async-start(bf16[16,128,128]{2,1,0:T(8,128)(2,1)} %attend.4.refs_4_), calls=%async_computation | async-start | bytes 1048576 | tf_op jit(solution)/shard_map/all_to_all | solution.py:272
  97.8 2.6 repack.6
  100.4 1.9 collective-permute-start.17
  102.3 2.4 collective-permute-start.18
  104.7 3.0 pack.7
  107.8 1.0 copy-done
  108.8 17.0 %attend.5.refs_4_ = bf16[16,128,128]{2,1,0:T(8,128)(2,1)} custom-call(s32[1]{0:T(128)} %bitcast.2.me_ref, bf16[4,384,128]{2,1,0:T(8,128)(2,1)S(1)} %copy-done.2, bf16[4,384,128]{2,1,0:T(8,128)(2,1)S(1)} %collective-permute-done.10.refs_1_, bf16[4,384,128]{2,1,0:T(8,128)(2,1)S(1)} %collective-permute-done.11.refs_2_, ...), custom_call_target="tpu_custom_call" | custom-call | flops 8589934592 | bytes 2097152 | tf_op jit(solution)/shard_map/attend/pallas_call | solution.py:136
  125.7 13.1 %collective-permute-done.18.refs_2_ = bf16[4,384,128]{2,1,0:T(8,128)(2,1)S(1)} collective-permute-done((bf16[4,384,128]{2,1,0:T(8,128)(2,1)}, bf16[4,384,128]{2,1,0:T(8,128)(2,1)S(1)}, u32[]{:S(2)}, u32[]{:S(2)}) %collective-permute-start.18) | collective-permute-done | bytes 393248 | tf_op jit(solution)/shard_map/ppermute | solution.py:241
  138.8 17.0 %attend.6.refs_4_ = bf16[16,128,128]{2,1,0:T(8,128)(2,1)} custom-call(s32[1]{0:T(128)} %bitcast.2.me_ref, bf16[4,384,128]{2,1,0:T(8,128)(2,1)S(1)} %copy-done.3, bf16[4,384,128]{2,1,0:T(8,128)(2,1)S(1)} %collective-permute-done.17.refs_1_, bf16[4,384,128]{2,1,0:T(8,128)(2,1)S(1)} %collective-permute-done.18.refs_2_, ...), custom_call_target="tpu_custom_call" | custom-call | flops 8589934592 | bytes 2097152 | tf_op jit(solution)/shard_map/attend/pallas_call | solution.py:136
  155.8 10.8 %all-to-all-start.2 = ((bf16[16,128,128]{2,1,0:T(8,128)(2,1)}), bf16[16,128,128]{2,1,0:T(8,128)(2,1)S(1)}, u32[]{:S(2)}, u32[]{:S(2)}) async-start(bf16[16,128,128]{2,1,0:T(8,128)(2,1)} %attend.6.refs_4_), calls=%async_computation.2 | async-start | bytes 1048576 | tf_op jit(solution)/shard_map/all_to_all | solution.py:272
  166.6 0.4 collective-permute-start.21
  167.0 1.7 collective-permute-start.22
  168.7 15.5 %collective-permute-done.22.refs_2_ = bf16[4,384,128]{2,1,0:T(8,128)(2,1)S(1)} collective-permute-done((bf16[4,384,128]{2,1,0:T(8,128)(2,1)S(1)}, bf16[4,384,128]{2,1,0:T(8,128)(2,1)S(1)}, u32[]{:S(2)}, u32[]{:S(2)}) %collective-permute-start.22) | collective-permute-done | bytes 393248 | tf_op jit(solution)/shard_map/ppermute | solution.py:241
  184.3 7.5 %collective-permute-done.23.refs_3_ = bf16[4,384,128]{2,1,0:T(8,128)(2,1)S(1)} collective-permute-done((bf16[4,384,128]{2,1,0:T(8,128)(2,1)S(1)}, bf16[4,384,128]{2,1,0:T(8,128)(2,1)S(1)}, u32[]{:S(2)}, u32[]{:S(2)}) %collective-permute-start.23) | collective-permute-done | bytes 393248 | tf_op jit(solution)/shard_map/ppermute | solution.py:241
  191.7 0.8 copy-done.21
  192.5 2.6 repack.7
  195.1 1.5 collective-permute-start.24
  196.6 2.5 collective-permute-start.25
  199.1 0.5 collective-permute-start.26
  199.5 4.8 %all-to-all-start.1 = ((bf16[16,128,128]{2,1,0:T(8,128)(2,1)}), bf16[16,128,128]{2,1,0:T(8,128)(2,1)S(1)}, u32[]{:S(2)}, u32[]{:S(2)}) async-start(bf16[16,128,128]{2,1,0:T(8,128)(2,1)} %attend.5.refs_4_), calls=%async_computation.1 | async-start | bytes 1048576 | tf_op jit(solution)/shard_map/all_to_all | solution.py:272
  204.3 10.8 %collective-permute-done.24.refs_1_ = bf16[4,384,128]{2,1,0:T(8,128)(2,1)S(1)} collective-permute-done((bf16[4,384,128]{2,1,0:T(8,128)(2,1)}, bf16[4,384,128]{2,1,0:T(8,128)(2,1)S(1)}, u32[]{:S(2)}, u32[]{:S(2)}) %collective-permute-start.24) | collective-permute-done | bytes 393248 | tf_op jit(solution)/shard_map/ppermute | solution.py:241
  215.1 14.8 %collective-permute-done.25.refs_2_ = bf16[4,384,128]{2,1,0:T(8,128)(2,1)S(1)} collective-permute-done((bf16[4,384,128]{2,1,0:T(8,128)(2,1)}, bf16[4,384,128]{2,1,0:T(8,128)(2,1)S(1)}, u32[]{:S(2)}, u32[]{:S(2)}) %collective-permute-start.25) | collective-permute-done | bytes 393248 | tf_op jit(solution)/shard_map/ppermute | solution.py:241
  230.0 1.0 copy-done.5
  231.0 17.0 %attend.7 = bf16[16,128,128]{2,1,0:T(8,128)(2,1)} custom-call(s32[1]{0:T(128)} %bitcast.2.me_ref, bf16[4,384,128]{2,1,0:T(8,128)(2,1)S(1)} %copy-done.5, bf16[4,384,128]{2,1,0:T(8,128)(2,1)S(1)} %collective-permute-done.24.refs_1_, bf16[4,384,128]{2,1,0:T(8,128)(2,1)S(1)} %collective-permute-done.25.refs_2_, ...), custom_call_target="tpu_custom_call" | custom-call | flops 8589934592 | bytes 2097152 | tf_op jit(solution)/shard_map/attend/pallas_call | solution.py:136
  247.9 13.6 %all-to-all-start.3 = ((bf16[16,128,128]{2,1,0:T(8,128)(2,1)}), bf16[16,128,128]{2,1,0:T(8,128)(2,1)S(1)}, u32[]{:S(2)}, u32[]{:S(2)}) async-start(bf16[16,128,128]{2,1,0:T(8,128)(2,1)} %attend.7), calls=%async_computation.3 | async-start | bytes 1048576 | tf_op jit(solution)/shard_map/all_to_all | solution.py:272
  261.6 1.6 collective-permute-start.9
  263.2 0.5 collective-permute-start.16
  263.7 1.5 collective-permute-start.20
  265.2 10.8 %all-to-all-done.3.refs_5_ = bf16[16,128,128]{2,1,0:T(8,128)(2,1)S(1)} async-done(((bf16[16,128,128]{2,1,0:T(8,128)(2,1)}), bf16[16,128,128]{2,1,0:T(8,128)(2,1)S(1)}, u32[]{:S(2)}, u32[]{:S(2)}) %all-to-all-start.3) | async-done | bytes 524320 | tf_op jit(solution)/shard_map/all_to_all | solution.py:272
  276.0 1.5 collective-permute-start.27
  277.6 4.4 %combine.4 = (bf16[4,1,128,2048]{3,2,1,0:T(8,128)(2,1)}, bf16[4,1,128,2048]{3,2,1,0:T(8,128)(2,1)}) custom-call(s32[1]{0:T(128)} %bitcast.view_ref, bf16[4,1,128,2048]{3,2,1,0:T(8,128)(2,1)} %refs_2_.13, bf16[2,4,1,128,2048]{4,3,2,1,0:T(8,128)(2,1)} %bitcast.4, bf16[2,4,1,128,2048]{4,3,2,1,0:T(8,128)(2,1)} %bitcast.5, bf16[16,128,128]{2,1,0:T(8,128)(2,1)} %copy-done.6, ...), custom_call_target="tpu_custom_call" | custom-call | flops 536870912 | bytes 3670016 | tf_op jit(solution)/shard_map/combine/pallas_call | solution.py:217
  282.0 5.7 %collective-permute-done.16.refs_6_ = bf16[16,128,128]{2,1,0:T(8,128)(2,1)} collective-permute-done((bf16[16,128,128]{2,1,0:T(8,128)(2,1)S(1)}, bf16[16,128,128]{2,1,0:T(8,128)(2,1)}, u32[]{:S(2)}, u32[]{:S(2)}) %collective-permute-start.16) | collective-permute-done | bytes 524320 | tf_op jit(solution)/shard_map/ppermute | solution.py:241
  287.7 4.4 %combine.5 = (bf16[4,1,128,2048]{3,2,1,0:T(8,128)(2,1)}, bf16[4,1,128,2048]{3,2,1,0:T(8,128)(2,1)}) custom-call(s32[1]{0:T(128)} %bitcast.view_ref, bf16[4,1,128,2048]{3,2,1,0:T(8,128)(2,1)} %get-tuple-element.54.refs_0_, bf16[4,1,128,2048]{3,2,1,0:T(8,128)(2,1)} %get-tuple-element.55.refs_1_, ...), custom_call_target="tpu_custom_call", output_to_operand_aliasing={{0}: (1, {}), {1}: (2, {})} | custom-call | flops 536870912 | bytes 3670016 | tf_op jit(solution)/shard_map/combine/pallas_call | solution.py:217
  292.1 6.7 %collective-permute-done.20.refs_6_ = bf16[16,128,128]{2,1,0:T(8,128)(2,1)S(1)} collective-permute-done((bf16[16,128,128]{2,1,0:T(8,128)(2,1)S(1)}, bf16[16,128,128]{2,1,0:T(8,128)(2,1)S(1)}, u32[]{:S(2)}, u32[]{:S(2)}) %collective-permute-start.20) | collective-permute-done | bytes 524320 | tf_op jit(solution)/shard_map/ppermute | solution.py:241
  298.8 0.8 copy-done.11
  299.7 4.4 %combine.6 = (bf16[4,1,128,2048]{3,2,1,0:T(8,128)(2,1)}, bf16[4,1,128,2048]{3,2,1,0:T(8,128)(2,1)}) custom-call(s32[1]{0:T(128)} %bitcast.view_ref, bf16[4,1,128,2048]{3,2,1,0:T(8,128)(2,1)} %get-tuple-element.64.refs_0_, bf16[4,1,128,2048]{3,2,1,0:T(8,128)(2,1)} %get-tuple-element.65.refs_1_, ...), custom_call_target="tpu_custom_call", output_to_operand_aliasing={{0}: (1, {}), {1}: (2, {})} | custom-call | flops 536870912 | bytes 3670016 | tf_op jit(solution)/shard_map/combine/pallas_call | solution.py:217
  304.1 5.5 %collective-permute-done.27.refs_6_ = bf16[16,128,128]{2,1,0:T(8,128)(2,1)S(1)} collective-permute-done((bf16[16,128,128]{2,1,0:T(8,128)(2,1)S(1)}, bf16[16,128,128]{2,1,0:T(8,128)(2,1)S(1)}, u32[]{:S(2)}, u32[]{:S(2)}) %collective-permute-start.27) | collective-permute-done | bytes 524320 | tf_op jit(solution)/shard_map/ppermute | solution.py:241
  309.6 0.8 copy-done.10
  310.4 4.4 %combine.7 = (bf16[4,1,128,2048]{3,2,1,0:T(8,128)(2,1)}, bf16[4,1,128,2048]{3,2,1,0:T(8,128)(2,1)}) custom-call(s32[1]{0:T(128)} %bitcast.view_ref, bf16[4,1,128,2048]{3,2,1,0:T(8,128)(2,1)} %get-tuple-element.69.refs_0_, bf16[4,1,128,2048]{3,2,1,0:T(8,128)(2,1)} %get-tuple-element.70.refs_1_, ...), custom_call_target="tpu_custom_call", output_to_operand_aliasing={{0}: (1, {}), {1}: (2, {})} | custom-call | flops 536870912 | bytes 3670016 | tf_op jit(solution)/shard_map/combine/pallas_call | solution.py:217
  (67 shorter events, 1.4 us)
Async XLA Ops:
  7.2 100.6 %all-gather.3.cloned.1.call-start = ((), (), s32[]{:S(2)}) async-start(), calls=%async_computation.4 | async-start | bytes 6291456 | tf_op jit(solution)/shard_map/all_gather | solution.py:256
  10.8 20.0 %collective-permute-start = (bf16[4,384,128]{2,1,0:T(8,128)(2,1)}, bf16[4,384,128]{2,1,0:T(8,128)(2,1)S(1)}, u32[]{:S(2)}, u32[]{:S(2)}) collective-permute-start(bf16[4,384,128]{2,1,0:T(8,128)(2,1)} %get-tuple-element.41), channel_id=1, source_target_pairs={{0,4},{1,5},{2,6},{3,7},{4,0},{5,1},{6,2},{7,3},{8,12},{9,13},{10,... | collective-permute-start | bytes 1179656 | tf_op jit(solution)/shard_map/ppermute | solution.py:241
  13.9 30.0 %collective-permute-start.1 = (bf16[4,384,128]{2,1,0:T(8,128)(2,1)}, bf16[4,384,128]{2,1,0:T(8,128)(2,1)S(1)}, u32[]{:S(2)}, u32[]{:S(2)}) collective-permute-start(bf16[4,384,128]{2,1,0:T(8,128)(2,1)} %get-tuple-element.42), channel_id=1, source_target_pairs={{0,8},{1,9},{2,10},{3,11},{4,12},{5,13},{6,14},{7,15},{8,0},{9,1},... | collective-permute-start | bytes 1179656 | tf_op jit(solution)/shard_map/ppermute | solution.py:241
  16.4 27.4 %collective-permute-start.2 = (bf16[4,384,128]{2,1,0:T(8,128)(2,1)}, bf16[4,384,128]{2,1,0:T(8,128)(2,1)S(1)}, u32[]{:S(2)}, u32[]{:S(2)}) collective-permute-start(bf16[4,384,128]{2,1,0:T(8,128)(2,1)} %get-tuple-element.43), channel_id=1, source_target_pairs={{0,12},{1,13},{2,14},{3,15},{4,8},{5,9},{6,10},{7,11},{8,4},{9,5},... | collective-permute-start | bytes 1179656 | tf_op jit(solution)/shard_map/ppermute | solution.py:241
  19.4 30.1 %collective-permute-start.6 = (bf16[4,384,128]{2,1,0:T(8,128)(2,1)}, bf16[4,384,128]{2,1,0:T(8,128)(2,1)S(1)}, u32[]{:S(2)}, u32[]{:S(2)}) collective-permute-start(bf16[4,384,128]{2,1,0:T(8,128)(2,1)} %get-tuple-element.49), channel_id=1, source_target_pairs={{0,1},{1,0},{2,3},{3,2},{4,5},{5,4},{6,7},{7,6},{8,9},{9,8},{10,11... | collective-permute-start | bytes 1179656 | tf_op jit(solution)/shard_map/ppermute | solution.py:241
  19.4 30.5 %collective-permute-start.7 = (bf16[4,384,128]{2,1,0:T(8,128)(2,1)}, bf16[4,384,128]{2,1,0:T(8,128)(2,1)S(1)}, u32[]{:S(2)}, u32[]{:S(2)}) collective-permute-start(bf16[4,384,128]{2,1,0:T(8,128)(2,1)} %get-tuple-element.50), channel_id=1, source_target_pairs={{0,2},{1,3},{2,0},{3,1},{4,6},{5,7},{6,4},{7,5},{8,10},{9,11},{10,... | collective-permute-start | bytes 1179656 | tf_op jit(solution)/shard_map/ppermute | solution.py:241
  30.8 13.0 %copy-start.16 = (bf16[4,384,128]{2,1,0:T(8,128)(2,1)}, bf16[4,384,128]{2,1,0:T(8,128)(2,1)S(1)}, u32[]{:S(2)}) copy-start(bf16[4,384,128]{2,1,0:T(8,128)(2,1)S(1)} %collective-permute-done.refs_1_) | copy-start | bytes 1179652
  30.8 19.0 %collective-permute-start.8 = (bf16[4,384,128]{2,1,0:T(8,128)(2,1)}, bf16[4,384,128]{2,1,0:T(8,128)(2,1)S(1)}, u32[]{:S(2)}, u32[]{:S(2)}) collective-permute-start(bf16[4,384,128]{2,1,0:T(8,128)(2,1)} %get-tuple-element.51), channel_id=1, source_target_pairs={{0,3},{1,2},{2,1},{3,0},{4,7},{5,6},{6,5},{7,4},{8,11},{9,10},{10,... | collective-permute-start | bytes 1179656 | tf_op jit(solution)/shard_map/ppermute | solution.py:241
  43.9 0.8 copy-start.17
  44.7 0.8 copy-start.18
  48.0 15.4 %collective-permute-start.3 = (bf16[4,384,128]{2,1,0:T(8,128)(2,1)}, bf16[4,384,128]{2,1,0:T(8,128)(2,1)S(1)}, u32[]{:S(2)}, u32[]{:S(2)}) collective-permute-start(bf16[4,384,128]{2,1,0:T(8,128)(2,1)} %get-tuple-element.45), channel_id=1, source_target_pairs={{0,1},{1,0},{2,3},{3,2},{4,5},{5,4},{6,7},{7,6},{8,9},{9,8},{10,11... | collective-permute-start | bytes 1179656 | tf_op jit(solution)/shard_map/ppermute | solution.py:241
  48.0 16.4 %collective-permute-start.4 = (bf16[4,384,128]{2,1,0:T(8,128)(2,1)}, bf16[4,384,128]{2,1,0:T(8,128)(2,1)S(1)}, u32[]{:S(2)}, u32[]{:S(2)}) collective-permute-start(bf16[4,384,128]{2,1,0:T(8,128)(2,1)} %get-tuple-element.46), channel_id=1, source_target_pairs={{0,2},{1,3},{2,0},{3,1},{4,6},{5,7},{6,4},{7,5},{8,10},{9,11},{10,... | collective-permute-start | bytes 1179656 | tf_op jit(solution)/shard_map/ppermute | solution.py:241
  49.5 0.7 copy-start.13
  49.5 18.3 %collective-permute-start.5 = (bf16[4,384,128]{2,1,0:T(8,128)(2,1)}, bf16[4,384,128]{2,1,0:T(8,128)(2,1)S(1)}, u32[]{:S(2)}, u32[]{:S(2)}) collective-permute-start(bf16[4,384,128]{2,1,0:T(8,128)(2,1)} %get-tuple-element.47), channel_id=1, source_target_pairs={{0,3},{1,2},{2,1},{3,0},{4,7},{5,6},{6,5},{7,4},{8,11},{9,10},{10,... | collective-permute-start | bytes 1179656 | tf_op jit(solution)/shard_map/ppermute | solution.py:241
  49.9 0.7 copy-start.14
  49.9 0.9 copy-start.15
  53.4 16.7 %copy-start.4 = (bf16[4,384,128]{2,1,0:T(8,128)(2,1)S(1)}, bf16[4,384,128]{2,1,0:T(8,128)(2,1)}, u32[]{:S(2)}) copy-start(bf16[4,384,128]{2,1,0:T(8,128)(2,1)} %get-tuple-element.44.refs_0_) | copy-start | bytes 1179652
  56.3 13.0 %collective-permute-start.13 = (bf16[4,384,128]{2,1,0:T(8,128)(2,1)}, bf16[4,384,128]{2,1,0:T(8,128)(2,1)S(1)}, u32[]{:S(2)}, u32[]{:S(2)}) collective-permute-start(bf16[4,384,128]{2,1,0:T(8,128)(2,1)} %get-tuple-element.59), channel_id=1, source_target_pairs={{0,1},{1,0},{2,3},{3,2},{4,5},{5,4},{6,7},{7,6},{8,9},{9,8},{10,11... | collective-permute-start | bytes 1179656 | tf_op jit(solution)/shard_map/ppermute | solution.py:241
  56.6 51.0 %collective-permute-start.10 = (bf16[4,384,128]{2,1,0:T(8,128)(2,1)}, bf16[4,384,128]{2,1,0:T(8,128)(2,1)S(1)}, u32[]{:S(2)}, u32[]{:S(2)}) collective-permute-start(bf16[4,384,128]{2,1,0:T(8,128)(2,1)} %get-tuple-element.56), channel_id=1, source_target_pairs={{0,4},{1,5},{2,6},{3,7},{4,0},{5,1},{6,2},{7,3},{8,12},{9,13},{10,... | collective-permute-start | bytes 1179656 | tf_op jit(solution)/shard_map/ppermute | solution.py:241
  63.4 44.3 %collective-permute-start.11 = (bf16[4,384,128]{2,1,0:T(8,128)(2,1)}, bf16[4,384,128]{2,1,0:T(8,128)(2,1)S(1)}, u32[]{:S(2)}, u32[]{:S(2)}) collective-permute-start(bf16[4,384,128]{2,1,0:T(8,128)(2,1)} %get-tuple-element.57), channel_id=1, source_target_pairs={{0,8},{1,9},{2,10},{3,11},{4,12},{5,13},{6,14},{7,15},{8,0},{9,1},... | collective-permute-start | bytes 1179656 | tf_op jit(solution)/shard_map/ppermute | solution.py:241
  64.4 43.3 %collective-permute-start.12 = (bf16[4,384,128]{2,1,0:T(8,128)(2,1)}, bf16[4,384,128]{2,1,0:T(8,128)(2,1)S(1)}, u32[]{:S(2)}, u32[]{:S(2)}) collective-permute-start(bf16[4,384,128]{2,1,0:T(8,128)(2,1)} %get-tuple-element.58), channel_id=1, source_target_pairs={{0,12},{1,13},{2,14},{3,15},{4,8},{5,9},{6,10},{7,11},{8,4},{9,5},... | collective-permute-start | bytes 1179656 | tf_op jit(solution)/shard_map/ppermute | solution.py:241
  67.8 30.0 %collective-permute-start.14 = (bf16[4,384,128]{2,1,0:T(8,128)(2,1)}, bf16[4,384,128]{2,1,0:T(8,128)(2,1)}, u32[]{:S(2)}, u32[]{:S(2)}) collective-permute-start(bf16[4,384,128]{2,1,0:T(8,128)(2,1)} %get-tuple-element.60), channel_id=1, source_target_pairs={{0,2},{1,3},{2,0},{3,1},{4,6},{5,7},{6,4},{7,5},{8,10},{9,11},{10,... | collective-permute-start | bytes 1179656 | tf_op jit(solution)/shard_map/ppermute | solution.py:241
  69.3 0.8 copy-start.12
  69.3 28.5 %collective-permute-start.15 = (bf16[4,384,128]{2,1,0:T(8,128)(2,1)}, bf16[4,384,128]{2,1,0:T(8,128)(2,1)}, u32[]{:S(2)}, u32[]{:S(2)}) collective-permute-start(bf16[4,384,128]{2,1,0:T(8,128)(2,1)} %get-tuple-element.61), channel_id=1, source_target_pairs={{0,3},{1,2},{2,1},{3,0},{4,7},{5,6},{6,5},{7,4},{8,11},{9,10},{10,... | collective-permute-start | bytes 1179656 | tf_op jit(solution)/shard_map/ppermute | solution.py:241
  70.1 1.0 copy-start.1
  88.0 67.7 %all-to-all-start = ((bf16[16,128,128]{2,1,0:T(8,128)(2,1)}), bf16[16,128,128]{2,1,0:T(8,128)(2,1)S(1)}, u32[]{:S(2)}, u32[]{:S(2)}) async-start(bf16[16,128,128]{2,1,0:T(8,128)(2,1)} %attend.4.refs_4_), calls=%async_computation | async-start | bytes 1048576 | tf_op jit(solution)/shard_map/all_to_all | solution.py:272
  100.4 25.4 %collective-permute-start.17 = (bf16[4,384,128]{2,1,0:T(8,128)(2,1)}, bf16[4,384,128]{2,1,0:T(8,128)(2,1)S(1)}, u32[]{:S(2)}, u32[]{:S(2)}) collective-permute-start(bf16[4,384,128]{2,1,0:T(8,128)(2,1)} %get-tuple-element.66), channel_id=1, source_target_pairs={{0,4},{1,5},{2,6},{3,7},{4,0},{5,1},{6,2},{7,3},{8,12},{9,13},{10,... | collective-permute-start | bytes 1179656 | tf_op jit(solution)/shard_map/ppermute | solution.py:241
  102.3 36.5 %collective-permute-start.18 = (bf16[4,384,128]{2,1,0:T(8,128)(2,1)}, bf16[4,384,128]{2,1,0:T(8,128)(2,1)S(1)}, u32[]{:S(2)}, u32[]{:S(2)}) collective-permute-start(bf16[4,384,128]{2,1,0:T(8,128)(2,1)} %get-tuple-element.67), channel_id=1, source_target_pairs={{0,8},{1,9},{2,10},{3,11},{4,12},{5,13},{6,14},{7,15},{8,0},{9,1},... | collective-permute-start | bytes 1179656 | tf_op jit(solution)/shard_map/ppermute | solution.py:241
  104.7 3.1 copy-start.2
  107.6 31.2 %collective-permute-start.19 = (bf16[4,384,128]{2,1,0:T(8,128)(2,1)}, bf16[4,384,128]{2,1,0:T(8,128)(2,1)S(1)}, u32[]{:S(2)}, u32[]{:S(2)}) collective-permute-start(bf16[4,384,128]{2,1,0:T(8,128)(2,1)} %get-tuple-element.68), channel_id=1, source_target_pairs={{0,12},{1,13},{2,14},{3,15},{4,8},{5,9},{6,10},{7,11},{8,4},{9,5},... | collective-permute-start | bytes 1179656 | tf_op jit(solution)/shard_map/ppermute | solution.py:241
  107.8 1.0 copy-start
  108.8 30.1 %copy-start.3 = (bf16[4,384,128]{2,1,0:T(8,128)(2,1)S(1)}, bf16[4,384,128]{2,1,0:T(8,128)(2,1)}, u32[]{:S(2)}) copy-start(bf16[4,384,128]{2,1,0:T(8,128)(2,1)} %get-tuple-element.62.refs_3_.refs_0_) | copy-start | bytes 1179652
  125.7 41.3 %copy-start.23 = (bf16[4,384,128]{2,1,0:T(8,128)(2,1)S(1)}, bf16[4,384,128]{2,1,0:T(8,128)(2,1)}, u32[]{:S(2)}) copy-start(bf16[4,384,128]{2,1,0:T(8,128)(2,1)} %get-tuple-element.72) | copy-start | bytes 1179652
  125.7 43.0 %copy-start.22 = (bf16[4,384,128]{2,1,0:T(8,128)(2,1)S(1)}, bf16[4,384,128]{2,1,0:T(8,128)(2,1)}, u32[]{:S(2)}) copy-start(bf16[4,384,128]{2,1,0:T(8,128)(2,1)} %get-tuple-element.73) | copy-start | bytes 1179652
  155.8 105.8 %copy-start.6 = (bf16[16,128,128]{2,1,0:T(8,128)(2,1)}, bf16[16,128,128]{2,1,0:T(8,128)(2,1)S(1)}, u32[]{:S(2)}) copy-start(bf16[16,128,128]{2,1,0:T(8,128)(2,1)S(1)} %all-to-all-done.refs_3_) | copy-start | bytes 1572868
  155.8 43.7 %all-to-all-start.2 = ((bf16[16,128,128]{2,1,0:T(8,128)(2,1)}), bf16[16,128,128]{2,1,0:T(8,128)(2,1)S(1)}, u32[]{:S(2)}, u32[]{:S(2)}) async-start(bf16[16,128,128]{2,1,0:T(8,128)(2,1)} %attend.6.refs_4_), calls=%async_computation.2 | async-start | bytes 1048576 | tf_op jit(solution)/shard_map/all_to_all | solution.py:272
  166.6 2.1 collective-permute-start.21
  167.0 17.2 %collective-permute-start.22 = (bf16[4,384,128]{2,1,0:T(8,128)(2,1)S(1)}, bf16[4,384,128]{2,1,0:T(8,128)(2,1)S(1)}, u32[]{:S(2)}, u32[]{:S(2)}) collective-permute-start(bf16[4,384,128]{2,1,0:T(8,128)(2,1)S(1)} %copy-done.23), channel_id=1, source_target_pairs={{0,2},{1,3},{2,0},{3,1},{4,6},{5,7},{6,4},{7,5},{8,10},{9,11},{10,... | collective-permute-start | bytes 1179656 | tf_op jit(solution)/shard_map/ppermute | solution.py:241
  168.7 23.0 %collective-permute-start.23 = (bf16[4,384,128]{2,1,0:T(8,128)(2,1)S(1)}, bf16[4,384,128]{2,1,0:T(8,128)(2,1)S(1)}, u32[]{:S(2)}, u32[]{:S(2)}) collective-permute-start(bf16[4,384,128]{2,1,0:T(8,128)(2,1)S(1)} %copy-done.22), channel_id=1, source_target_pairs={{0,3},{1,2},{2,1},{3,0},{4,7},{5,6},{6,5},{7,4},{8,11},{9,10},{10,... | collective-permute-start | bytes 1179656 | tf_op jit(solution)/shard_map/ppermute | solution.py:241
  168.7 23.0 %copy-start.19 = (bf16[4,384,128]{2,1,0:T(8,128)(2,1)}, bf16[4,384,128]{2,1,0:T(8,128)(2,1)S(1)}, u32[]{:S(2)}) copy-start(bf16[4,384,128]{2,1,0:T(8,128)(2,1)S(1)} %collective-permute-done.21.refs_1_) | copy-start | bytes 1179652
  184.2 7.5 %copy-start.20 = (bf16[4,384,128]{2,1,0:T(8,128)(2,1)}, bf16[4,384,128]{2,1,0:T(8,128)(2,1)S(1)}, u32[]{:S(2)}) copy-start(bf16[4,384,128]{2,1,0:T(8,128)(2,1)S(1)} %collective-permute-done.22.refs_2_) | copy-start | bytes 1179652
  191.7 0.8 copy-start.21
  195.1 20.0 %collective-permute-start.24 = (bf16[4,384,128]{2,1,0:T(8,128)(2,1)}, bf16[4,384,128]{2,1,0:T(8,128)(2,1)S(1)}, u32[]{:S(2)}, u32[]{:S(2)}) collective-permute-start(bf16[4,384,128]{2,1,0:T(8,128)(2,1)} %get-tuple-element.75), channel_id=1, source_target_pairs={{0,4},{1,5},{2,6},{3,7},{4,0},{5,1},{6,2},{7,3},{8,12},{9,13},{10,... | collective-permute-start | bytes 1179656 | tf_op jit(solution)/shard_map/ppermute | solution.py:241
  196.6 33.4 %collective-permute-start.25 = (bf16[4,384,128]{2,1,0:T(8,128)(2,1)}, bf16[4,384,128]{2,1,0:T(8,128)(2,1)S(1)}, u32[]{:S(2)}, u32[]{:S(2)}) collective-permute-start(bf16[4,384,128]{2,1,0:T(8,128)(2,1)} %get-tuple-element.76), channel_id=1, source_target_pairs={{0,8},{1,9},{2,10},{3,11},{4,12},{5,13},{6,14},{7,15},{8,0},{9,1},... | collective-permute-start | bytes 1179656 | tf_op jit(solution)/shard_map/ppermute | solution.py:241
  199.1 30.9 %collective-permute-start.26 = (bf16[4,384,128]{2,1,0:T(8,128)(2,1)}, bf16[4,384,128]{2,1,0:T(8,128)(2,1)S(1)}, u32[]{:S(2)}, u32[]{:S(2)}) collective-permute-start(bf16[4,384,128]{2,1,0:T(8,128)(2,1)} %get-tuple-element.77), channel_id=1, source_target_pairs={{0,12},{1,13},{2,14},{3,15},{4,8},{5,9},{6,10},{7,11},{8,4},{9,5},... | collective-permute-start | bytes 1179656 | tf_op jit(solution)/shard_map/ppermute | solution.py:241
  199.5 64.1 %copy-start.7 = (bf16[16,128,128]{2,1,0:T(8,128)(2,1)}, bf16[16,128,128]{2,1,0:T(8,128)(2,1)S(1)}, u32[]{:S(2)}) copy-start(bf16[16,128,128]{2,1,0:T(8,128)(2,1)S(1)} %all-to-all-done.2.refs_5_) | copy-start | bytes 1572868
  199.5 48.4 %all-to-all-start.1 = ((bf16[16,128,128]{2,1,0:T(8,128)(2,1)}), bf16[16,128,128]{2,1,0:T(8,128)(2,1)S(1)}, u32[]{:S(2)}, u32[]{:S(2)}) async-start(bf16[16,128,128]{2,1,0:T(8,128)(2,1)} %attend.5.refs_4_), calls=%async_computation.1 | async-start | bytes 1048576 | tf_op jit(solution)/shard_map/all_to_all | solution.py:272
  230.0 1.0 copy-start.5
  247.9 34.1 %copy-start.8 = (bf16[16,128,128]{2,1,0:T(8,128)(2,1)}, bf16[16,128,128]{2,1,0:T(8,128)(2,1)S(1)}, u32[]{:S(2)}) copy-start(bf16[16,128,128]{2,1,0:T(8,128)(2,1)S(1)} %all-to-all-done.1.refs_5_) | copy-start | bytes 1572868
  247.9 28.1 %all-to-all-start.3 = ((bf16[16,128,128]{2,1,0:T(8,128)(2,1)}), bf16[16,128,128]{2,1,0:T(8,128)(2,1)S(1)}, u32[]{:S(2)}, u32[]{:S(2)}) async-start(bf16[16,128,128]{2,1,0:T(8,128)(2,1)} %attend.7), calls=%async_computation.3 | async-start | bytes 1048576 | tf_op jit(solution)/shard_map/all_to_all | solution.py:272
  261.6 16.0 %collective-permute-start.9 = (bf16[16,128,128]{2,1,0:T(8,128)(2,1)S(1)}, bf16[16,128,128]{2,1,0:T(8,128)(2,1)}, u32[]{:S(2)}, u32[]{:S(2)}) collective-permute-start(bf16[16,128,128]{2,1,0:T(8,128)(2,1)S(1)} %all-to-all-done.refs_3_), channel_id=1, source_target_pairs={{0,16},{16,0},{1,17},{17,1},{2,18},{18,2},{3,19},{19,3},{4,20},{20... | collective-permute-start | bytes 1572872 | tf_op jit(solution)/shard_map/ppermute | solution.py:241
  263.2 24.5 %collective-permute-start.16 = (bf16[16,128,128]{2,1,0:T(8,128)(2,1)S(1)}, bf16[16,128,128]{2,1,0:T(8,128)(2,1)}, u32[]{:S(2)}, u32[]{:S(2)}) collective-permute-start(bf16[16,128,128]{2,1,0:T(8,128)(2,1)S(1)} %all-to-all-done.1.refs_5_), channel_id=1, source_target_pairs={{0,16},{16,0},{1,17},{17,1},{2,18},{18,2},{3,19},{19,3},{4,20},{20... | collective-permute-start | bytes 1572872 | tf_op jit(solution)/shard_map/ppermute | solution.py:241
  263.7 35.2 %collective-permute-start.20 = (bf16[16,128,128]{2,1,0:T(8,128)(2,1)S(1)}, bf16[16,128,128]{2,1,0:T(8,128)(2,1)S(1)}, u32[]{:S(2)}, u32[]{:S(2)}) collective-permute-start(bf16[16,128,128]{2,1,0:T(8,128)(2,1)S(1)} %all-to-all-done.2.refs_5_), channel_id=1, source_target_pairs={{0,16},{16,0},{1,17},{17,1},{2,18},{18,2},{3,19},{19,3},{4,20},{20... | collective-permute-start | bytes 1572872 | tf_op jit(solution)/shard_map/ppermute | solution.py:241
  276.0 6.0 %copy-start.9 = (bf16[16,128,128]{2,1,0:T(8,128)(2,1)}, bf16[16,128,128]{2,1,0:T(8,128)(2,1)S(1)}, u32[]{:S(2)}) copy-start(bf16[16,128,128]{2,1,0:T(8,128)(2,1)S(1)} %all-to-all-done.3.refs_5_) | copy-start | bytes 1572868
  276.0 33.6 %collective-permute-start.27 = (bf16[16,128,128]{2,1,0:T(8,128)(2,1)S(1)}, bf16[16,128,128]{2,1,0:T(8,128)(2,1)S(1)}, u32[]{:S(2)}, u32[]{:S(2)}) collective-permute-start(bf16[16,128,128]{2,1,0:T(8,128)(2,1)S(1)} %all-to-all-done.3.refs_5_), channel_id=1, source_target_pairs={{0,16},{16,0},{1,17},{17,1},{2,18},{18,2},{3,19},{19,3},{4,20},{20... | collective-permute-start | bytes 1572872 | tf_op jit(solution)/shard_map/ppermute | solution.py:241
  298.8 0.8 copy-start.11
  309.6 0.8 copy-start.10
Sparse Core Ops, SparseCore 0:
  9.5 59.4 all-gather.2

commit v3 on v2

--- a/solution.py
+++ b/solution.py
@@ -17,41 +17,37 @@
     return 1 << ((parts.bit_length() - 1) // 2)
 
 
-def distances(me, near, far_first, outer, inner):
-    shift_high, shift_low = (outer, inner) if far_first else (inner, outer)
-    return (me // near ^ shift_high) * near + (me % near ^ shift_low)
-
-
-def pack_kernel(near, far_first, per_chunk, rows, ahead, me_ref, *refs):
+def pack_kernel(near, per_chunk, rows, ahead, me_ref, *refs):
     sources, out_refs = refs[:3], refs[3 + ahead :]
     lane_blocks = sources[0].shape[3] // LANES
-    for outer, out_ref in enumerate(out_refs):
-        for inner in range(out_ref.shape[0]):
-            block = distances(me_ref[0], near, far_first, outer, inner)
+    high = me_ref[0] // near
+    for shift, out_ref in enumerate(out_refs):
+        for low in range(near):
+            block = (high ^ shift) * near + low
             video = 0 if per_chunk == 1 else block // lane_blocks
             column = block if per_chunk == 1 else block % lane_blocks
             lanes = pl.ds(pl.multiple_of(column * LANES, LANES), LANES)
             for which, source in enumerate(sources):
                 here = slice(which * rows, (which + 1) * rows)
-                out_ref[inner, here, :] = source[video, 0, :, lanes]
-
-
-def pack(me, sources, first_batch, per_chunk, parts, far_first, after=()):
+                out_ref[low, here, :] = source[video, 0, :, lanes]
+
+
+def pack(me, sources, first_batch, per_chunk, parts, after=()):
     batch_size, single, rows, width = sources[0].shape
     near = split_size(parts)
-    count = parts // near if far_first else near
+    far = parts // near
     spec = pl.BlockSpec(
         (per_chunk, 1, rows, width), lambda i: (first_batch // per_chunk, 0, 0, 0)
     )
-    shape = (parts // count, 3 * rows, LANES)
+    shape = (near, 3 * rows, LANES)
     return pl.pallas_call(
-        functools.partial(pack_kernel, near, far_first, per_chunk, rows, len(after)),
+        functools.partial(pack_kernel, near, per_chunk, rows, len(after)),
         grid=(1,),
         in_specs=[pl.BlockSpec(memory_space=pltpu.SMEM)]
         + [spec] * 3
         + [pl.BlockSpec(memory_space=pl.ANY)] * len(after),
-        out_specs=[pl.BlockSpec(shape, lambda i: (0, 0, 0))] * count,
-        out_shape=[jax.ShapeDtypeStruct(shape, sources[0].dtype)] * count,
+        out_specs=[pl.BlockSpec(shape, lambda i: (0, 0, 0))] * far,
+        out_shape=[jax.ShapeDtypeStruct(shape, sources[0].dtype)] * far,
         cost_estimate=pl.CostEstimate(
             flops=0, bytes_accessed=parts * 3 * rows * LANES * 4, transcendentals=0
         ),
@@ -59,28 +55,35 @@
     )(me, *sources, *after)
 
 
-def repack_kernel(count, *refs):
-    in_refs, out_refs = refs[:count], refs[count:]
-    for outer, out_ref in enumerate(out_refs):
-        for inner, in_ref in enumerate(in_refs):
-            out_ref[inner] = in_ref[outer]
-
-
-def repack(blocks):
-    count = len(blocks)
-    far, rows, lanes = blocks[0].shape
-    shape = (count, rows, lanes)
+def repack_kernel(near, far, ahead, me_ref, *refs):
+    in_refs, out_refs = refs[:far], refs[far + ahead :]
+    low = me_ref[0] % near
+    for shift, in_ref in enumerate(in_refs):
+        for other in range(near):
+            if len(out_refs) == 1:
+                out_refs[0][other, shift] = in_ref[other]
+            else:
+                out_refs[other][shift] = in_ref[low ^ other]
+
+
+def repack(me, blocks, single, after=()):
+    far = len(blocks)
+    near, rows, lanes = blocks[0].shape
+    shape, count = ((near, far, rows, lanes), 1) if single else ((far, rows, lanes), near)
     return pl.pallas_call(
-        functools.partial(repack_kernel, count),
-        out_shape=[jax.ShapeDtypeStruct(shape, blocks[0].dtype)] * far,
+        functools.partial(repack_kernel, near, far, len(after)),
+        in_specs=[pl.BlockSpec(memory_space=pltpu.SMEM)]
+        + [pl.BlockSpec(memory_space=pltpu.VMEM)] * far
+        + [pl.BlockSpec(memory_space=pl.ANY)] * len(after),
+        out_shape=[jax.ShapeDtypeStruct(shape, blocks[0].dtype)] * count,
         cost_estimate=pl.CostEstimate(
-            flops=0, bytes_accessed=count * far * rows * lanes * 4, transcendentals=0
+            flops=0, bytes_accessed=near * far * rows * lanes * 4, transcendentals=0
         ),
         name="repack",
-    )(*blocks)
-
-
-def attend_kernel(group, rows, parts, near, far_first, count, me_ref, *refs):
+    )(me, *blocks, *after)
+
+
+def attend_kernel(group, rows, parts, near, count, me_ref, *refs):
     in_refs = refs[:count]
     out_ref, query_scr, key_scr, value_scr = refs[-4:]
     step = pl.program_id(0)
@@ -98,9 +101,13 @@
     @pl.when(step == 0)
     def _():
         value_scr[:, LANES : 2 * LANES] = jnp.ones((length, LANES), value_scr.dtype)
-        for outer, in_ref in enumerate(in_refs):
-            for inner in range(in_ref.shape[0]):
-                load(in_ref, inner, distances(me_ref[0], near, far_first, outer, inner))
+        high, low = me_ref[0] // near, me_ref[0] % near
+        for shift in range(parts // near):
+            for other in range(near):
+                if count == 1:
+                    load(in_refs[0].at[other], shift, (high ^ shift) * near + other)
+                else:
+                    load(in_refs[other], shift, (high ^ shift) * near + (low ^ other))
 
     block = group * rows
     here = pl.ds(pl.multiple_of(step * block, block), block)
@@ -126,20 +133,18 @@
     out_ref[...] = merged.reshape(group, rows, LANES)
 
 
-def attend(me, arrived, parts, far_first, after=()):
-    triple = arrived[0].shape[1]
+def attend(me, arrived, parts, after=()):
+    triple = arrived[0].shape[-2]
     rows = triple // 3
     length = parts * rows
     dtype = arrived[0].dtype
-    group = max(1, 256 // rows)
+    group = max(1, 512 // rows)
     count = len(arrived)
     return pl.pallas_call(
-        functools.partial(
-            attend_kernel, group, rows, parts, split_size(parts), far_first, count
-        ),
+        functools.partial(attend_kernel, group, rows, parts, split_size(parts), count),
         grid=(parts // group,),
         in_specs=[pl.BlockSpec(memory_space=pltpu.SMEM)]
-        + [pl.BlockSpec(value.shape, lambda i: (0, 0, 0)) for value in arrived]
+        + [pl.BlockSpec(value.shape, lambda i, n=value.ndim: (0,) * n) for value in arrived]
         + [pl.BlockSpec(memory_space=pl.ANY)] * len(after),
         out_specs=pl.BlockSpec((group, rows, LANES), lambda i: (i, 0, 0)),
         out_shape=jax.ShapeDtypeStruct((parts, rows, LANES), dtype),
@@ -187,15 +192,15 @@
         joined = None
         for value_ref, part in zip(value_refs, expo):
             weight = (part * inverse).astype(jnp.bfloat16).astype(jnp.float32)
-            term = weight * value_ref[j].astype(jnp.float32)
+            term = weight * value_ref[0, j].astype(jnp.float32)
             joined = term if joined is None else joined + term
         joined_ref[0, 0, :, lanes] = joined.astype(joined_ref.dtype)
-        spatial_ref[0, 0, :, lanes] = value_refs[0][j]
+        spatial_ref[0, 0, :, lanes] = value_refs[0][0, j]
 
 
 def combine(view, carry, view_queries, keys, outputs, first_batch):
     batch_size, single, rows, width = view_queries.shape
-    parts = outputs[0].shape[0]
+    parts = outputs[0].shape[-3]
     views = len(outputs)
     group = 4
     steps = width // LANES // group
@@ -211,7 +216,14 @@
         pl.BlockSpec((1, 1, 1, rows, group * LANES), functools.partial(key_place, shift))
         for shift in range(views)
     ]
-    narrow = pl.BlockSpec((group, rows, LANES), lambda i, view_ref: (i, 0, 0))
+
+    def output_place(shift, i, view_ref):
+        return (view_ref[0] ^ shift if outputs[shift].shape[0] > 1 else 0, i, 0, 0)
+
+    output_specs = [
+        pl.BlockSpec((1, group, rows, LANES), functools.partial(output_place, shift))
+        for shift in range(views)
+    ]
     shape = jax.ShapeDtypeStruct(view_queries.shape, view_queries.dtype)
     carried = len(carry)
     return pl.pallas_call(
@@ -222,7 +234,7 @@
             in_specs=[pl.BlockSpec(memory_space=pl.ANY)] * carried
             + [wide]
             + key_specs
-            + [narrow] * views,
+            + output_specs,
             out_specs=[wide, wide],
         ),
         out_shape=[shape, shape],
@@ -237,10 +249,12 @@
 
 
 def swap(blocks, axis, size, stride):
-    return [blocks[0]] + [
-        lax.ppermute(blocks[shift], axis, [(i, i ^ (shift * stride)) for i in range(size)])
-        for shift in range(1, len(blocks))
-    ]
+    arrived = list(blocks)
+    for shift in reversed(range(1, len(blocks))):
+        arrived[shift] = lax.ppermute(
+            blocks[shift], axis, [(i, i ^ (shift * stride)) for i in range(size)]
+        )
+    return arrived
 
 
 def local(seq_size, views, queries, key_rows, value_rows, view_queries):
@@ -253,24 +267,41 @@
     exchange = functools.partial(
         lax.all_to_all, axis_name="seq", split_axis=0, concat_axis=0, tiled=True
     )
+    neighbours = [list(range(i, i + near)) for i in range(0, seq_size, near)]
     keys = lax.all_gather(key_rows, "view")
     sources = (queries, key_rows, value_rows)
-    received, first_packed, after = [], [], ()
+    packed, crossed, received = [], [], []
     for c in range(chunks):
-        strides = (near, 1) if c == 0 else (1, near)
-        packed = pack(me, sources, c * per_chunk, per_chunk, seq_size, c == 0, after)
-        first_packed.append(packed[0])
-        blocks = repack(swap(packed, "seq", seq_size, strides[0]))
-        after = (packed[0],) if c == 0 else (blocks[0],)
-        received.append(swap(blocks, "seq", seq_size, strides[1]))
+        after = tuple(blocks[0] for blocks in packed[-1:])
+        packed.append(pack(me, sources, c * per_chunk, per_chunk, seq_size, after))
+        crossed.append(swap(packed[c], "seq", seq_size, near))
+    repacked, received = [], []
+
+    def arrive(c, after):
+        repacked.append(repack(me, crossed[c], 2 * c < chunks, after))
+        if 2 * c < chunks:
+            received.append([exchange(repacked[c][0], axis_index_groups=neighbours)])
+        else:
+            received.append(swap(repacked[c], "seq", seq_size, 1))
+
+    arrive(0, ())
     carry, attended = (), ()
     for c in range(chunks):
-        after = attended + tuple(first_packed[c + 2 : c + 3])
+        after = attended + tuple(blocks[1] for blocks in crossed[c + 1 : c + 2])
+        if c + 1 < chunks - 1:
+            arrive(c + 1, attended or (repacked[0][0],))
+            after += (repacked[c + 1][0],)
         if c == 1:
             after += (keys,)
-        attended = (attend(me, received[c], seq_size, c > 0, after),)
+        attended = (attend(me, received[c], seq_size, after),)
+        if c + 1 == chunks - 1:
+            arrive(c + 1, attended)
         returned = exchange(attended[0])
-        outputs = swap([returned] * views, "view", views, 1)
+        own = returned[None]
+        if c + 2 < chunks:
+            outputs = [own] + [lax.all_gather(returned, "view")] * (views - 1)
+        else:
+            outputs = swap([own] * views, "view", views, 1)
         carry = combine(view, carry, view_queries, keys, outputs, c * per_chunk)
     return tuple(carry)
 

time: 323 us -> 307 us (0.950)
  waiting for transfers between devices: 116 us -> 99.1 us
  Pallas kernels: 108 us -> 101 us
  starting transfers between devices: 76 us -> 79.3 us
  local copies, waits for them, and re-layouts: 8.25 us -> 11.5 us
    ppermute x28 -> x20, waiting for transfers between devices: 104 us -> 69.8 us  [swap(): lax.ppermute(blocks[shift], axis, [(i, i ^ shift * stride) for i in range...]
    all_gather x0 -> x2, waiting for transfers between devices: none -> 15.1 us  [local(): outputs = [own] + [lax.all_gather(returned, 'view')] * (views - 1)]
    all_to_all x0 -> x2, starting transfers between devices: none -> 7.13 us  [arrive(): received.append([exchange(repacked[c][0], axis_index_groups=neighbours)])]
    all_to_all x4, starting transfers between devices: 38.9 us -> 32 us  [local(): returned = exchange(attended[0])]
    pallas_call x4, Pallas kernels: 67.9 us -> 61.4 us  [attend(): pl.pallas_call(functools.partial(attend_kernel, group, rows, parts, split...]
    unnamed x48 -> x44, local copies, waits for them, and re-layouts: 8.25 us -> 11.5 us
    ppermute x28 -> x20, starting transfers between devices: 37.1 us -> 40.1 us  [swap(): lax.ppermute(blocks[shift], axis, [(i, i ^ shift * stride) for i in range...]
  transfers between devices with their start and end apart: 33 -> 29, of which waited for: 12 -> 8; matrix products, arithmetic and copies ran while one was open for 0% -> 0% of each run, Pallas kernels for 32% -> 32%
where the time goes in v3:
time: 307 us; the launch traced here: 305 us
  Pallas kernels  101 us (33%)
  waiting for transfers between devices  99.1 us (32%)
  starting transfers between devices  79.3 us (26%)
  between operations  13.9 us (5%)
  local copies, waits for them, and re-layouts  11.5 us (4%)
    ppermute x20, waiting for transfers between devices, swap(): lax.ppermute(blocks[shift], axis, [(i, i ^ shift * stride) for i in range...  69.8 us
    pallas_call x4, Pallas kernels, attend(): pl.pallas_call(functools.partial(attend_kernel, group, rows, parts, split...  61.4 us
    ppermute x20, starting transfers between devices, swap(): lax.ppermute(blocks[shift], axis, [(i, i ^ shift * stride) for i in range...  40.1 us
    all_to_all x4, starting transfers between devices, local(): returned = exchange(attended[0])  32 us
    pallas_call x4, Pallas kernels, combine(): pl.pallas_call(functools.partial(combine_kernel, views, group, carried),...  17.6 us
    all_gather x2, waiting for transfers between devices, local(): outputs = [own] + [lax.all_gather(returned, 'view')] * (views - 1)  15.1 us
    all_to_all x4, waiting for transfers between devices, local(): returned = exchange(attended[0])  12.2 us
    pallas_call x4, Pallas kernels, pack(): pl.pallas_call(functools.partial(pack_kernel, near, per_chunk, rows, len(...  11.9 us
  transfers between devices with their start and end apart: 29, of which 8 were waited for; matrix products, arithmetic and copies ran while one was open for 0% of the time, Pallas kernels for 32%

profile of v3, /device:TPU:0, one launch (start us, length us, event | category | flops | bytes accessed | tf_op | source)
XLA Modules:
  0.0 305.2 jit_solution(6597494396809132692)
XLA Ops:
  7.2 0.7 all-gather.7.cloned.1.call-update
  7.9 2.9 pack.4
  10.8 3.0 collective-permute-start
  13.8 2.6 collective-permute-start.1
  16.4 14.4 %collective-permute-done.refs_1_ = bf16[4,384,128]{2,1,0:T(8,128)(2,1)S(1)} collective-permute-done((bf16[4,384,128]{2,1,0:T(8,128)(2,1)}, bf16[4,384,128]{2,1,0:T(8,128)(2,1)S(1)}, u32[]{:S(2)}, u32[]{:S(2)}) %collective-permute-start) | collective-permute-done | bytes 393248 | tf_op jit(solution)/shard_map/ppermute | solution.py:254
  30.8 13.0 %collective-permute-done.1.refs_2_ = bf16[4,384,128]{2,1,0:T(8,128)(2,1)S(1)} collective-permute-done((bf16[4,384,128]{2,1,0:T(8,128)(2,1)}, bf16[4,384,128]{2,1,0:T(8,128)(2,1)S(1)}, u32[]{:S(2)}, u32[]{:S(2)}) %collective-permute-start.1) | collective-permute-done | bytes 393248 | tf_op jit(solution)/shard_map/ppermute | solution.py:254
  43.8 0.7 copy-done.20
  44.6 0.1 copy-done.21
  44.7 2.6 repack.4.refs_4_
  47.3 3.6 %all-to-all-start = ((bf16[4,4,384,128]{3,2,1,0:T(8,128)(2,1)}), bf16[4,4,384,128]{3,2,1,0:T(8,128)(2,1)S(1)}, u32[]{:S(2)}, u32[]{:S(2)}) async-start(bf16[4,4,384,128]{3,2,1,0:T(8,128)(2,1)} %repack.4.refs_4_), calls=%async_computation | async-start | bytes 3145728 | tf_op jit(solution)/shard_map/all_to_all | solution.py:283
  50.9 3.0 pack.5
  53.9 7.4 %collective-permute-start.3 = (bf16[4,384,128]{2,1,0:T(8,128)(2,1)}, bf16[4,384,128]{2,1,0:T(8,128)(2,1)S(1)}, u32[]{:S(2)}, u32[]{:S(2)}) collective-permute-start(bf16[4,384,128]{2,1,0:T(8,128)(2,1)} %get-tuple-element.36), channel_id=1, source_target_pairs={{0,4},{1,5},{2,6},{3,7},{4,0},{5,1},{6,2},{7,3},{8,12},{9,13},{10,... | collective-permute-start | bytes 1179656 | tf_op jit(solution)/shard_map/ppermute | solution.py:254
  61.3 1.0 collective-permute-start.4
  62.3 1.5 collective-permute-start.5
  63.8 15.5 %collective-permute-done.3.refs_1_ = bf16[4,384,128]{2,1,0:T(8,128)(2,1)S(1)} collective-permute-done((bf16[4,384,128]{2,1,0:T(8,128)(2,1)}, bf16[4,384,128]{2,1,0:T(8,128)(2,1)S(1)}, u32[]{:S(2)}, u32[]{:S(2)}) %collective-permute-start.3) | collective-permute-done | bytes 393248 | tf_op jit(solution)/shard_map/ppermute | solution.py:254
  79.2 12.0 %collective-permute-done.4.refs_2_ = bf16[4,384,128]{2,1,0:T(8,128)(2,1)S(1)} collective-permute-done((bf16[4,384,128]{2,1,0:T(8,128)(2,1)}, bf16[4,384,128]{2,1,0:T(8,128)(2,1)S(1)}, u32[]{:S(2)}, u32[]{:S(2)}) %collective-permute-start.4) | collective-permute-done | bytes 393248 | tf_op jit(solution)/shard_map/ppermute | solution.py:254
  91.3 0.7 copy-done.17
  92.0 0.1 copy-done.18
  92.2 2.6 repack.5.refs_2_
  94.8 1.1 copy-done.1
  95.9 3.6 %all-to-all-start.2 = ((bf16[4,4,384,128]{3,2,1,0:T(8,128)(2,1)}), bf16[4,4,384,128]{3,2,1,0:T(8,128)(2,1)S(1)}, u32[]{:S(2)}, u32[]{:S(2)}) async-start(bf16[4,4,384,128]{3,2,1,0:T(8,128)(2,1)} %repack.5.refs_2_), calls=%async_computation.2 | async-start | bytes 3145728 | tf_op jit(solution)/shard_map/all_to_all | solution.py:283
  99.5 3.1 %pack.6 = (bf16[4,384,128]{2,1,0:T(8,128)(2,1)}, bf16[4,384,128]{2,1,0:T(8,128)(2,1)}, bf16[4,384,128]{2,1,0:T(8,128)(2,1)}, bf16[4,384,128]{2,1,0:T(8,128)(2,1)}) custom-call(s32[1]{0:T(128)} %bitcast.2.me_ref, bf16[4,1,128,2048]{3,2,1,0:T(8,128)(2,1)} %refs_0_.9, bf16[4,1,128,2048]{3,2,1,0:T(8,128)(2,1)} %refs_1_.7, bf16[4,1,128,2048]{3,2,1,0:T(8,128)(2,1)} %refs_2_.11, ...), custom_call_target="tpu_custom_call" | custom-call | bytes 3145728 | tf_op jit(solution)/shard_map/pack/pallas_call | solution.py:43
  102.6 8.1 %collective-permute-start.6 = (bf16[4,384,128]{2,1,0:T(8,128)(2,1)}, bf16[4,384,128]{2,1,0:T(8,128)(2,1)S(1)}, u32[]{:S(2)}, u32[]{:S(2)}) collective-permute-start(bf16[4,384,128]{2,1,0:T(8,128)(2,1)} %get-tuple-element.42), channel_id=1, source_target_pairs={{0,4},{1,5},{2,6},{3,7},{4,0},{5,1},{6,2},{7,3},{8,12},{9,13},{10,... | collective-permute-start | bytes 1179656 | tf_op jit(solution)/shard_map/ppermute | solution.py:254
  110.7 1.0 collective-permute-start.7
  111.7 1.5 collective-permute-start.8
  113.2 1.4 copy-done.2
  114.6 1.0 copy-done.7
  115.6 15.3 %attend.4.refs_4_.refs_1_ = bf16[16,128,128]{2,1,0:T(8,128)(2,1)} custom-call(s32[1]{0:T(128)} %bitcast.2.me_ref, bf16[4,4,384,128]{3,2,1,0:T(8,128)(2,1)S(1)} %copy-done.2, bf16[4,384,128]{2,1,0:T(8,128)(2,1)S(1)} %copy-done.7, bf16[4,4,384,128]{3,2,1,0:T(8,128)(2,1)S(1)} %copy-done), custom_call_target="tpu_custom_call" | custom-call | flops 8589934592 | bytes 2097152 | tf_op jit(solution)/shard_map/attend/pallas_call | solution.py:143
  130.9 5.2 %all-to-all-start.1 = ((bf16[16,128,128]{2,1,0:T(8,128)(2,1)}), bf16[16,128,128]{2,1,0:T(8,128)(2,1)}, u32[]{:S(2)}, u32[]{:S(2)}) async-start(bf16[16,128,128]{2,1,0:T(8,128)(2,1)} %attend.4.refs_4_.refs_1_), calls=%async_computation.1 | async-start | bytes 1048576 | tf_op jit(solution)/shard_map/all_to_all | solution.py:299
  136.1 3.0 pack.7
  139.1 1.9 collective-permute-start.12
  140.9 2.4 collective-permute-start.14
  143.3 0.7 copy-done.4
  144.0 2.6 repack.6
  146.7 1.5 collective-permute-start.10
  148.1 0.4 collective-permute-start.11
  148.5 1.0 copy-done.5
  149.5 1.0 copy-done.8
  150.5 15.3 %attend.5.refs_4_ = bf16[16,128,128]{2,1,0:T(8,128)(2,1)} custom-call(s32[1]{0:T(128)} %bitcast.2.me_ref, bf16[4,4,384,128]{3,2,1,0:T(8,128)(2,1)S(1)} %all-to-all-done.2.refs_0_, bf16[16,128,128]{2,1,0:T(8,128)(2,1)} %attend.4.refs_4_.refs_1_, bf16[4,384,128]{2,1,0:T(8,128)(2,1)S(1)} %copy-done.5, bf16[4,384,128]{2,1,0:T(8,128)(2,1)S(1)} %copy-done.8, ...), custom_call_target="tpu_custom_call" | custom-call | flops 8589934592 | bytes 2097152 | tf_op jit(solution)/shard_map/attend/pallas_call | solution.py:143
  165.9 2.7 collective-permute-start.15
  168.6 13.0 %all-to-all-start.3 = ((bf16[16,128,128]{2,1,0:T(8,128)(2,1)}), bf16[16,128,128]{2,1,0:T(8,128)(2,1)S(1)}, u32[]{:S(2)}, u32[]{:S(2)}) async-start(bf16[16,128,128]{2,1,0:T(8,128)(2,1)} %attend.5.refs_4_), calls=%async_computation.3 | async-start | bytes 1048576 | tf_op jit(solution)/shard_map/all_to_all | solution.py:299
  181.6 15.4 %attend.6.refs_4_ = bf16[16,128,128]{2,1,0:T(8,128)(2,1)} custom-call(s32[1]{0:T(128)} %bitcast.2.me_ref, bf16[4,384,128]{2,1,0:T(8,128)(2,1)S(1)} %copy-done.9, bf16[4,384,128]{2,1,0:T(8,128)(2,1)S(1)} %collective-permute-done.9.refs_1_, bf16[4,384,128]{2,1,0:T(8,128)(2,1)S(1)} %collective-permute-done.10.refs_2_, ...), custom_call_target="tpu_custom_call" | custom-call | flops 8589934592 | bytes 2097152 | tf_op jit(solution)/shard_map/attend/pallas_call | solution.py:143
  197.0 0.8 copy-done.16
  197.8 2.7 repack.7
  200.4 0.4 collective-permute-start.16
  200.8 1.7 collective-permute-start.17
  202.5 6.8 %all-to-all-start.4 = ((bf16[16,128,128]{2,1,0:T(8,128)(2,1)}), bf16[16,128,128]{2,1,0:T(8,128)(2,1)S(1)}, u32[]{:S(2)}, u32[]{:S(2)}) async-start(bf16[16,128,128]{2,1,0:T(8,128)(2,1)} %attend.6.refs_4_), calls=%async_computation.4 | async-start | bytes 1048576 | tf_op jit(solution)/shard_map/all_to_all | solution.py:299
  209.3 0.7 all-gather.9.cloned.1.call-update
  210.1 2.9 collective-permute-done.17.refs_2_
  213.0 12.0 %collective-permute-done.18.refs_3_ = bf16[4,384,128]{2,1,0:T(8,128)(2,1)S(1)} collective-permute-done((bf16[4,384,128]{2,1,0:T(8,128)(2,1)}, bf16[4,384,128]{2,1,0:T(8,128)(2,1)S(1)}, u32[]{:S(2)}, u32[]{:S(2)}) %collective-permute-start.18) | collective-permute-done | bytes 393248 | tf_op jit(solution)/shard_map/ppermute | solution.py:254
  225.0 1.0 copy-done.10
  226.0 15.3 %attend.7 = bf16[16,128,128]{2,1,0:T(8,128)(2,1)} custom-call(s32[1]{0:T(128)} %bitcast.2.me_ref, bf16[4,384,128]{2,1,0:T(8,128)(2,1)S(1)} %copy-done.10, bf16[4,384,128]{2,1,0:T(8,128)(2,1)S(1)} %collective-permute-done.16.refs_1_, bf16[4,384,128]{2,1,0:T(8,128)(2,1)S(1)} %collective-permute-done.17.refs_2_, ...), custom_call_target="tpu_custom_call" | custom-call | flops 8589934592 | bytes 2097152 | tf_op jit(solution)/shard_map/attend/pallas_call | solution.py:143
  241.3 7.1 %all-to-all-start.5 = ((bf16[16,128,128]{2,1,0:T(8,128)(2,1)}), bf16[16,128,128]{2,1,0:T(8,128)(2,1)S(1)}, u32[]{:S(2)}, u32[]{:S(2)}) async-start(bf16[16,128,128]{2,1,0:T(8,128)(2,1)} %attend.7), calls=%async_computation.5 | async-start | bytes 1048576 | tf_op jit(solution)/shard_map/all_to_all | solution.py:299
  248.4 0.7 all-gather.11.cloned.1.call-update
  249.1 1.6 collective-permute-start.13
  250.7 12.1 %all-to-all-done.5 = bf16[16,128,128]{2,1,0:T(8,128)(2,1)S(1)} async-done(((bf16[16,128,128]{2,1,0:T(8,128)(2,1)}), bf16[16,128,128]{2,1,0:T(8,128)(2,1)S(1)}, u32[]{:S(2)}, u32[]{:S(2)}) %all-to-all-start.5) | async-done | bytes 524320 | tf_op jit(solution)/shard_map/all_to_all | solution.py:299
  262.8 1.5 collective-permute-start.19
  264.4 4.4 %combine.4 = (bf16[4,1,128,2048]{3,2,1,0:T(8,128)(2,1)}, bf16[4,1,128,2048]{3,2,1,0:T(8,128)(2,1)}) custom-call(s32[1]{0:T(128)} %bitcast.view_ref, bf16[4,1,128,2048]{3,2,1,0:T(8,128)(2,1)} %refs_2_.13, bf16[2,4,1,128,2048]{4,3,2,1,0:T(8,128)(2,1)} %bitcast.10, bf16[2,4,1,128,2048]{4,3,2,1,0:T(8,128)(2,1)} %bitcast.11, ...), custom_call_target="tpu_custom_call" | custom-call | flops 536870912 | bytes 3670016 | tf_op jit(solution)/shard_map/combine/pallas_call | solution.py:229
  268.8 15.1 %all-gather.11.cloned.1.call-done = bf16[32,128,128]{2,1,0:T(8,128)(2,1)} async-done(((bf16[16,128,128]{2,1,0:T(8,128)(2,1)}), bf16[32,128,128]{2,1,0:T(8,128)(2,1)}) %all-gather.11.cloned.1.call-update) | async-done | bytes 1048592 | tf_op jit(solution)/shard_map/all_gather | solution.py:302
  283.8 4.4 %combine.5 = (bf16[4,1,128,2048]{3,2,1,0:T(8,128)(2,1)}, bf16[4,1,128,2048]{3,2,1,0:T(8,128)(2,1)}) custom-call(s32[1]{0:T(128)} %bitcast.view_ref, bf16[4,1,128,2048]{3,2,1,0:T(8,128)(2,1)} %get-tuple-element.40.refs_0_, bf16[4,1,128,2048]{3,2,1,0:T(8,128)(2,1)} %get-tuple-element.41.refs_1_, ...), custom_call_target="tpu_custom_call", output_to_operand_aliasing={{0}: (1, {}), {1}: (2, {})} | custom-call | flops 536870912 | bytes 3670016 | tf_op jit(solution)/shard_map/combine/pallas_call | solution.py:229
  288.2 0.8 copy-done.15
  289.1 4.4 %combine.6 = (bf16[4,1,128,2048]{3,2,1,0:T(8,128)(2,1)}, bf16[4,1,128,2048]{3,2,1,0:T(8,128)(2,1)}) custom-call(s32[1]{0:T(128)} %bitcast.view_ref, bf16[4,1,128,2048]{3,2,1,0:T(8,128)(2,1)} %get-tuple-element.47.refs_0_, bf16[4,1,128,2048]{3,2,1,0:T(8,128)(2,1)} %get-tuple-element.48.refs_1_, ...), custom_call_target="tpu_custom_call", output_to_operand_aliasing={{0}: (1, {}), {1}: (2, {})} | custom-call | flops 536870912 | bytes 3670016 | tf_op jit(solution)/shard_map/combine/pallas_call | solution.py:229
  293.5 0.8 copy-done.14
  294.3 4.4 %combine.7 = (bf16[4,1,128,2048]{3,2,1,0:T(8,128)(2,1)}, bf16[4,1,128,2048]{3,2,1,0:T(8,128)(2,1)}) custom-call(s32[1]{0:T(128)} %bitcast.view_ref, bf16[4,1,128,2048]{3,2,1,0:T(8,128)(2,1)} %get-tuple-element.53.refs_0_, bf16[4,1,128,2048]{3,2,1,0:T(8,128)(2,1)} %get-tuple-element.54.refs_1_, ...), custom_call_target="tpu_custom_call", output_to_operand_aliasing={{0}: (1, {}), {1}: (2, {})} | custom-call | flops 536870912 | bytes 3670016 | tf_op jit(solution)/shard_map/combine/pallas_call | solution.py:229
  (57 shorter events, 0.2 us)
Async XLA Ops:
  7.2 141.4 %all-gather.7.cloned.1.call-start = ((), (), s32[]{:S(2)}) async-start(), calls=%async_computation.6 | async-start | bytes 6291456 | tf_op jit(solution)/shard_map/all_gather | solution.py:271
  10.8 20.0 %collective-permute-start = (bf16[4,384,128]{2,1,0:T(8,128)(2,1)}, bf16[4,384,128]{2,1,0:T(8,128)(2,1)S(1)}, u32[]{:S(2)}, u32[]{:S(2)}) collective-permute-start(bf16[4,384,128]{2,1,0:T(8,128)(2,1)} %get-tuple-element.33), channel_id=1, source_target_pairs={{0,4},{1,5},{2,6},{3,7},{4,0},{5,1},{6,2},{7,3},{8,12},{9,13},{10,... | collective-permute-start | bytes 1179656 | tf_op jit(solution)/shard_map/ppermute | solution.py:254
  13.8 30.0 %collective-permute-start.1 = (bf16[4,384,128]{2,1,0:T(8,128)(2,1)}, bf16[4,384,128]{2,1,0:T(8,128)(2,1)S(1)}, u32[]{:S(2)}, u32[]{:S(2)}) collective-permute-start(bf16[4,384,128]{2,1,0:T(8,128)(2,1)} %get-tuple-element.34), channel_id=1, source_target_pairs={{0,8},{1,9},{2,10},{3,11},{4,12},{5,13},{6,14},{7,15},{8,0},{9,1},... | collective-permute-start | bytes 1179656 | tf_op jit(solution)/shard_map/ppermute | solution.py:254
  16.4 27.4 %collective-permute-start.2 = (bf16[4,384,128]{2,1,0:T(8,128)(2,1)}, bf16[4,384,128]{2,1,0:T(8,128)(2,1)S(1)}, u32[]{:S(2)}, u32[]{:S(2)}) collective-permute-start(bf16[4,384,128]{2,1,0:T(8,128)(2,1)} %get-tuple-element.35), channel_id=1, source_target_pairs={{0,12},{1,13},{2,14},{3,15},{4,8},{5,9},{6,10},{7,11},{8,4},{9,5},... | collective-permute-start | bytes 1179656 | tf_op jit(solution)/shard_map/ppermute | solution.py:254
  30.8 13.0 %copy-start.19 = (bf16[4,384,128]{2,1,0:T(8,128)(2,1)}, bf16[4,384,128]{2,1,0:T(8,128)(2,1)S(1)}, u32[]{:S(2)}) copy-start(bf16[4,384,128]{2,1,0:T(8,128)(2,1)S(1)} %collective-permute-done.refs_1_) | copy-start | bytes 1179652
  43.8 0.8 copy-start.20
  43.8 0.9 copy-start.21
  47.3 47.4 %all-to-all-start = ((bf16[4,4,384,128]{3,2,1,0:T(8,128)(2,1)}), bf16[4,4,384,128]{3,2,1,0:T(8,128)(2,1)S(1)}, u32[]{:S(2)}, u32[]{:S(2)}) async-start(bf16[4,4,384,128]{3,2,1,0:T(8,128)(2,1)} %repack.4.refs_4_), calls=%async_computation | async-start | bytes 3145728 | tf_op jit(solution)/shard_map/all_to_all | solution.py:283
  53.9 25.4 %collective-permute-start.3 = (bf16[4,384,128]{2,1,0:T(8,128)(2,1)}, bf16[4,384,128]{2,1,0:T(8,128)(2,1)S(1)}, u32[]{:S(2)}, u32[]{:S(2)}) collective-permute-start(bf16[4,384,128]{2,1,0:T(8,128)(2,1)} %get-tuple-element.36), channel_id=1, source_target_pairs={{0,4},{1,5},{2,6},{3,7},{4,0},{5,1},{6,2},{7,3},{8,12},{9,13},{10,... | collective-permute-start | bytes 1179656 | tf_op jit(solution)/shard_map/ppermute | solution.py:254
  61.3 30.0 %collective-permute-start.4 = (bf16[4,384,128]{2,1,0:T(8,128)(2,1)}, bf16[4,384,128]{2,1,0:T(8,128)(2,1)S(1)}, u32[]{:S(2)}, u32[]{:S(2)}) collective-permute-start(bf16[4,384,128]{2,1,0:T(8,128)(2,1)} %get-tuple-element.38), channel_id=1, source_target_pairs={{0,8},{1,9},{2,10},{3,11},{4,12},{5,13},{6,14},{7,15},{8,0},{9,1},... | collective-permute-start | bytes 1179656 | tf_op jit(solution)/shard_map/ppermute | solution.py:254
  62.3 29.0 %collective-permute-start.5 = (bf16[4,384,128]{2,1,0:T(8,128)(2,1)}, bf16[4,384,128]{2,1,0:T(8,128)(2,1)S(1)}, u32[]{:S(2)}, u32[]{:S(2)}) collective-permute-start(bf16[4,384,128]{2,1,0:T(8,128)(2,1)} %get-tuple-element.39), channel_id=1, source_target_pairs={{0,12},{1,13},{2,14},{3,15},{4,8},{5,9},{6,10},{7,11},{8,4},{9,5},... | collective-permute-start | bytes 1179656 | tf_op jit(solution)/shard_map/ppermute | solution.py:254
  79.2 12.0 %copy-start.6 = (bf16[4,384,128]{2,1,0:T(8,128)(2,1)}, bf16[4,384,128]{2,1,0:T(8,128)(2,1)S(1)}, u32[]{:S(2)}) copy-start(bf16[4,384,128]{2,1,0:T(8,128)(2,1)S(1)} %collective-permute-done.3.refs_1_) | copy-start | bytes 1179652
  91.3 0.8 copy-start.17
  91.3 0.9 copy-start.18
  94.7 1.1 copy-start.1
  95.9 35.0 %all-to-all-start.2 = ((bf16[4,4,384,128]{3,2,1,0:T(8,128)(2,1)}), bf16[4,4,384,128]{3,2,1,0:T(8,128)(2,1)S(1)}, u32[]{:S(2)}, u32[]{:S(2)}) async-start(bf16[4,4,384,128]{3,2,1,0:T(8,128)(2,1)} %repack.5.refs_2_), calls=%async_computation.2 | async-start | bytes 3145728 | tf_op jit(solution)/shard_map/all_to_all | solution.py:283
  99.5 13.7 %copy-start = (bf16[4,4,384,128]{3,2,1,0:T(8,128)(2,1)S(1)}, bf16[4,4,384,128]{3,2,1,0:T(8,128)(2,1)}, u32[]{:S(2)}) copy-start(bf16[4,4,384,128]{3,2,1,0:T(8,128)(2,1)} %repack.5.refs_2_) | copy-start | bytes 4718596
  102.6 40.7 %collective-permute-start.6 = (bf16[4,384,128]{2,1,0:T(8,128)(2,1)}, bf16[4,384,128]{2,1,0:T(8,128)(2,1)S(1)}, u32[]{:S(2)}, u32[]{:S(2)}) collective-permute-start(bf16[4,384,128]{2,1,0:T(8,128)(2,1)} %get-tuple-element.42), channel_id=1, source_target_pairs={{0,4},{1,5},{2,6},{3,7},{4,0},{5,1},{6,2},{7,3},{8,12},{9,13},{10,... | collective-permute-start | bytes 1179656 | tf_op jit(solution)/shard_map/ppermute | solution.py:254
  110.7 32.6 %collective-permute-start.7 = (bf16[4,384,128]{2,1,0:T(8,128)(2,1)}, bf16[4,384,128]{2,1,0:T(8,128)(2,1)}, u32[]{:S(2)}, u32[]{:S(2)}) collective-permute-start(bf16[4,384,128]{2,1,0:T(8,128)(2,1)} %get-tuple-element.44), channel_id=1, source_target_pairs={{0,8},{1,9},{2,10},{3,11},{4,12},{5,13},{6,14},{7,15},{8,0},{9,1},... | collective-permute-start | bytes 1179656 | tf_op jit(solution)/shard_map/ppermute | solution.py:254
  111.7 31.6 %collective-permute-start.8 = (bf16[4,384,128]{2,1,0:T(8,128)(2,1)}, bf16[4,384,128]{2,1,0:T(8,128)(2,1)}, u32[]{:S(2)}, u32[]{:S(2)}) collective-permute-start(bf16[4,384,128]{2,1,0:T(8,128)(2,1)} %get-tuple-element.45), channel_id=1, source_target_pairs={{0,12},{1,13},{2,14},{3,15},{4,8},{5,9},{6,10},{7,11},{8,4},{9,5},... | collective-permute-start | bytes 1179656 | tf_op jit(solution)/shard_map/ppermute | solution.py:254
  113.1 1.4 copy-start.2
  114.6 1.0 copy-start.7
  130.9 37.7 %all-to-all-start.1 = ((bf16[16,128,128]{2,1,0:T(8,128)(2,1)}), bf16[16,128,128]{2,1,0:T(8,128)(2,1)}, u32[]{:S(2)}, u32[]{:S(2)}) async-start(bf16[16,128,128]{2,1,0:T(8,128)(2,1)} %attend.4.refs_4_.refs_1_), calls=%async_computation.1 | async-start | bytes 1048576 | tf_op jit(solution)/shard_map/all_to_all | solution.py:299
  139.1 26.8 %collective-permute-start.12 = (bf16[4,384,128]{2,1,0:T(8,128)(2,1)}, bf16[4,384,128]{2,1,0:T(8,128)(2,1)S(1)}, u32[]{:S(2)}, u32[]{:S(2)}) collective-permute-start(bf16[4,384,128]{2,1,0:T(8,128)(2,1)} %get-tuple-element.52), channel_id=1, source_target_pairs={{0,4},{1,5},{2,6},{3,7},{4,0},{5,1},{6,2},{7,3},{8,12},{9,13},{10,... | collective-permute-start | bytes 1179656 | tf_op jit(solution)/shard_map/ppermute | solution.py:254
  140.9 56.1 %collective-permute-start.14 = (bf16[4,384,128]{2,1,0:T(8,128)(2,1)}, bf16[4,384,128]{2,1,0:T(8,128)(2,1)}, u32[]{:S(2)}, u32[]{:S(2)}) collective-permute-start(bf16[4,384,128]{2,1,0:T(8,128)(2,1)} %get-tuple-element.56), channel_id=1, source_target_pairs={{0,8},{1,9},{2,10},{3,11},{4,12},{5,13},{6,14},{7,15},{8,0},{9,1},... | collective-permute-start | bytes 1179656 | tf_op jit(solution)/shard_map/ppermute | solution.py:254
  143.3 0.7 copy-start.4
  146.7 34.9 %collective-permute-start.9 = (bf16[4,384,128]{2,1,0:T(8,128)(2,1)}, bf16[4,384,128]{2,1,0:T(8,128)(2,1)S(1)}, u32[]{:S(2)}, u32[]{:S(2)}) collective-permute-start(bf16[4,384,128]{2,1,0:T(8,128)(2,1)} %get-tuple-element.49), channel_id=1, source_target_pairs={{0,1},{1,0},{2,3},{3,2},{4,5},{5,4},{6,7},{7,6},{8,9},{9,8},{10,11... | collective-permute-start | bytes 1179656 | tf_op jit(solution)/shard_map/ppermute | solution.py:254
  146.7 34.9 %collective-permute-start.10 = (bf16[4,384,128]{2,1,0:T(8,128)(2,1)}, bf16[4,384,128]{2,1,0:T(8,128)(2,1)S(1)}, u32[]{:S(2)}, u32[]{:S(2)}) collective-permute-start(bf16[4,384,128]{2,1,0:T(8,128)(2,1)} %get-tuple-element.50), channel_id=1, source_target_pairs={{0,2},{1,3},{2,0},{3,1},{4,6},{5,7},{6,4},{7,5},{8,10},{9,11},{10,... | collective-permute-start | bytes 1179656 | tf_op jit(solution)/shard_map/ppermute | solution.py:254
  148.1 33.4 %collective-permute-start.11 = (bf16[4,384,128]{2,1,0:T(8,128)(2,1)}, bf16[4,384,128]{2,1,0:T(8,128)(2,1)S(1)}, u32[]{:S(2)}, u32[]{:S(2)}) collective-permute-start(bf16[4,384,128]{2,1,0:T(8,128)(2,1)} %get-tuple-element.51), channel_id=1, source_target_pairs={{0,3},{1,2},{2,1},{3,0},{4,7},{5,6},{6,5},{7,4},{8,11},{9,10},{10,... | collective-permute-start | bytes 1179656 | tf_op jit(solution)/shard_map/ppermute | solution.py:254
  148.5 1.0 copy-start.5
  149.5 1.0 copy-start.8
  150.5 31.1 %copy-start.9 = (bf16[4,384,128]{2,1,0:T(8,128)(2,1)S(1)}, bf16[4,384,128]{2,1,0:T(8,128)(2,1)}, u32[]{:S(2)}) copy-start(bf16[4,384,128]{2,1,0:T(8,128)(2,1)} %get-tuple-element.46.refs_3_.refs_0_) | copy-start | bytes 1179652
  165.9 31.1 %copy-start.3 = (bf16[4,384,128]{2,1,0:T(8,128)(2,1)}, bf16[4,384,128]{2,1,0:T(8,128)(2,1)S(1)}, u32[]{:S(2)}) copy-start(bf16[4,384,128]{2,1,0:T(8,128)(2,1)S(1)} %collective-permute-done.12.refs_5_.refs_1_) | copy-start | bytes 1179652
  165.9 31.1 %collective-permute-start.15 = (bf16[4,384,128]{2,1,0:T(8,128)(2,1)}, bf16[4,384,128]{2,1,0:T(8,128)(2,1)S(1)}, u32[]{:S(2)}, u32[]{:S(2)}) collective-permute-start(bf16[4,384,128]{2,1,0:T(8,128)(2,1)} %get-tuple-element.57), channel_id=1, source_target_pairs={{0,12},{1,13},{2,14},{3,15},{4,8},{5,9},{6,10},{7,11},{8,4},{9,5},... | collective-permute-start | bytes 1179656 | tf_op jit(solution)/shard_map/ppermute | solution.py:254
  168.6 34.0 %all-to-all-start.3 = ((bf16[16,128,128]{2,1,0:T(8,128)(2,1)}), bf16[16,128,128]{2,1,0:T(8,128)(2,1)S(1)}, u32[]{:S(2)}, u32[]{:S(2)}) async-start(bf16[16,128,128]{2,1,0:T(8,128)(2,1)} %attend.5.refs_4_), calls=%async_computation.3 | async-start | bytes 1048576 | tf_op jit(solution)/shard_map/all_to_all | solution.py:299
  197.0 0.8 copy-start.16
  200.4 9.6 %collective-permute-start.16 = (bf16[4,384,128]{2,1,0:T(8,128)(2,1)}, bf16[4,384,128]{2,1,0:T(8,128)(2,1)S(1)}, u32[]{:S(2)}, u32[]{:S(2)}) collective-permute-start(bf16[4,384,128]{2,1,0:T(8,128)(2,1)} %get-tuple-element.59), channel_id=1, source_target_pairs={{0,1},{1,0},{2,3},{3,2},{4,5},{5,4},{6,7},{7,6},{8,9},{9,8},{10,11... | collective-permute-start | bytes 1179656 | tf_op jit(solution)/shard_map/ppermute | solution.py:254
  200.8 12.2 %collective-permute-start.17 = (bf16[4,384,128]{2,1,0:T(8,128)(2,1)}, bf16[4,384,128]{2,1,0:T(8,128)(2,1)S(1)}, u32[]{:S(2)}, u32[]{:S(2)}) collective-permute-start(bf16[4,384,128]{2,1,0:T(8,128)(2,1)} %get-tuple-element.60), channel_id=1, source_target_pairs={{0,2},{1,3},{2,0},{3,1},{4,6},{5,7},{6,4},{7,5},{8,10},{9,11},{10,... | collective-permute-start | bytes 1179656 | tf_op jit(solution)/shard_map/ppermute | solution.py:254
  202.5 22.4 %collective-permute-start.18 = (bf16[4,384,128]{2,1,0:T(8,128)(2,1)}, bf16[4,384,128]{2,1,0:T(8,128)(2,1)S(1)}, u32[]{:S(2)}, u32[]{:S(2)}) collective-permute-start(bf16[4,384,128]{2,1,0:T(8,128)(2,1)} %get-tuple-element.61), channel_id=1, source_target_pairs={{0,3},{1,2},{2,1},{3,0},{4,7},{5,6},{6,5},{7,4},{8,11},{9,10},{10,... | collective-permute-start | bytes 1179656 | tf_op jit(solution)/shard_map/ppermute | solution.py:254
  202.5 38.8 %copy-start.11 = (bf16[16,128,128]{2,1,0:T(8,128)(2,1)}, bf16[16,128,128]{2,1,0:T(8,128)(2,1)S(1)}, u32[]{:S(2)}) copy-start(bf16[16,128,128]{2,1,0:T(8,128)(2,1)S(1)} %all-to-all-done.3) | copy-start | bytes 1572868
  202.5 38.8 %all-to-all-start.4 = ((bf16[16,128,128]{2,1,0:T(8,128)(2,1)}), bf16[16,128,128]{2,1,0:T(8,128)(2,1)S(1)}, u32[]{:S(2)}, u32[]{:S(2)}) async-start(bf16[16,128,128]{2,1,0:T(8,128)(2,1)} %attend.6.refs_4_), calls=%async_computation.4 | async-start | bytes 1048576 | tf_op jit(solution)/shard_map/all_to_all | solution.py:299
  209.3 55.1 %all-gather.9.cloned.1.call-start = ((), (), s32[]{:S(2)}) async-start(), calls=%async_computation.7 | async-start | bytes 1572864 | tf_op jit(solution)/shard_map/all_gather | solution.py:302
  225.0 1.0 copy-start.10
  241.3 27.5 %copy-start.12 = (bf16[16,128,128]{2,1,0:T(8,128)(2,1)}, bf16[16,128,128]{2,1,0:T(8,128)(2,1)S(1)}, u32[]{:S(2)}) copy-start(bf16[16,128,128]{2,1,0:T(8,128)(2,1)S(1)} %all-to-all-done.4) | copy-start | bytes 1572868
  241.3 21.5 %all-to-all-start.5 = ((bf16[16,128,128]{2,1,0:T(8,128)(2,1)}), bf16[16,128,128]{2,1,0:T(8,128)(2,1)S(1)}, u32[]{:S(2)}, u32[]{:S(2)}) async-start(bf16[16,128,128]{2,1,0:T(8,128)(2,1)} %attend.7), calls=%async_computation.5 | async-start | bytes 1048576 | tf_op jit(solution)/shard_map/all_to_all | solution.py:299
  248.4 35.5 %all-gather.11.cloned.1.call-start = ((), (), s32[]{:S(2)}) async-start(), calls=%async_computation.8 | async-start | bytes 1572864 | tf_op jit(solution)/shard_map/all_gather | solution.py:302
  249.1 39.1 %collective-permute-start.13 = (bf16[1,16,128,128]{3,2,1,0:T(8,128)(2,1)S(1)}, bf16[1,16,128,128]{3,2,1,0:T(8,128)(2,1)S(1)}, u32[]{:S(2)}, u32[]{:S(2)}) collective-permute-start(bf16[1,16,128,128]{3,2,1,0:T(8,128)(2,1)S(1)} %bitcast.19), channel_id=1, source_target_pairs={{0,16},{16,0},{1,17},{17,1},{2,18},{18,2},{3,19},{19,3},{4,20},{20... | collective-permute-start | bytes 1572872 | tf_op jit(solution)/shard_map/ppermute | solution.py:254
  262.8 5.9 %copy-start.13 = (bf16[16,128,128]{2,1,0:T(8,128)(2,1)}, bf16[16,128,128]{2,1,0:T(8,128)(2,1)S(1)}, u32[]{:S(2)}) copy-start(bf16[16,128,128]{2,1,0:T(8,128)(2,1)S(1)} %all-to-all-done.5) | copy-start | bytes 1572868
  262.8 30.6 %collective-permute-start.19 = (bf16[1,16,128,128]{3,2,1,0:T(8,128)(2,1)S(1)}, bf16[1,16,128,128]{3,2,1,0:T(8,128)(2,1)S(1)}, u32[]{:S(2)}, u32[]{:S(2)}) collective-permute-start(bf16[1,16,128,128]{3,2,1,0:T(8,128)(2,1)S(1)} %bitcast.21), channel_id=1, source_target_pairs={{0,16},{16,0},{1,17},{17,1},{2,18},{18,2},{3,19},{19,3},{4,20},{20... | collective-permute-start | bytes 1572872 | tf_op jit(solution)/shard_map/ppermute | solution.py:254
  288.2 0.8 copy-start.15
  293.5 0.8 copy-start.14
Sparse Core Ops, SparseCore 0:
  9.5 59.4 all-gather.6
  211.7 22.6 all-gather.8
  250.7 33.0 all-gather.10

commit v4 on v3

--- a/solution.py
+++ b/solution.py
@@ -21,33 +21,37 @@
     sources, out_refs = refs[:3], refs[3 + ahead :]
     lane_blocks = sources[0].shape[3] // LANES
     high = me_ref[0] // near
-    for shift, out_ref in enumerate(out_refs):
+    single = len(out_refs) == 1
+    far = out_refs[0].shape[1] if single else len(out_refs)
+    for shift in range(far):
         for low in range(near):
+            target = out_refs[0].at[low, shift] if single else out_refs[shift].at[low]
             block = (high ^ shift) * near + low
             video = 0 if per_chunk == 1 else block // lane_blocks
             column = block if per_chunk == 1 else block % lane_blocks
             lanes = pl.ds(pl.multiple_of(column * LANES, LANES), LANES)
             for which, source in enumerate(sources):
                 here = slice(which * rows, (which + 1) * rows)
-                out_ref[low, here, :] = source[video, 0, :, lanes]
-
-
-def pack(me, sources, first_batch, per_chunk, parts, after=()):
-    batch_size, single, rows, width = sources[0].shape
+                target[here, :] = source[video, 0, :, lanes]
+
+
+def pack(me, sources, first_batch, per_chunk, parts, single, after=()):
+    batch_size, _, rows, width = sources[0].shape
     near = split_size(parts)
     far = parts // near
     spec = pl.BlockSpec(
         (per_chunk, 1, rows, width), lambda i: (first_batch // per_chunk, 0, 0, 0)
     )
-    shape = (near, 3 * rows, LANES)
+    shape = (near, far, 3 * rows, LANES) if single else (near, 3 * rows, LANES)
+    count = 1 if single else far
     return pl.pallas_call(
         functools.partial(pack_kernel, near, per_chunk, rows, len(after)),
         grid=(1,),
         in_specs=[pl.BlockSpec(memory_space=pltpu.SMEM)]
         + [spec] * 3
         + [pl.BlockSpec(memory_space=pl.ANY)] * len(after),
-        out_specs=[pl.BlockSpec(shape, lambda i: (0, 0, 0))] * far,
-        out_shape=[jax.ShapeDtypeStruct(shape, sources[0].dtype)] * far,
+        out_specs=[pl.BlockSpec(shape, lambda i: (0,) * len(shape))] * count,
+        out_shape=[jax.ShapeDtypeStruct(shape, sources[0].dtype)] * count,
         cost_estimate=pl.CostEstimate(
             flops=0, bytes_accessed=parts * 3 * rows * LANES * 4, transcendentals=0
         ),
@@ -83,7 +87,28 @@
     )(me, *blocks, *after)
 
 
-def attend_kernel(group, rows, parts, near, count, me_ref, *refs):
+def unpack_kernel(near, ahead, in_ref, *refs):
+    for shift, out_ref in enumerate(refs[ahead:]):
+        for other in range(near):
+            out_ref[other] = in_ref[other, shift]
+
+
+def unpack(block, after=()):
+    near, far, rows, lanes = block.shape
+    shape = (near, rows, lanes)
+    return pl.pallas_call(
+        functools.partial(unpack_kernel, near, len(after)),
+        in_specs=[pl.BlockSpec(memory_space=pltpu.VMEM)]
+        + [pl.BlockSpec(memory_space=pl.ANY)] * len(after),
+        out_shape=[jax.ShapeDtypeStruct(shape, block.dtype)] * far,
+        cost_estimate=pl.CostEstimate(
+            flops=0, bytes_accessed=near * far * rows * lanes * 4, transcendentals=0
+        ),
+        name="unpack",
+    )(block, *after)
+
+
+def attend_kernel(group, rows, parts, near, by_far, count, me_ref, *refs):
     in_refs = refs[:count]
     out_ref, query_scr, key_scr, value_scr = refs[-4:]
     step = pl.program_id(0)
@@ -104,7 +129,9 @@
         high, low = me_ref[0] // near, me_ref[0] % near
         for shift in range(parts // near):
             for other in range(near):
-                if count == 1:
+                if by_far:
+                    load(in_refs[shift], other, (high ^ shift) * near + other)
+                elif count == 1:
                     load(in_refs[0].at[other], shift, (high ^ shift) * near + other)
                 else:
                     load(in_refs[other], shift, (high ^ shift) * near + (low ^ other))
@@ -133,7 +160,7 @@
     out_ref[...] = merged.reshape(group, rows, LANES)
 
 
-def attend(me, arrived, parts, after=()):
+def attend(me, arrived, parts, by_far, after=()):
     triple = arrived[0].shape[-2]
     rows = triple // 3
     length = parts * rows
@@ -141,7 +168,9 @@
     group = max(1, 512 // rows)
     count = len(arrived)
     return pl.pallas_call(
-        functools.partial(attend_kernel, group, rows, parts, split_size(parts), count),
+        functools.partial(
+            attend_kernel, group, rows, parts, split_size(parts), by_far, count
+        ),
         grid=(parts // group,),
         in_specs=[pl.BlockSpec(memory_space=pltpu.SMEM)]
         + [pl.BlockSpec(value.shape, lambda i, n=value.ndim: (0,) * n) for value in arrived]
@@ -270,36 +299,59 @@
     neighbours = [list(range(i, i + near)) for i in range(0, seq_size, near)]
     keys = lax.all_gather(key_rows, "view")
     sources = (queries, key_rows, value_rows)
-    packed, crossed, received = [], [], []
+    last = chunks - 1 if chunks > 1 else None
+
+    def lay_out(c, single, after=()):
+        return pack(me, sources, c * per_chunk, per_chunk, seq_size, single, after)
+
+    crossed, first = {}, ()
     for c in range(chunks):
-        after = tuple(blocks[0] for blocks in packed[-1:])
-        packed.append(pack(me, sources, c * per_chunk, per_chunk, seq_size, after))
-        crossed.append(swap(packed[c], "seq", seq_size, near))
-    repacked, received = [], []
+        if c != last:
+            blocks = lay_out(c, False, first)
+            first = (blocks[0],)
+            crossed[c] = swap(blocks, "seq", seq_size, near)
+        if c == 1 or (c == 0 and last == 1):
+            (blocks,) = lay_out(last, True, first + (crossed[0][1],))
+            last_blocks = unpack(exchange(blocks, axis_index_groups=neighbours))
+    if last is not None:
+        crossed[last] = swap(last_blocks, "seq", seq_size, near)
+
+    repacked, received = {}, {}
 
     def arrive(c, after):
-        repacked.append(repack(me, crossed[c], 2 * c < chunks, after))
-        if 2 * c < chunks:
-            received.append([exchange(repacked[c][0], axis_index_groups=neighbours)])
+        if c == last:
+            received[c] = crossed[c]
+            return
+        if c + 1 in crossed:
+            after += (crossed[c + 1][1],)
+        if c == 1:
+            after += (last_blocks[0],)
+        repacked[c] = repack(me, crossed[c], c < 2, after)
+        if c < 2:
+            received[c] = [exchange(repacked[c][0], axis_index_groups=neighbours)]
         else:
-            received.append(swap(repacked[c], "seq", seq_size, 1))
+            received[c] = swap(repacked[c], "seq", seq_size, 1)
 
     arrive(0, ())
-    carry, attended = (), ()
+    if chunks > 1:
+        arrive(1, ())
+    carry, attended, first_output = (), (), ()
     for c in range(chunks):
-        after = attended + tuple(blocks[1] for blocks in crossed[c + 1 : c + 2])
-        if c + 1 < chunks - 1:
-            arrive(c + 1, attended or (repacked[0][0],))
+        after = attended
+        if 1 < c + 1 < chunks:
+            arrive(c + 1, attended)
+        if c + 1 in repacked and c > 0:
             after += (repacked[c + 1][0],)
         if c == 1:
             after += (keys,)
-        attended = (attend(me, received[c], seq_size, after),)
-        if c + 1 == chunks - 1:
-            arrive(c + 1, attended)
+        if c == last and c > 1:
+            after += first_output
+        attended = (attend(me, received[c], seq_size, c == last, after),)
         returned = exchange(attended[0])
         own = returned[None]
-        if c + 2 < chunks:
+        if c + 2 < chunks and c == 0:
             outputs = [own] + [lax.all_gather(returned, "view")] * (views - 1)
+            first_output = tuple(outputs[1:2])
         else:
             outputs = swap([own] * views, "view", views, 1)
         carry = combine(view, carry, view_queries, keys, outputs, c * per_chunk)

time: 307 us -> 314 us (1.023)
  starting transfers between devices: 79.3 us -> 97 us
  waiting for transfers between devices: 99.1 us -> 90.8 us
  local copies, waits for them, and re-layouts: 11.5 us -> 7.91 us
    all_to_all x4, starting transfers between devices: 32 us -> 50.1 us  [local(): returned = exchange(attended[0])]
    all_gather x2 -> x1, waiting for transfers between devices: 15.1 us -> 0.01 us  [local(): outputs = [own] + [lax.all_gather(returned, 'view')] * (views - 1)]
    ppermute x20 -> x18, waiting for transfers between devices: 69.8 us -> 77 us  [swap(): lax.ppermute(blocks[shift], axis, [(i, i ^ shift * stride) for i in range...]
    ppermute x20 -> x18, starting transfers between devices: 40.1 us -> 36 us  [swap(): lax.ppermute(blocks[shift], axis, [(i, i ^ shift * stride) for i in range...]
    all_to_all x2 -> x3, starting transfers between devices: 7.13 us -> 10.8 us  [the longest x2 7.13 us: arrive(): received[c] = [exchange(repacked[c][0], axis_index_groups=neighbours)]]
    unnamed x44, local copies, waits for them, and re-layouts: 11.5 us -> 7.91 us
    pallas_call x4 -> x3, Pallas kernels: 10.5 us -> 7.86 us  [repack(): pl.pallas_call(functools.partial(repack_kernel, near, far, len(after)), i...]
  transfers between devices with their start and end apart: 29 -> 27, of which waited for: 8 -> 11; matrix products, arithmetic and copies ran while one was open for 0% -> 0% of each run, Pallas kernels for 32% -> 31%
where the time goes in v4:
time: 314 us; the launch traced here: 312 us
  Pallas kernels  102 us (32%)
  starting transfers between devices  97 us (31%)
  waiting for transfers between devices  90.8 us (29%)
  between operations  14.2 us (5%)
  local copies, waits for them, and re-layouts  7.91 us (3%)
    ppermute x18, waiting for transfers between devices, swap(): lax.ppermute(blocks[shift], axis, [(i, i ^ shift * stride) for i in range...  77 us
    pallas_call x4, Pallas kernels, attend(): pl.pallas_call(functools.partial(attend_kernel, group, rows, parts, split...  62.4 us
    all_to_all x4, starting transfers between devices, local(): returned = exchange(attended[0])  50.1 us
    ppermute x18, starting transfers between devices, swap(): lax.ppermute(blocks[shift], axis, [(i, i ^ shift * stride) for i in range...  36 us
    pallas_call x4, Pallas kernels, combine(): pl.pallas_call(functools.partial(combine_kernel, views, group, carried),...  17.6 us
    all_to_all x4, waiting for transfers between devices, local(): returned = exchange(attended[0])  12.4 us
    pallas_call x4, Pallas kernels, pack(): pl.pallas_call(functools.partial(pack_kernel, near, per_chunk, rows, len(...  11.9 us
    unnamed x44, local copies, waits for them, and re-layouts  7.91 us
  transfers between devices with their start and end apart: 27, of which 11 were waited for; matrix products, arithmetic and copies ran while one was open for 0% of the time, Pallas kernels for 31%

profile of v4, /device:TPU:0, one launch (start us, length us, event | category | flops | bytes accessed | tf_op | source)
XLA Modules:
  0.0 312.2 jit_solution(7050238618148122720)
XLA Ops:
  7.2 0.0 all-gather.5.cloned.1.call-start
  7.2 0.7 all-gather.5.cloned.1.call-update
  7.9 2.9 pack.4
  10.8 3.0 collective-permute-start
  13.8 2.9 pack.5
  16.8 6.4 %collective-permute-done.refs_1_.refs_4_ = bf16[4,384,128]{2,1,0:T(8,128)(2,1)S(1)} collective-permute-done((bf16[4,384,128]{2,1,0:T(8,128)(2,1)}, bf16[4,384,128]{2,1,0:T(8,128)(2,1)S(1)}, u32[]{:S(2)}, u32[]{:S(2)}) %collective-permute-start) | collective-permute-done | bytes 393248 | tf_op jit(solution)/shard_map/ppermute | solution.py:283
  23.2 0.7 copy-done.11
  23.9 3.0 pack.7
  26.9 3.7 %all-to-all-start.2 = ((bf16[4,4,384,128]{3,2,1,0:T(8,128)(2,1)}), bf16[4,4,384,128]{3,2,1,0:T(8,128)(2,1)S(1)}, u32[]{:S(2)}, u32[]{:S(2)}) async-start(bf16[4,4,384,128]{3,2,1,0:T(8,128)(2,1)} %pack.7), calls=%async_computation.2 | async-start | bytes 3145728 | tf_op jit(solution)/shard_map/all_to_all | solution.py:315
  30.7 2.8 collective-permute-start.1
  33.5 1.3 collective-permute-start.2
  34.8 0.3 collective-permute-start.3
  35.1 25.5 %collective-permute-done.1.refs_2_ = bf16[4,384,128]{2,1,0:T(8,128)(2,1)S(1)} collective-permute-done((bf16[4,384,128]{2,1,0:T(8,128)(2,1)}, bf16[4,384,128]{2,1,0:T(8,128)(2,1)S(1)}, u32[]{:S(2)}, u32[]{:S(2)}) %collective-permute-start.1) | collective-permute-done | bytes 393248 | tf_op jit(solution)/shard_map/ppermute | solution.py:283
  60.6 0.7 collective-permute-done.3.refs_4_.refs_1_
  61.4 0.2 copy-done.19
  61.6 0.8 copy-done.13
  62.4 2.6 repack.3
  65.0 3.6 %all-to-all-start = ((bf16[4,4,384,128]{3,2,1,0:T(8,128)(2,1)}), bf16[4,4,384,128]{3,2,1,0:T(8,128)(2,1)S(1)}, u32[]{:S(2)}, u32[]{:S(2)}) async-start(bf16[4,4,384,128]{3,2,1,0:T(8,128)(2,1)} %repack.3), calls=%async_computation | async-start | bytes 3145728 | tf_op jit(solution)/shard_map/all_to_all | solution.py:331
  68.5 10.6 %collective-permute-start.4 = (bf16[4,384,128]{2,1,0:T(8,128)(2,1)}, bf16[4,384,128]{2,1,0:T(8,128)(2,1)S(1)}, u32[]{:S(2)}, u32[]{:S(2)}) collective-permute-start(bf16[4,384,128]{2,1,0:T(8,128)(2,1)} %get-tuple-element.36), channel_id=1, source_target_pairs={{0,8},{1,9},{2,10},{3,11},{4,12},{5,13},{6,14},{7,15},{8,0},{9,1},... | collective-permute-start | bytes 1179656 | tf_op jit(solution)/shard_map/ppermute | solution.py:283
  79.1 0.5 collective-permute-start.5
  79.6 3.0 pack.6
  82.6 0.2 collective-permute-start.6
  82.8 2.6 unpack.1
  85.4 20.8 %collective-permute-done.4.refs_2_ = bf16[4,384,128]{2,1,0:T(8,128)(2,1)S(1)} collective-permute-done((bf16[4,384,128]{2,1,0:T(8,128)(2,1)}, bf16[4,384,128]{2,1,0:T(8,128)(2,1)S(1)}, u32[]{:S(2)}, u32[]{:S(2)}) %collective-permute-start.4) | collective-permute-done | bytes 393248 | tf_op jit(solution)/shard_map/ppermute | solution.py:283
  106.2 4.0 %collective-permute-done.6.refs_4_.refs_1_ = bf16[4,384,128]{2,1,0:T(8,128)(2,1)S(1)} collective-permute-done((bf16[4,384,128]{2,1,0:T(8,128)(2,1)}, bf16[4,384,128]{2,1,0:T(8,128)(2,1)S(1)}, u32[]{:S(2)}, u32[]{:S(2)}) %collective-permute-start.6) | collective-permute-done | bytes 393248 | tf_op jit(solution)/shard_map/ppermute | solution.py:283
  110.2 0.8 copy-done.12
  111.0 2.6 repack.4
  113.6 3.6 %all-to-all-start.3 = ((bf16[4,4,384,128]{3,2,1,0:T(8,128)(2,1)}), bf16[4,4,384,128]{3,2,1,0:T(8,128)(2,1)S(1)}, u32[]{:S(2)}, u32[]{:S(2)}) async-start(bf16[4,4,384,128]{3,2,1,0:T(8,128)(2,1)} %repack.4), calls=%async_computation.3 | async-start | bytes 3145728 | tf_op jit(solution)/shard_map/all_to_all | solution.py:331
  117.2 3.9 %collective-permute-start.7 = (bf16[4,384,128]{2,1,0:T(8,128)(2,1)}, bf16[4,384,128]{2,1,0:T(8,128)(2,1)}, u32[]{:S(2)}, u32[]{:S(2)}) collective-permute-start(bf16[4,384,128]{2,1,0:T(8,128)(2,1)} %get-tuple-element.41), channel_id=1, source_target_pairs={{0,8},{1,9},{2,10},{3,11},{4,12},{5,13},{6,14},{7,15},{8,0},{9,1},... | collective-permute-start | bytes 1179656 | tf_op jit(solution)/shard_map/ppermute | solution.py:283
  121.0 3.4 %collective-permute-start.8 = (bf16[4,384,128]{2,1,0:T(8,128)(2,1)}, bf16[4,384,128]{2,1,0:T(8,128)(2,1)}, u32[]{:S(2)}, u32[]{:S(2)}) collective-permute-start(bf16[4,384,128]{2,1,0:T(8,128)(2,1)} %get-tuple-element.42), channel_id=1, source_target_pairs={{0,12},{1,13},{2,14},{3,15},{4,8},{5,9},{6,10},{7,11},{8,4},{9,5},... | collective-permute-start | bytes 1179656 | tf_op jit(solution)/shard_map/ppermute | solution.py:283
  124.4 15.3 %attend.4.refs_4_.refs_1_ = bf16[16,128,128]{2,1,0:T(8,128)(2,1)} custom-call(s32[1]{0:T(128)} %bitcast.2.me_ref, bf16[4,4,384,128]{3,2,1,0:T(8,128)(2,1)S(1)} %all-to-all-done.refs_0_), custom_call_target="tpu_custom_call" | custom-call | flops 8589934592 | bytes 2097152 | tf_op jit(solution)/shard_map/attend/pallas_call | solution.py:170
  139.7 4.8 %all-to-all-start.1 = ((bf16[16,128,128]{2,1,0:T(8,128)(2,1)}), bf16[16,128,128]{2,1,0:T(8,128)(2,1)S(1)}, u32[]{:S(2)}, u32[]{:S(2)}) async-start(bf16[16,128,128]{2,1,0:T(8,128)(2,1)} %attend.4.refs_4_.refs_1_), calls=%async_computation.1 | async-start | bytes 1048576 | tf_op jit(solution)/shard_map/all_to_all | solution.py:350
  144.5 3.7 %collective-permute-done.7.refs_2_ = bf16[4,384,128]{2,1,0:T(8,128)(2,1)} collective-permute-done((bf16[4,384,128]{2,1,0:T(8,128)(2,1)}, bf16[4,384,128]{2,1,0:T(8,128)(2,1)}, u32[]{:S(2)}, u32[]{:S(2)}) %collective-permute-start.7) | collective-permute-done | bytes 393248 | tf_op jit(solution)/shard_map/ppermute | solution.py:283
  148.2 2.0 collective-permute-done.9.refs_5_.refs_1_
  150.3 0.8 copy-done.2
  151.0 2.7 repack.5
  153.7 1.9 collective-permute-start.12
  155.6 0.2 collective-permute-start.13
  155.8 1.0 copy-done.4
  156.8 15.3 %attend.5.refs_4_ = bf16[16,128,128]{2,1,0:T(8,128)(2,1)} custom-call(s32[1]{0:T(128)} %bitcast.2.me_ref, bf16[4,4,384,128]{3,2,1,0:T(8,128)(2,1)S(1)} %all-to-all-done.3.refs_0_, bf16[16,128,128]{2,1,0:T(8,128)(2,1)} %attend.4.refs_4_.refs_1_, bf16[4,384,128]{2,1,0:T(8,128)(2,1)S(1)} %copy-done.4, bf16[2,4,1,128,2048]{4,3,2,1,0:T(8,128)(2,1)} %bitcast.10), custom_call_target="tpu_custom_call" | custom-call | flops 8589934592 | bytes 2097152 | tf_op jit(solution)/shard_map/attend/pallas_call | solution.py:170
  172.1 16.7 %all-to-all-start.4 = ((bf16[16,128,128]{2,1,0:T(8,128)(2,1)}), bf16[16,128,128]{2,1,0:T(8,128)(2,1)S(1)}, u32[]{:S(2)}, u32[]{:S(2)}) async-start(bf16[16,128,128]{2,1,0:T(8,128)(2,1)} %attend.5.refs_4_), calls=%async_computation.4 | async-start | bytes 1048576 | tf_op jit(solution)/shard_map/all_to_all | solution.py:350
  188.8 0.0 all-gather.7.cloned.1.call-start
  188.9 0.7 all-gather.7.cloned.1.call-update
  189.6 2.9 collective-permute-start.15
  192.5 1.5 collective-permute-start.16
  194.0 16.4 %attend.6.refs_4_ = bf16[16,128,128]{2,1,0:T(8,128)(2,1)} custom-call(s32[1]{0:T(128)} %bitcast.2.me_ref, bf16[4,384,128]{2,1,0:T(8,128)(2,1)S(1)} %copy-done.5, bf16[4,384,128]{2,1,0:T(8,128)(2,1)S(1)} %collective-permute-done.11.refs_1_, bf16[4,384,128]{2,1,0:T(8,128)(2,1)S(1)} %collective-permute-done.12.refs_2_, ...), custom_call_target="tpu_custom_call" | custom-call | flops 8589934592 | bytes 2097152 | tf_op jit(solution)/shard_map/attend/pallas_call | solution.py:170
  210.4 14.3 %all-to-all-start.5 = ((bf16[16,128,128]{2,1,0:T(8,128)(2,1)}), bf16[16,128,128]{2,1,0:T(8,128)(2,1)S(1)}, u32[]{:S(2)}, u32[]{:S(2)}) async-start(bf16[16,128,128]{2,1,0:T(8,128)(2,1)} %attend.6.refs_4_), calls=%async_computation.5 | async-start | bytes 1048576 | tf_op jit(solution)/shard_map/all_to_all | solution.py:350
  224.6 7.8 %collective-permute-done.15.refs_2_ = bf16[4,384,128]{2,1,0:T(8,128)(2,1)S(1)} collective-permute-done((bf16[4,384,128]{2,1,0:T(8,128)(2,1)}, bf16[4,384,128]{2,1,0:T(8,128)(2,1)S(1)}, u32[]{:S(2)}, u32[]{:S(2)}) %collective-permute-start.15) | collective-permute-done | bytes 393248 | tf_op jit(solution)/shard_map/ppermute | solution.py:283
  232.5 1.2 copy-done
  233.7 15.3 %attend.7 = bf16[16,128,128]{2,1,0:T(8,128)(2,1)} custom-call(s32[1]{0:T(128)} %bitcast.2.me_ref, bf16[4,384,128]{2,1,0:T(8,128)(2,1)S(1)} %copy-done.1, bf16[4,384,128]{2,1,0:T(8,128)(2,1)S(1)} %copy-done.3, bf16[4,384,128]{2,1,0:T(8,128)(2,1)S(1)} %collective-permute-done.15.refs_2_, bf16[4,384,128]{2,1,0:T(8,128)(2,1)S(1)} %collective-permute-done.16.refs_3_, ...), custom_call_target="tpu_custom_call" | custom-call | flops 8589934592 | bytes 2097152 | tf_op jit(solution)/shard_map/attend/pallas_call | solution.py:170
  249.1 14.3 %all-to-all-start.6 = ((bf16[16,128,128]{2,1,0:T(8,128)(2,1)}), bf16[16,128,128]{2,1,0:T(8,128)(2,1)S(1)}, u32[]{:S(2)}, u32[]{:S(2)}) async-start(bf16[16,128,128]{2,1,0:T(8,128)(2,1)} %attend.7), calls=%async_computation.6 | async-start | bytes 1048576 | tf_op jit(solution)/shard_map/all_to_all | solution.py:350
  263.4 1.6 collective-permute-start.10
  265.0 0.5 collective-permute-start.14
  265.5 12.4 %all-to-all-done.6 = bf16[16,128,128]{2,1,0:T(8,128)(2,1)S(1)} async-done(((bf16[16,128,128]{2,1,0:T(8,128)(2,1)}), bf16[16,128,128]{2,1,0:T(8,128)(2,1)S(1)}, u32[]{:S(2)}, u32[]{:S(2)}) %all-to-all-start.6) | async-done | bytes 524320 | tf_op jit(solution)/shard_map/all_to_all | solution.py:350
  277.8 1.5 collective-permute-start.17
  279.3 4.4 %combine.4 = (bf16[4,1,128,2048]{3,2,1,0:T(8,128)(2,1)}, bf16[4,1,128,2048]{3,2,1,0:T(8,128)(2,1)}) custom-call(s32[1]{0:T(128)} %bitcast.view_ref, bf16[4,1,128,2048]{3,2,1,0:T(8,128)(2,1)} %refs_2_.13, bf16[2,4,1,128,2048]{4,3,2,1,0:T(8,128)(2,1)} %bitcast.11, bf16[2,4,1,128,2048]{4,3,2,1,0:T(8,128)(2,1)} %bitcast.12, bf16[1,16,128,128]{3,2,1,0:T(8,128)(2,1)} %bitcast.19, ...), custom_call_target="tpu_custom_call" | custom-call | flops 536870912 | bytes 3670016 | tf_op jit(solution)/shard_map/combine/pallas_call | solution.py:258
  283.8 0.8 copy-done.16
  284.6 4.4 %combine.5 = (bf16[4,1,128,2048]{3,2,1,0:T(8,128)(2,1)}, bf16[4,1,128,2048]{3,2,1,0:T(8,128)(2,1)}) custom-call(s32[1]{0:T(128)} %bitcast.view_ref, bf16[4,1,128,2048]{3,2,1,0:T(8,128)(2,1)} %get-tuple-element.33.refs_0_, bf16[4,1,128,2048]{3,2,1,0:T(8,128)(2,1)} %get-tuple-element.34.refs_1_, ...), custom_call_target="tpu_custom_call", output_to_operand_aliasing={{0}: (1, {}), {1}: (2, {})} | custom-call | flops 536870912 | bytes 3670016 | tf_op jit(solution)/shard_map/combine/pallas_call | solution.py:258
  289.0 0.4 collective-permute-done.14.refs_6_
  289.4 0.8 copy-done.15
  290.2 4.4 %combine.6 = (bf16[4,1,128,2048]{3,2,1,0:T(8,128)(2,1)}, bf16[4,1,128,2048]{3,2,1,0:T(8,128)(2,1)}) custom-call(s32[1]{0:T(128)} %bitcast.view_ref, bf16[4,1,128,2048]{3,2,1,0:T(8,128)(2,1)} %get-tuple-element.45.refs_0_, bf16[4,1,128,2048]{3,2,1,0:T(8,128)(2,1)} %get-tuple-element.46.refs_1_, ...), custom_call_target="tpu_custom_call", output_to_operand_aliasing={{0}: (1, {}), {1}: (2, {})} | custom-call | flops 536870912 | bytes 3670016 | tf_op jit(solution)/shard_map/combine/pallas_call | solution.py:258
  294.6 5.5 %collective-permute-done.17.refs_6_ = bf16[1,16,128,128]{3,2,1,0:T(8,128)(2,1)S(1)} collective-permute-done((bf16[1,16,128,128]{3,2,1,0:T(8,128)(2,1)S(1)}, bf16[1,16,128,128]{3,2,1,0:T(8,128)(2,1)S(1)}, u32[]{:S(2)}, u32[]{:S(2)}) %collective-permute-start.17) | collective-permute-done | bytes 524320 | tf_op jit(solution)/shard_map/ppermute | solution.py:283
  300.2 0.8 copy-done.14
  301.0 4.4 %combine.7 = (bf16[4,1,128,2048]{3,2,1,0:T(8,128)(2,1)}, bf16[4,1,128,2048]{3,2,1,0:T(8,128)(2,1)}) custom-call(s32[1]{0:T(128)} %bitcast.view_ref, bf16[4,1,128,2048]{3,2,1,0:T(8,128)(2,1)} %get-tuple-element.50.refs_0_, bf16[4,1,128,2048]{3,2,1,0:T(8,128)(2,1)} %get-tuple-element.51.refs_1_, ...), custom_call_target="tpu_custom_call", output_to_operand_aliasing={{0}: (1, {}), {1}: (2, {})} | custom-call | flops 536870912 | bytes 3670016 | tf_op jit(solution)/shard_map/combine/pallas_call | solution.py:258
  (52 shorter events, 0.1 us)
Async XLA Ops:
  7.2 148.6 %all-gather.5.cloned.1.call-start = ((), (), s32[]{:S(2)}) async-start(), calls=%async_computation.7 | async-start | bytes 6291456 | tf_op jit(solution)/shard_map/all_gather | solution.py:300
  10.8 12.3 %collective-permute-start = (bf16[4,384,128]{2,1,0:T(8,128)(2,1)}, bf16[4,384,128]{2,1,0:T(8,128)(2,1)S(1)}, u32[]{:S(2)}, u32[]{:S(2)}) collective-permute-start(bf16[4,384,128]{2,1,0:T(8,128)(2,1)} %get-tuple-element.29), channel_id=1, source_target_pairs={{0,4},{1,5},{2,6},{3,7},{4,0},{5,1},{6,2},{7,3},{8,12},{9,13},{10,... | collective-permute-start | bytes 1179656 | tf_op jit(solution)/shard_map/ppermute | solution.py:283
  23.2 0.7 copy-start.11
  26.9 6.5 %copy-start.20 = (bf16[4,384,128]{2,1,0:T(8,128)(2,1)S(1)}, bf16[4,384,128]{2,1,0:T(8,128)(2,1)}, u32[]{:S(2)}) copy-start(bf16[4,384,128]{2,1,0:T(8,128)(2,1)} %get-tuple-element.31) | copy-start | bytes 1179652
  26.9 7.9 %copy-start.21 = (bf16[4,384,128]{2,1,0:T(8,128)(2,1)S(1)}, bf16[4,384,128]{2,1,0:T(8,128)(2,1)}, u32[]{:S(2)}) copy-start(bf16[4,384,128]{2,1,0:T(8,128)(2,1)} %get-tuple-element.32) | copy-start | bytes 1179652
  26.9 38.0 %all-to-all-start.2 = ((bf16[4,4,384,128]{3,2,1,0:T(8,128)(2,1)}), bf16[4,4,384,128]{3,2,1,0:T(8,128)(2,1)S(1)}, u32[]{:S(2)}, u32[]{:S(2)}) async-start(bf16[4,4,384,128]{3,2,1,0:T(8,128)(2,1)} %pack.7), calls=%async_computation.2 | async-start | bytes 3145728 | tf_op jit(solution)/shard_map/all_to_all | solution.py:315
  30.7 30.0 %collective-permute-start.1 = (bf16[4,384,128]{2,1,0:T(8,128)(2,1)}, bf16[4,384,128]{2,1,0:T(8,128)(2,1)S(1)}, u32[]{:S(2)}, u32[]{:S(2)}) collective-permute-start(bf16[4,384,128]{2,1,0:T(8,128)(2,1)} %get-tuple-element.30), channel_id=1, source_target_pairs={{0,8},{1,9},{2,10},{3,11},{4,12},{5,13},{6,14},{7,15},{8,0},{9,1},... | collective-permute-start | bytes 1179656 | tf_op jit(solution)/shard_map/ppermute | solution.py:283
  33.5 27.2 %collective-permute-start.2 = (bf16[4,384,128]{2,1,0:T(8,128)(2,1)S(1)}, bf16[4,384,128]{2,1,0:T(8,128)(2,1)S(1)}, u32[]{:S(2)}, u32[]{:S(2)}) collective-permute-start(bf16[4,384,128]{2,1,0:T(8,128)(2,1)S(1)} %copy-done.20), channel_id=1, source_target_pairs={{0,12},{1,13},{2,14},{3,15},{4,8},{5,9},{6,10},{7,11},{8,4},{9,5},... | collective-permute-start | bytes 1179656 | tf_op jit(solution)/shard_map/ppermute | solution.py:283
  34.8 26.6 %collective-permute-start.3 = (bf16[4,384,128]{2,1,0:T(8,128)(2,1)S(1)}, bf16[4,384,128]{2,1,0:T(8,128)(2,1)S(1)}, u32[]{:S(2)}, u32[]{:S(2)}) collective-permute-start(bf16[4,384,128]{2,1,0:T(8,128)(2,1)S(1)} %copy-done.21), channel_id=1, source_target_pairs={{0,4},{1,5},{2,6},{3,7},{4,0},{5,1},{6,2},{7,3},{8,12},{9,13},{10,... | collective-permute-start | bytes 1179656 | tf_op jit(solution)/shard_map/ppermute | solution.py:283
  60.6 0.8 copy-start.18
  60.6 0.9 copy-start.19
  61.6 0.8 copy-start.13
  65.0 17.6 %copy-start.6 = (bf16[4,4,384,128]{3,2,1,0:T(8,128)(2,1)}, bf16[4,4,384,128]{3,2,1,0:T(8,128)(2,1)S(1)}, u32[]{:S(2)}) copy-start(bf16[4,4,384,128]{3,2,1,0:T(8,128)(2,1)S(1)} %all-to-all-done.2.in_ref) | copy-start | bytes 4718596
  65.0 48.6 %all-to-all-start = ((bf16[4,4,384,128]{3,2,1,0:T(8,128)(2,1)}), bf16[4,4,384,128]{3,2,1,0:T(8,128)(2,1)S(1)}, u32[]{:S(2)}, u32[]{:S(2)}) async-start(bf16[4,4,384,128]{3,2,1,0:T(8,128)(2,1)} %repack.3), calls=%async_computation | async-start | bytes 3145728 | tf_op jit(solution)/shard_map/all_to_all | solution.py:331
  68.5 37.7 %collective-permute-start.4 = (bf16[4,384,128]{2,1,0:T(8,128)(2,1)}, bf16[4,384,128]{2,1,0:T(8,128)(2,1)S(1)}, u32[]{:S(2)}, u32[]{:S(2)}) collective-permute-start(bf16[4,384,128]{2,1,0:T(8,128)(2,1)} %get-tuple-element.36), channel_id=1, source_target_pairs={{0,8},{1,9},{2,10},{3,11},{4,12},{5,13},{6,14},{7,15},{8,0},{9,1},... | collective-permute-start | bytes 1179656 | tf_op jit(solution)/shard_map/ppermute | solution.py:283
  79.1 27.1 %collective-permute-start.5 = (bf16[4,384,128]{2,1,0:T(8,128)(2,1)}, bf16[4,384,128]{2,1,0:T(8,128)(2,1)}, u32[]{:S(2)}, u32[]{:S(2)}) collective-permute-start(bf16[4,384,128]{2,1,0:T(8,128)(2,1)} %get-tuple-element.37), channel_id=1, source_target_pairs={{0,12},{1,13},{2,14},{3,15},{4,8},{5,9},{6,10},{7,11},{8,4},{9,5},... | collective-permute-start | bytes 1179656 | tf_op jit(solution)/shard_map/ppermute | solution.py:283
  82.6 27.7 %collective-permute-start.6 = (bf16[4,384,128]{2,1,0:T(8,128)(2,1)}, bf16[4,384,128]{2,1,0:T(8,128)(2,1)S(1)}, u32[]{:S(2)}, u32[]{:S(2)}) collective-permute-start(bf16[4,384,128]{2,1,0:T(8,128)(2,1)} %get-tuple-element.38), channel_id=1, source_target_pairs={{0,4},{1,5},{2,6},{3,7},{4,0},{5,1},{6,2},{7,3},{8,12},{9,13},{10,... | collective-permute-start | bytes 1179656 | tf_op jit(solution)/shard_map/ppermute | solution.py:283
  106.2 4.0 %copy-start.17 = (bf16[4,384,128]{2,1,0:T(8,128)(2,1)}, bf16[4,384,128]{2,1,0:T(8,128)(2,1)S(1)}, u32[]{:S(2)}) copy-start(bf16[4,384,128]{2,1,0:T(8,128)(2,1)S(1)} %collective-permute-done.4.refs_2_) | copy-start | bytes 1179652
  110.2 0.8 copy-start.12
  113.6 26.1 %all-to-all-start.3 = ((bf16[4,4,384,128]{3,2,1,0:T(8,128)(2,1)}), bf16[4,4,384,128]{3,2,1,0:T(8,128)(2,1)S(1)}, u32[]{:S(2)}, u32[]{:S(2)}) async-start(bf16[4,4,384,128]{3,2,1,0:T(8,128)(2,1)} %repack.4), calls=%async_computation.3 | async-start | bytes 3145728 | tf_op jit(solution)/shard_map/all_to_all | solution.py:331
  117.2 31.0 %collective-permute-start.7 = (bf16[4,384,128]{2,1,0:T(8,128)(2,1)}, bf16[4,384,128]{2,1,0:T(8,128)(2,1)}, u32[]{:S(2)}, u32[]{:S(2)}) collective-permute-start(bf16[4,384,128]{2,1,0:T(8,128)(2,1)} %get-tuple-element.41), channel_id=1, source_target_pairs={{0,8},{1,9},{2,10},{3,11},{4,12},{5,13},{6,14},{7,15},{8,0},{9,1},... | collective-permute-start | bytes 1179656 | tf_op jit(solution)/shard_map/ppermute | solution.py:283
  121.0 27.2 %collective-permute-start.8 = (bf16[4,384,128]{2,1,0:T(8,128)(2,1)}, bf16[4,384,128]{2,1,0:T(8,128)(2,1)}, u32[]{:S(2)}, u32[]{:S(2)}) collective-permute-start(bf16[4,384,128]{2,1,0:T(8,128)(2,1)} %get-tuple-element.42), channel_id=1, source_target_pairs={{0,12},{1,13},{2,14},{3,15},{4,8},{5,9},{6,10},{7,11},{8,4},{9,5},... | collective-permute-start | bytes 1179656 | tf_op jit(solution)/shard_map/ppermute | solution.py:283
  124.4 25.9 %collective-permute-start.9 = (bf16[4,384,128]{2,1,0:T(8,128)(2,1)}, bf16[4,384,128]{2,1,0:T(8,128)(2,1)S(1)}, u32[]{:S(2)}, u32[]{:S(2)}) collective-permute-start(bf16[4,384,128]{2,1,0:T(8,128)(2,1)} %get-tuple-element.43), channel_id=1, source_target_pairs={{0,4},{1,5},{2,6},{3,7},{4,0},{5,1},{6,2},{7,3},{8,12},{9,13},{10,... | collective-permute-start | bytes 1179656 | tf_op jit(solution)/shard_map/ppermute | solution.py:283
  139.7 32.4 %all-to-all-start.1 = ((bf16[16,128,128]{2,1,0:T(8,128)(2,1)}), bf16[16,128,128]{2,1,0:T(8,128)(2,1)S(1)}, u32[]{:S(2)}, u32[]{:S(2)}) async-start(bf16[16,128,128]{2,1,0:T(8,128)(2,1)} %attend.4.refs_4_.refs_1_), calls=%async_computation.1 | async-start | bytes 1048576 | tf_op jit(solution)/shard_map/all_to_all | solution.py:350
  150.3 0.8 copy-start.2
  153.7 40.3 %collective-permute-start.11 = (bf16[4,384,128]{2,1,0:T(8,128)(2,1)}, bf16[4,384,128]{2,1,0:T(8,128)(2,1)S(1)}, u32[]{:S(2)}, u32[]{:S(2)}) collective-permute-start(bf16[4,384,128]{2,1,0:T(8,128)(2,1)} %get-tuple-element.47), channel_id=1, source_target_pairs={{0,1},{1,0},{2,3},{3,2},{4,5},{5,4},{6,7},{7,6},{8,9},{9,8},{10,11... | collective-permute-start | bytes 1179656 | tf_op jit(solution)/shard_map/ppermute | solution.py:283
  153.7 40.3 %collective-permute-start.12 = (bf16[4,384,128]{2,1,0:T(8,128)(2,1)}, bf16[4,384,128]{2,1,0:T(8,128)(2,1)S(1)}, u32[]{:S(2)}, u32[]{:S(2)}) collective-permute-start(bf16[4,384,128]{2,1,0:T(8,128)(2,1)} %get-tuple-element.48), channel_id=1, source_target_pairs={{0,2},{1,3},{2,0},{3,1},{4,6},{5,7},{6,4},{7,5},{8,10},{9,11},{10,... | collective-permute-start | bytes 1179656 | tf_op jit(solution)/shard_map/ppermute | solution.py:283
  155.6 38.3 %collective-permute-start.13 = (bf16[4,384,128]{2,1,0:T(8,128)(2,1)}, bf16[4,384,128]{2,1,0:T(8,128)(2,1)}, u32[]{:S(2)}, u32[]{:S(2)}) collective-permute-start(bf16[4,384,128]{2,1,0:T(8,128)(2,1)} %get-tuple-element.49), channel_id=1, source_target_pairs={{0,3},{1,2},{2,1},{3,0},{4,7},{5,6},{6,5},{7,4},{8,11},{9,10},{10,... | collective-permute-start | bytes 1179656 | tf_op jit(solution)/shard_map/ppermute | solution.py:283
  155.8 1.0 copy-start.4
  156.8 37.2 %copy-start.5 = (bf16[4,384,128]{2,1,0:T(8,128)(2,1)S(1)}, bf16[4,384,128]{2,1,0:T(8,128)(2,1)}, u32[]{:S(2)}) copy-start(bf16[4,384,128]{2,1,0:T(8,128)(2,1)} %get-tuple-element.44.refs_2_.refs_0_) | copy-start | bytes 1179652
  172.1 16.8 %copy-start.7 = (bf16[16,128,128]{2,1,0:T(8,128)(2,1)}, bf16[16,128,128]{2,1,0:T(8,128)(2,1)S(1)}, u32[]{:S(2)}) copy-start(bf16[16,128,128]{2,1,0:T(8,128)(2,1)S(1)} %all-to-all-done.1) | copy-start | bytes 1572868
  172.1 38.2 %all-to-all-start.4 = ((bf16[16,128,128]{2,1,0:T(8,128)(2,1)}), bf16[16,128,128]{2,1,0:T(8,128)(2,1)S(1)}, u32[]{:S(2)}, u32[]{:S(2)}) async-start(bf16[16,128,128]{2,1,0:T(8,128)(2,1)} %attend.5.refs_4_), calls=%async_computation.4 | async-start | bytes 1048576 | tf_op jit(solution)/shard_map/all_to_all | solution.py:350
  188.8 43.6 %all-gather.7.cloned.1.call-start = ((), (), s32[]{:S(2)}) async-start(), calls=%async_computation.8 | async-start | bytes 1572864 | tf_op jit(solution)/shard_map/all_gather | solution.py:353
  189.6 42.9 %collective-permute-start.15 = (bf16[4,384,128]{2,1,0:T(8,128)(2,1)}, bf16[4,384,128]{2,1,0:T(8,128)(2,1)S(1)}, u32[]{:S(2)}, u32[]{:S(2)}) collective-permute-start(bf16[4,384,128]{2,1,0:T(8,128)(2,1)} %get-tuple-element.52), channel_id=1, source_target_pairs={{0,8},{1,9},{2,10},{3,11},{4,12},{5,13},{6,14},{7,15},{8,0},{9,1},... | collective-permute-start | bytes 1179656 | tf_op jit(solution)/shard_map/ppermute | solution.py:283
  192.5 40.0 %copy-start.1 = (bf16[4,384,128]{2,1,0:T(8,128)(2,1)S(1)}, bf16[4,384,128]{2,1,0:T(8,128)(2,1)}, u32[]{:S(2)}) copy-start(bf16[4,384,128]{2,1,0:T(8,128)(2,1)} %get-tuple-element.39.refs_5_.refs_0_) | copy-start | bytes 1179652
  192.5 40.0 %copy-start.3 = (bf16[4,384,128]{2,1,0:T(8,128)(2,1)S(1)}, bf16[4,384,128]{2,1,0:T(8,128)(2,1)}, u32[]{:S(2)}) copy-start(bf16[4,384,128]{2,1,0:T(8,128)(2,1)} %copy-done.2) | copy-start | bytes 1179652
  192.5 40.0 %collective-permute-start.16 = (bf16[4,384,128]{2,1,0:T(8,128)(2,1)}, bf16[4,384,128]{2,1,0:T(8,128)(2,1)S(1)}, u32[]{:S(2)}, u32[]{:S(2)}) collective-permute-start(bf16[4,384,128]{2,1,0:T(8,128)(2,1)} %get-tuple-element.53), channel_id=1, source_target_pairs={{0,12},{1,13},{2,14},{3,15},{4,8},{5,9},{6,10},{7,11},{8,4},{9,5},... | collective-permute-start | bytes 1179656 | tf_op jit(solution)/shard_map/ppermute | solution.py:283
  210.3 53.0 %copy-start.8 = (bf16[16,128,128]{2,1,0:T(8,128)(2,1)}, bf16[16,128,128]{2,1,0:T(8,128)(2,1)S(1)}, u32[]{:S(2)}) copy-start(bf16[16,128,128]{2,1,0:T(8,128)(2,1)S(1)} %all-to-all-done.4) | copy-start | bytes 1572868
  210.4 38.7 %all-to-all-start.5 = ((bf16[16,128,128]{2,1,0:T(8,128)(2,1)}), bf16[16,128,128]{2,1,0:T(8,128)(2,1)S(1)}, u32[]{:S(2)}, u32[]{:S(2)}) async-start(bf16[16,128,128]{2,1,0:T(8,128)(2,1)} %attend.6.refs_4_), calls=%async_computation.5 | async-start | bytes 1048576 | tf_op jit(solution)/shard_map/all_to_all | solution.py:350
  232.5 1.2 copy-start
  249.1 34.7 %copy-start.9 = (bf16[16,128,128]{2,1,0:T(8,128)(2,1)}, bf16[16,128,128]{2,1,0:T(8,128)(2,1)S(1)}, u32[]{:S(2)}) copy-start(bf16[16,128,128]{2,1,0:T(8,128)(2,1)S(1)} %all-to-all-done.5) | copy-start | bytes 1572868
  249.1 28.8 %all-to-all-start.6 = ((bf16[16,128,128]{2,1,0:T(8,128)(2,1)}), bf16[16,128,128]{2,1,0:T(8,128)(2,1)S(1)}, u32[]{:S(2)}, u32[]{:S(2)}) async-start(bf16[16,128,128]{2,1,0:T(8,128)(2,1)} %attend.7), calls=%async_computation.6 | async-start | bytes 1048576 | tf_op jit(solution)/shard_map/all_to_all | solution.py:350
  263.4 20.4 %collective-permute-start.10 = (bf16[1,16,128,128]{3,2,1,0:T(8,128)(2,1)S(1)}, bf16[1,16,128,128]{3,2,1,0:T(8,128)(2,1)S(1)}, u32[]{:S(2)}, u32[]{:S(2)}) collective-permute-start(bf16[1,16,128,128]{3,2,1,0:T(8,128)(2,1)S(1)} %bitcast.20), channel_id=1, source_target_pairs={{0,16},{16,0},{1,17},{17,1},{2,18},{18,2},{3,19},{19,3},{4,20},{20... | collective-permute-start | bytes 1572872 | tf_op jit(solution)/shard_map/ppermute | solution.py:283
  265.0 24.4 %collective-permute-start.14 = (bf16[1,16,128,128]{3,2,1,0:T(8,128)(2,1)S(1)}, bf16[1,16,128,128]{3,2,1,0:T(8,128)(2,1)S(1)}, u32[]{:S(2)}, u32[]{:S(2)}) collective-permute-start(bf16[1,16,128,128]{3,2,1,0:T(8,128)(2,1)S(1)} %bitcast.22), channel_id=1, source_target_pairs={{0,16},{16,0},{1,17},{17,1},{2,18},{18,2},{3,19},{19,3},{4,20},{20... | collective-permute-start | bytes 1572872 | tf_op jit(solution)/shard_map/ppermute | solution.py:283
  277.8 5.9 %copy-start.10 = (bf16[16,128,128]{2,1,0:T(8,128)(2,1)}, bf16[16,128,128]{2,1,0:T(8,128)(2,1)S(1)}, u32[]{:S(2)}) copy-start(bf16[16,128,128]{2,1,0:T(8,128)(2,1)S(1)} %all-to-all-done.6) | copy-start | bytes 1572868
  277.8 22.3 %collective-permute-start.17 = (bf16[1,16,128,128]{3,2,1,0:T(8,128)(2,1)S(1)}, bf16[1,16,128,128]{3,2,1,0:T(8,128)(2,1)S(1)}, u32[]{:S(2)}, u32[]{:S(2)}) collective-permute-start(bf16[1,16,128,128]{3,2,1,0:T(8,128)(2,1)S(1)} %bitcast.24), channel_id=1, source_target_pairs={{0,16},{16,0},{1,17},{17,1},{2,18},{18,2},{3,19},{19,3},{4,20},{20... | collective-permute-start | bytes 1572872 | tf_op jit(solution)/shard_map/ppermute | solution.py:283
  283.8 0.8 copy-start.16
  289.4 0.8 copy-start.15
  300.2 0.8 copy-start.14
Sparse Core Ops, SparseCore 0:
  9.5 59.4 all-gather.4
  191.2 22.6 all-gather.6

commit v5 on v3

--- a/solution.py
+++ b/solution.py
@@ -298,7 +298,7 @@
             arrive(c + 1, attended)
         returned = exchange(attended[0])
         own = returned[None]
-        if c + 2 < chunks:
+        if c == 0 and chunks > 2:
             outputs = [own] + [lax.all_gather(returned, "view")] * (views - 1)
         else:
             outputs = swap([own] * views, "view", views, 1)

time: 307 us -> 313 us (1.020)
  waiting for transfers between devices: 99.1 us -> 104 us
    all_gather x2 -> x1, waiting for transfers between devices: 15.1 us -> 20.4 us  [local(): outputs = [own] + [lax.all_gather(returned, 'view')] * (views - 1)]
    unnamed x44 -> x46, local copies, waits for them, and re-layouts: 11.5 us -> 12.2 us
    ppermute x20 -> x21, waiting for transfers between devices: 69.8 us -> 70.6 us  [swap(): lax.ppermute(blocks[shift], axis, [(i, i ^ shift * stride) for i in range...]
    ppermute x20 -> x21, starting transfers between devices: 40.1 us -> 40.6 us  [swap(): lax.ppermute(blocks[shift], axis, [(i, i ^ shift * stride) for i in range...]
  transfers between devices with their start and end apart: 29 -> 29, of which waited for: 8 -> 8; matrix products, arithmetic and copies ran while one was open for 0% -> 0% of each run, Pallas kernels for 32% -> 31%
where the time goes in v5:
time: 313 us; the launch traced here: 311 us
  waiting for transfers between devices  104 us (33%)
  Pallas kernels  101 us (32%)
  starting transfers between devices  79.6 us (25%)
  between operations  14.2 us (5%)
  local copies, waits for them, and re-layouts  12.2 us (4%)
    ppermute x21, waiting for transfers between devices, swap(): lax.ppermute(blocks[shift], axis, [(i, i ^ shift * stride) for i in range...  70.6 us
    pallas_call x4, Pallas kernels, attend(): pl.pallas_call(functools.partial(attend_kernel, group, rows, parts, split...  61.4 us
    ppermute x21, starting transfers between devices, swap(): lax.ppermute(blocks[shift], axis, [(i, i ^ shift * stride) for i in range...  40.6 us
    all_to_all x4, starting transfers between devices, local(): returned = exchange(attended[0])  31.9 us
    all_gather x1, waiting for transfers between devices, local(): outputs = [own] + [lax.all_gather(returned, 'view')] * (views - 1)  20.4 us
    pallas_call x4, Pallas kernels, combine(): pl.pallas_call(functools.partial(combine_kernel, views, group, carried),...  17.6 us
    unnamed x46, local copies, waits for them, and re-layouts  12.2 us
    pallas_call x4, Pallas kernels, pack(): pl.pallas_call(functools.partial(pack_kernel, near, per_chunk, rows, len(...  11.9 us
  transfers between devices with their start and end apart: 29, of which 8 were waited for; matrix products, arithmetic and copies ran while one was open for 0% of the time, Pallas kernels for 31%

profile of v5, /device:TPU:0, one launch (start us, length us, event | category | flops | bytes accessed | tf_op | source)
XLA Modules:
  0.0 311.5 jit_solution(8923676993863441769)
XLA Ops:
  7.2 0.7 all-gather.5.cloned.1.call-update
  7.9 2.9 pack.4
  10.8 3.0 collective-permute-start
  13.8 2.6 collective-permute-start.1
  16.4 14.4 %collective-permute-done.refs_1_ = bf16[4,384,128]{2,1,0:T(8,128)(2,1)S(1)} collective-permute-done((bf16[4,384,128]{2,1,0:T(8,128)(2,1)}, bf16[4,384,128]{2,1,0:T(8,128)(2,1)S(1)}, u32[]{:S(2)}, u32[]{:S(2)}) %collective-permute-start) | collective-permute-done | bytes 393248 | tf_op jit(solution)/shard_map/ppermute | solution.py:254
  30.8 13.0 %collective-permute-done.1.refs_2_ = bf16[4,384,128]{2,1,0:T(8,128)(2,1)S(1)} collective-permute-done((bf16[4,384,128]{2,1,0:T(8,128)(2,1)}, bf16[4,384,128]{2,1,0:T(8,128)(2,1)S(1)}, u32[]{:S(2)}, u32[]{:S(2)}) %collective-permute-start.1) | collective-permute-done | bytes 393248 | tf_op jit(solution)/shard_map/ppermute | solution.py:254
  43.8 0.7 copy-done.21
  44.6 0.1 copy-done.22
  44.7 2.6 repack.4.refs_4_
  47.3 3.6 %all-to-all-start = ((bf16[4,4,384,128]{3,2,1,0:T(8,128)(2,1)}), bf16[4,4,384,128]{3,2,1,0:T(8,128)(2,1)S(1)}, u32[]{:S(2)}, u32[]{:S(2)}) async-start(bf16[4,4,384,128]{3,2,1,0:T(8,128)(2,1)} %repack.4.refs_4_), calls=%async_computation | async-start | bytes 3145728 | tf_op jit(solution)/shard_map/all_to_all | solution.py:283
  50.9 2.9 pack.5
  53.8 7.4 %collective-permute-start.3 = (bf16[4,384,128]{2,1,0:T(8,128)(2,1)}, bf16[4,384,128]{2,1,0:T(8,128)(2,1)S(1)}, u32[]{:S(2)}, u32[]{:S(2)}) collective-permute-start(bf16[4,384,128]{2,1,0:T(8,128)(2,1)} %get-tuple-element.36), channel_id=1, source_target_pairs={{0,4},{1,5},{2,6},{3,7},{4,0},{5,1},{6,2},{7,3},{8,12},{9,13},{10,... | collective-permute-start | bytes 1179656 | tf_op jit(solution)/shard_map/ppermute | solution.py:254
  61.3 1.0 collective-permute-start.4
  62.3 1.5 collective-permute-start.5
  63.7 15.5 %collective-permute-done.3.refs_1_ = bf16[4,384,128]{2,1,0:T(8,128)(2,1)S(1)} collective-permute-done((bf16[4,384,128]{2,1,0:T(8,128)(2,1)}, bf16[4,384,128]{2,1,0:T(8,128)(2,1)S(1)}, u32[]{:S(2)}, u32[]{:S(2)}) %collective-permute-start.3) | collective-permute-done | bytes 393248 | tf_op jit(solution)/shard_map/ppermute | solution.py:254
  79.2 12.0 %collective-permute-done.4.refs_2_ = bf16[4,384,128]{2,1,0:T(8,128)(2,1)S(1)} collective-permute-done((bf16[4,384,128]{2,1,0:T(8,128)(2,1)}, bf16[4,384,128]{2,1,0:T(8,128)(2,1)S(1)}, u32[]{:S(2)}, u32[]{:S(2)}) %collective-permute-start.4) | collective-permute-done | bytes 393248 | tf_op jit(solution)/shard_map/ppermute | solution.py:254
  91.2 0.7 copy-done.18
  92.1 2.6 repack.5.refs_2_
  94.7 1.1 copy-done.1
  95.9 3.6 %all-to-all-start.2 = ((bf16[4,4,384,128]{3,2,1,0:T(8,128)(2,1)}), bf16[4,4,384,128]{3,2,1,0:T(8,128)(2,1)S(1)}, u32[]{:S(2)}, u32[]{:S(2)}) async-start(bf16[4,4,384,128]{3,2,1,0:T(8,128)(2,1)} %repack.5.refs_2_), calls=%async_computation.2 | async-start | bytes 3145728 | tf_op jit(solution)/shard_map/all_to_all | solution.py:283
  99.4 3.1 pack.6
  102.5 8.1 %collective-permute-start.6 = (bf16[4,384,128]{2,1,0:T(8,128)(2,1)}, bf16[4,384,128]{2,1,0:T(8,128)(2,1)S(1)}, u32[]{:S(2)}, u32[]{:S(2)}) collective-permute-start(bf16[4,384,128]{2,1,0:T(8,128)(2,1)} %get-tuple-element.42), channel_id=1, source_target_pairs={{0,4},{1,5},{2,6},{3,7},{4,0},{5,1},{6,2},{7,3},{8,12},{9,13},{10,... | collective-permute-start | bytes 1179656 | tf_op jit(solution)/shard_map/ppermute | solution.py:254
  110.6 1.0 collective-permute-start.7
  111.6 1.5 collective-permute-start.8
  113.1 1.4 copy-done.2
  114.5 1.0 copy-done.7
  115.5 15.3 %attend.4.refs_4_.refs_1_ = bf16[16,128,128]{2,1,0:T(8,128)(2,1)} custom-call(s32[1]{0:T(128)} %bitcast.2.me_ref, bf16[4,4,384,128]{3,2,1,0:T(8,128)(2,1)S(1)} %copy-done.2, bf16[4,384,128]{2,1,0:T(8,128)(2,1)S(1)} %copy-done.7, bf16[4,4,384,128]{3,2,1,0:T(8,128)(2,1)S(1)} %copy-done), custom_call_target="tpu_custom_call" | custom-call | flops 8589934592 | bytes 2097152 | tf_op jit(solution)/shard_map/attend/pallas_call | solution.py:143
  130.8 5.2 %all-to-all-start.1 = ((bf16[16,128,128]{2,1,0:T(8,128)(2,1)}), bf16[16,128,128]{2,1,0:T(8,128)(2,1)}, u32[]{:S(2)}, u32[]{:S(2)}) async-start(bf16[16,128,128]{2,1,0:T(8,128)(2,1)} %attend.4.refs_4_.refs_1_), calls=%async_computation.1 | async-start | bytes 1048576 | tf_op jit(solution)/shard_map/all_to_all | solution.py:299
  136.0 2.9 pack.7
  139.0 1.9 collective-permute-start.13
  140.9 2.4 collective-permute-start.15
  143.2 0.7 copy-done.4
  144.0 2.6 repack.6
  146.6 1.5 collective-permute-start.11
  148.1 0.4 collective-permute-start.12
  148.5 1.0 copy-done.5
  149.5 1.0 copy-done.8
  150.4 15.3 %attend.5.refs_4_ = bf16[16,128,128]{2,1,0:T(8,128)(2,1)} custom-call(s32[1]{0:T(128)} %bitcast.2.me_ref, bf16[4,4,384,128]{3,2,1,0:T(8,128)(2,1)S(1)} %all-to-all-done.2.refs_0_, bf16[16,128,128]{2,1,0:T(8,128)(2,1)} %attend.4.refs_4_.refs_1_, bf16[4,384,128]{2,1,0:T(8,128)(2,1)S(1)} %copy-done.5, bf16[4,384,128]{2,1,0:T(8,128)(2,1)S(1)} %copy-done.8, ...), custom_call_target="tpu_custom_call" | custom-call | flops 8589934592 | bytes 2097152 | tf_op jit(solution)/shard_map/attend/pallas_call | solution.py:143
  165.8 2.7 collective-permute-start.16
  168.5 13.0 %all-to-all-start.3 = ((bf16[16,128,128]{2,1,0:T(8,128)(2,1)}), bf16[16,128,128]{2,1,0:T(8,128)(2,1)S(1)}, u32[]{:S(2)}, u32[]{:S(2)}) async-start(bf16[16,128,128]{2,1,0:T(8,128)(2,1)} %attend.5.refs_4_), calls=%async_computation.3 | async-start | bytes 1048576 | tf_op jit(solution)/shard_map/all_to_all | solution.py:299
  181.5 15.4 %attend.6.refs_4_ = bf16[16,128,128]{2,1,0:T(8,128)(2,1)} custom-call(s32[1]{0:T(128)} %bitcast.2.me_ref, bf16[4,384,128]{2,1,0:T(8,128)(2,1)S(1)} %copy-done.9, bf16[4,384,128]{2,1,0:T(8,128)(2,1)S(1)} %collective-permute-done.10.refs_1_, bf16[4,384,128]{2,1,0:T(8,128)(2,1)S(1)} %collective-permute-done.11.refs_2_, ...), custom_call_target="tpu_custom_call" | custom-call | flops 8589934592 | bytes 2097152 | tf_op jit(solution)/shard_map/attend/pallas_call | solution.py:143
  196.9 0.8 copy-done.17
  197.7 2.6 repack.7
  200.3 0.4 collective-permute-start.17
  200.7 1.7 collective-permute-start.18
  202.4 6.8 %all-to-all-start.4 = ((bf16[16,128,128]{2,1,0:T(8,128)(2,1)}), bf16[16,128,128]{2,1,0:T(8,128)(2,1)S(1)}, u32[]{:S(2)}, u32[]{:S(2)}) async-start(bf16[16,128,128]{2,1,0:T(8,128)(2,1)} %attend.6.refs_4_), calls=%async_computation.4 | async-start | bytes 1048576 | tf_op jit(solution)/shard_map/all_to_all | solution.py:299
  209.2 3.7 %collective-permute-done.18.refs_2_ = bf16[4,384,128]{2,1,0:T(8,128)(2,1)S(1)} collective-permute-done((bf16[4,384,128]{2,1,0:T(8,128)(2,1)}, bf16[4,384,128]{2,1,0:T(8,128)(2,1)S(1)}, u32[]{:S(2)}, u32[]{:S(2)}) %collective-permute-start.18) | collective-permute-done | bytes 393248 | tf_op jit(solution)/shard_map/ppermute | solution.py:254
  212.9 12.0 %collective-permute-done.19.refs_3_ = bf16[4,384,128]{2,1,0:T(8,128)(2,1)S(1)} collective-permute-done((bf16[4,384,128]{2,1,0:T(8,128)(2,1)}, bf16[4,384,128]{2,1,0:T(8,128)(2,1)S(1)}, u32[]{:S(2)}, u32[]{:S(2)}) %collective-permute-start.19) | collective-permute-done | bytes 393248 | tf_op jit(solution)/shard_map/ppermute | solution.py:254
  224.9 1.0 copy-done.10
  225.9 15.3 %attend.7 = bf16[16,128,128]{2,1,0:T(8,128)(2,1)} custom-call(s32[1]{0:T(128)} %bitcast.2.me_ref, bf16[4,384,128]{2,1,0:T(8,128)(2,1)S(1)} %copy-done.10, bf16[4,384,128]{2,1,0:T(8,128)(2,1)S(1)} %collective-permute-done.17.refs_1_, bf16[4,384,128]{2,1,0:T(8,128)(2,1)S(1)} %collective-permute-done.18.refs_2_, ...), custom_call_target="tpu_custom_call" | custom-call | flops 8589934592 | bytes 2097152 | tf_op jit(solution)/shard_map/attend/pallas_call | solution.py:143
  241.2 6.9 %all-to-all-start.5 = ((bf16[16,128,128]{2,1,0:T(8,128)(2,1)}), bf16[16,128,128]{2,1,0:T(8,128)(2,1)S(1)}, u32[]{:S(2)}, u32[]{:S(2)}) async-start(bf16[16,128,128]{2,1,0:T(8,128)(2,1)} %attend.7), calls=%async_computation.5 | async-start | bytes 1048576 | tf_op jit(solution)/shard_map/all_to_all | solution.py:299
  248.2 0.7 all-gather.7.cloned.1.call-update
  248.9 1.6 collective-permute-start.9
  250.5 0.5 collective-permute-start.14
  251.0 11.6 %all-to-all-done.5 = bf16[16,128,128]{2,1,0:T(8,128)(2,1)S(1)} async-done(((bf16[16,128,128]{2,1,0:T(8,128)(2,1)}), bf16[16,128,128]{2,1,0:T(8,128)(2,1)S(1)}, u32[]{:S(2)}, u32[]{:S(2)}) %all-to-all-start.5) | async-done | bytes 524320 | tf_op jit(solution)/shard_map/all_to_all | solution.py:299
  262.6 1.5 collective-permute-start.20
  264.1 20.4 %all-gather.7.cloned.1.call-done = bf16[32,128,128]{2,1,0:T(8,128)(2,1)} async-done(((bf16[16,128,128]{2,1,0:T(8,128)(2,1)}), bf16[32,128,128]{2,1,0:T(8,128)(2,1)}) %all-gather.7.cloned.1.call-update) | async-done | bytes 1048592 | tf_op jit(solution)/shard_map/all_gather | solution.py:302
  284.6 4.4 %combine.4 = (bf16[4,1,128,2048]{3,2,1,0:T(8,128)(2,1)}, bf16[4,1,128,2048]{3,2,1,0:T(8,128)(2,1)}) custom-call(s32[1]{0:T(128)} %bitcast.view_ref, bf16[4,1,128,2048]{3,2,1,0:T(8,128)(2,1)} %refs_2_.13, bf16[2,4,1,128,2048]{4,3,2,1,0:T(8,128)(2,1)} %bitcast.9, bf16[2,4,1,128,2048]{4,3,2,1,0:T(8,128)(2,1)} %bitcast.10, ...), custom_call_target="tpu_custom_call" | custom-call | flops 536870912 | bytes 3670016 | tf_op jit(solution)/shard_map/combine/pallas_call | solution.py:229
  289.0 0.8 copy-done.16
  289.8 4.4 %combine.5 = (bf16[4,1,128,2048]{3,2,1,0:T(8,128)(2,1)}, bf16[4,1,128,2048]{3,2,1,0:T(8,128)(2,1)}) custom-call(s32[1]{0:T(128)} %bitcast.view_ref, bf16[4,1,128,2048]{3,2,1,0:T(8,128)(2,1)} %get-tuple-element.40.refs_0_, bf16[4,1,128,2048]{3,2,1,0:T(8,128)(2,1)} %get-tuple-element.41.refs_1_, ...), custom_call_target="tpu_custom_call", output_to_operand_aliasing={{0}: (1, {}), {1}: (2, {})} | custom-call | flops 536870912 | bytes 3670016 | tf_op jit(solution)/shard_map/combine/pallas_call | solution.py:229
  294.2 0.8 copy-done.15
  295.0 4.4 %combine.6 = (bf16[4,1,128,2048]{3,2,1,0:T(8,128)(2,1)}, bf16[4,1,128,2048]{3,2,1,0:T(8,128)(2,1)}) custom-call(s32[1]{0:T(128)} %bitcast.view_ref, bf16[4,1,128,2048]{3,2,1,0:T(8,128)(2,1)} %get-tuple-element.47.refs_0_, bf16[4,1,128,2048]{3,2,1,0:T(8,128)(2,1)} %get-tuple-element.48.refs_1_, ...), custom_call_target="tpu_custom_call", output_to_operand_aliasing={{0}: (1, {}), {1}: (2, {})} | custom-call | flops 536870912 | bytes 3670016 | tf_op jit(solution)/shard_map/combine/pallas_call | solution.py:229
  299.4 0.8 copy-done.14
  300.2 4.4 %combine.7 = (bf16[4,1,128,2048]{3,2,1,0:T(8,128)(2,1)}, bf16[4,1,128,2048]{3,2,1,0:T(8,128)(2,1)}) custom-call(s32[1]{0:T(128)} %bitcast.view_ref, bf16[4,1,128,2048]{3,2,1,0:T(8,128)(2,1)} %get-tuple-element.53.refs_0_, bf16[4,1,128,2048]{3,2,1,0:T(8,128)(2,1)} %get-tuple-element.54.refs_1_, ...), custom_call_target="tpu_custom_call", output_to_operand_aliasing={{0}: (1, {}), {1}: (2, {})} | custom-call | flops 536870912 | bytes 3670016 | tf_op jit(solution)/shard_map/combine/pallas_call | solution.py:229
  (58 shorter events, 0.3 us)
Async XLA Ops:
  7.2 141.3 %all-gather.5.cloned.1.call-start = ((), (), s32[]{:S(2)}) async-start(), calls=%async_computation.6 | async-start | bytes 6291456 | tf_op jit(solution)/shard_map/all_gather | solution.py:271
  10.8 20.0 %collective-permute-start = (bf16[4,384,128]{2,1,0:T(8,128)(2,1)}, bf16[4,384,128]{2,1,0:T(8,128)(2,1)S(1)}, u32[]{:S(2)}, u32[]{:S(2)}) collective-permute-start(bf16[4,384,128]{2,1,0:T(8,128)(2,1)} %get-tuple-element.33), channel_id=1, source_target_pairs={{0,4},{1,5},{2,6},{3,7},{4,0},{5,1},{6,2},{7,3},{8,12},{9,13},{10,... | collective-permute-start | bytes 1179656 | tf_op jit(solution)/shard_map/ppermute | solution.py:254
  13.8 30.0 %collective-permute-start.1 = (bf16[4,384,128]{2,1,0:T(8,128)(2,1)}, bf16[4,384,128]{2,1,0:T(8,128)(2,1)S(1)}, u32[]{:S(2)}, u32[]{:S(2)}) collective-permute-start(bf16[4,384,128]{2,1,0:T(8,128)(2,1)} %get-tuple-element.34), channel_id=1, source_target_pairs={{0,8},{1,9},{2,10},{3,11},{4,12},{5,13},{6,14},{7,15},{8,0},{9,1},... | collective-permute-start | bytes 1179656 | tf_op jit(solution)/shard_map/ppermute | solution.py:254
  16.4 27.4 %collective-permute-start.2 = (bf16[4,384,128]{2,1,0:T(8,128)(2,1)}, bf16[4,384,128]{2,1,0:T(8,128)(2,1)S(1)}, u32[]{:S(2)}, u32[]{:S(2)}) collective-permute-start(bf16[4,384,128]{2,1,0:T(8,128)(2,1)} %get-tuple-element.35), channel_id=1, source_target_pairs={{0,12},{1,13},{2,14},{3,15},{4,8},{5,9},{6,10},{7,11},{8,4},{9,5},... | collective-permute-start | bytes 1179656 | tf_op jit(solution)/shard_map/ppermute | solution.py:254
  30.8 13.0 %copy-start.20 = (bf16[4,384,128]{2,1,0:T(8,128)(2,1)}, bf16[4,384,128]{2,1,0:T(8,128)(2,1)S(1)}, u32[]{:S(2)}) copy-start(bf16[4,384,128]{2,1,0:T(8,128)(2,1)S(1)} %collective-permute-done.refs_1_) | copy-start | bytes 1179652
  43.8 0.7 copy-start.21
  43.8 0.9 copy-start.22
  47.3 47.4 %all-to-all-start = ((bf16[4,4,384,128]{3,2,1,0:T(8,128)(2,1)}), bf16[4,4,384,128]{3,2,1,0:T(8,128)(2,1)S(1)}, u32[]{:S(2)}, u32[]{:S(2)}) async-start(bf16[4,4,384,128]{3,2,1,0:T(8,128)(2,1)} %repack.4.refs_4_), calls=%async_computation | async-start | bytes 3145728 | tf_op jit(solution)/shard_map/all_to_all | solution.py:283
  53.8 25.4 %collective-permute-start.3 = (bf16[4,384,128]{2,1,0:T(8,128)(2,1)}, bf16[4,384,128]{2,1,0:T(8,128)(2,1)S(1)}, u32[]{:S(2)}, u32[]{:S(2)}) collective-permute-start(bf16[4,384,128]{2,1,0:T(8,128)(2,1)} %get-tuple-element.36), channel_id=1, source_target_pairs={{0,4},{1,5},{2,6},{3,7},{4,0},{5,1},{6,2},{7,3},{8,12},{9,13},{10,... | collective-permute-start | bytes 1179656 | tf_op jit(solution)/shard_map/ppermute | solution.py:254
  61.3 30.0 %collective-permute-start.4 = (bf16[4,384,128]{2,1,0:T(8,128)(2,1)}, bf16[4,384,128]{2,1,0:T(8,128)(2,1)S(1)}, u32[]{:S(2)}, u32[]{:S(2)}) collective-permute-start(bf16[4,384,128]{2,1,0:T(8,128)(2,1)} %get-tuple-element.38), channel_id=1, source_target_pairs={{0,8},{1,9},{2,10},{3,11},{4,12},{5,13},{6,14},{7,15},{8,0},{9,1},... | collective-permute-start | bytes 1179656 | tf_op jit(solution)/shard_map/ppermute | solution.py:254
  62.3 29.0 %collective-permute-start.5 = (bf16[4,384,128]{2,1,0:T(8,128)(2,1)}, bf16[4,384,128]{2,1,0:T(8,128)(2,1)S(1)}, u32[]{:S(2)}, u32[]{:S(2)}) collective-permute-start(bf16[4,384,128]{2,1,0:T(8,128)(2,1)} %get-tuple-element.39), channel_id=1, source_target_pairs={{0,12},{1,13},{2,14},{3,15},{4,8},{5,9},{6,10},{7,11},{8,4},{9,5},... | collective-permute-start | bytes 1179656 | tf_op jit(solution)/shard_map/ppermute | solution.py:254
  79.2 12.0 %copy-start.6 = (bf16[4,384,128]{2,1,0:T(8,128)(2,1)}, bf16[4,384,128]{2,1,0:T(8,128)(2,1)S(1)}, u32[]{:S(2)}) copy-start(bf16[4,384,128]{2,1,0:T(8,128)(2,1)S(1)} %collective-permute-done.3.refs_1_) | copy-start | bytes 1179652
  91.2 0.7 copy-start.18
  91.2 0.9 copy-start.19
  94.7 1.1 copy-start.1
  95.9 35.0 %all-to-all-start.2 = ((bf16[4,4,384,128]{3,2,1,0:T(8,128)(2,1)}), bf16[4,4,384,128]{3,2,1,0:T(8,128)(2,1)S(1)}, u32[]{:S(2)}, u32[]{:S(2)}) async-start(bf16[4,4,384,128]{3,2,1,0:T(8,128)(2,1)} %repack.5.refs_2_), calls=%async_computation.2 | async-start | bytes 3145728 | tf_op jit(solution)/shard_map/all_to_all | solution.py:283
  99.4 13.7 %copy-start = (bf16[4,4,384,128]{3,2,1,0:T(8,128)(2,1)S(1)}, bf16[4,4,384,128]{3,2,1,0:T(8,128)(2,1)}, u32[]{:S(2)}) copy-start(bf16[4,4,384,128]{3,2,1,0:T(8,128)(2,1)} %repack.5.refs_2_) | copy-start | bytes 4718596
  102.5 40.7 %collective-permute-start.6 = (bf16[4,384,128]{2,1,0:T(8,128)(2,1)}, bf16[4,384,128]{2,1,0:T(8,128)(2,1)S(1)}, u32[]{:S(2)}, u32[]{:S(2)}) collective-permute-start(bf16[4,384,128]{2,1,0:T(8,128)(2,1)} %get-tuple-element.42), channel_id=1, source_target_pairs={{0,4},{1,5},{2,6},{3,7},{4,0},{5,1},{6,2},{7,3},{8,12},{9,13},{10,... | collective-permute-start | bytes 1179656 | tf_op jit(solution)/shard_map/ppermute | solution.py:254
  110.6 32.6 %collective-permute-start.7 = (bf16[4,384,128]{2,1,0:T(8,128)(2,1)}, bf16[4,384,128]{2,1,0:T(8,128)(2,1)}, u32[]{:S(2)}, u32[]{:S(2)}) collective-permute-start(bf16[4,384,128]{2,1,0:T(8,128)(2,1)} %get-tuple-element.44), channel_id=1, source_target_pairs={{0,8},{1,9},{2,10},{3,11},{4,12},{5,13},{6,14},{7,15},{8,0},{9,1},... | collective-permute-start | bytes 1179656 | tf_op jit(solution)/shard_map/ppermute | solution.py:254
  111.6 31.6 %collective-permute-start.8 = (bf16[4,384,128]{2,1,0:T(8,128)(2,1)}, bf16[4,384,128]{2,1,0:T(8,128)(2,1)}, u32[]{:S(2)}, u32[]{:S(2)}) collective-permute-start(bf16[4,384,128]{2,1,0:T(8,128)(2,1)} %get-tuple-element.45), channel_id=1, source_target_pairs={{0,12},{1,13},{2,14},{3,15},{4,8},{5,9},{6,10},{7,11},{8,4},{9,5},... | collective-permute-start | bytes 1179656 | tf_op jit(solution)/shard_map/ppermute | solution.py:254
  113.1 1.4 copy-start.2
  114.5 1.0 copy-start.7
  130.8 37.7 %all-to-all-start.1 = ((bf16[16,128,128]{2,1,0:T(8,128)(2,1)}), bf16[16,128,128]{2,1,0:T(8,128)(2,1)}, u32[]{:S(2)}, u32[]{:S(2)}) async-start(bf16[16,128,128]{2,1,0:T(8,128)(2,1)} %attend.4.refs_4_.refs_1_), calls=%async_computation.1 | async-start | bytes 1048576 | tf_op jit(solution)/shard_map/all_to_all | solution.py:299
  139.0 26.8 %collective-permute-start.13 = (bf16[4,384,128]{2,1,0:T(8,128)(2,1)}, bf16[4,384,128]{2,1,0:T(8,128)(2,1)S(1)}, u32[]{:S(2)}, u32[]{:S(2)}) collective-permute-start(bf16[4,384,128]{2,1,0:T(8,128)(2,1)} %get-tuple-element.52), channel_id=1, source_target_pairs={{0,4},{1,5},{2,6},{3,7},{4,0},{5,1},{6,2},{7,3},{8,12},{9,13},{10,... | collective-permute-start | bytes 1179656 | tf_op jit(solution)/shard_map/ppermute | solution.py:254
  140.9 56.1 %collective-permute-start.15 = (bf16[4,384,128]{2,1,0:T(8,128)(2,1)}, bf16[4,384,128]{2,1,0:T(8,128)(2,1)}, u32[]{:S(2)}, u32[]{:S(2)}) collective-permute-start(bf16[4,384,128]{2,1,0:T(8,128)(2,1)} %get-tuple-element.56), channel_id=1, source_target_pairs={{0,8},{1,9},{2,10},{3,11},{4,12},{5,13},{6,14},{7,15},{8,0},{9,1},... | collective-permute-start | bytes 1179656 | tf_op jit(solution)/shard_map/ppermute | solution.py:254
  143.2 0.7 copy-start.4
  146.6 34.9 %collective-permute-start.10 = (bf16[4,384,128]{2,1,0:T(8,128)(2,1)}, bf16[4,384,128]{2,1,0:T(8,128)(2,1)S(1)}, u32[]{:S(2)}, u32[]{:S(2)}) collective-permute-start(bf16[4,384,128]{2,1,0:T(8,128)(2,1)} %get-tuple-element.49), channel_id=1, source_target_pairs={{0,1},{1,0},{2,3},{3,2},{4,5},{5,4},{6,7},{7,6},{8,9},{9,8},{10,11... | collective-permute-start | bytes 1179656 | tf_op jit(solution)/shard_map/ppermute | solution.py:254
  146.6 34.9 %collective-permute-start.11 = (bf16[4,384,128]{2,1,0:T(8,128)(2,1)}, bf16[4,384,128]{2,1,0:T(8,128)(2,1)S(1)}, u32[]{:S(2)}, u32[]{:S(2)}) collective-permute-start(bf16[4,384,128]{2,1,0:T(8,128)(2,1)} %get-tuple-element.50), channel_id=1, source_target_pairs={{0,2},{1,3},{2,0},{3,1},{4,6},{5,7},{6,4},{7,5},{8,10},{9,11},{10,... | collective-permute-start | bytes 1179656 | tf_op jit(solution)/shard_map/ppermute | solution.py:254
  148.1 33.5 %collective-permute-start.12 = (bf16[4,384,128]{2,1,0:T(8,128)(2,1)}, bf16[4,384,128]{2,1,0:T(8,128)(2,1)S(1)}, u32[]{:S(2)}, u32[]{:S(2)}) collective-permute-start(bf16[4,384,128]{2,1,0:T(8,128)(2,1)} %get-tuple-element.51), channel_id=1, source_target_pairs={{0,3},{1,2},{2,1},{3,0},{4,7},{5,6},{6,5},{7,4},{8,11},{9,10},{10,... | collective-permute-start | bytes 1179656 | tf_op jit(solution)/shard_map/ppermute | solution.py:254
  148.5 1.0 copy-start.5
  149.5 1.0 copy-start.8
  150.4 31.1 %copy-start.9 = (bf16[4,384,128]{2,1,0:T(8,128)(2,1)S(1)}, bf16[4,384,128]{2,1,0:T(8,128)(2,1)}, u32[]{:S(2)}) copy-start(bf16[4,384,128]{2,1,0:T(8,128)(2,1)} %get-tuple-element.46.refs_3_.refs_0_) | copy-start | bytes 1179652
  165.8 31.1 %copy-start.3 = (bf16[4,384,128]{2,1,0:T(8,128)(2,1)}, bf16[4,384,128]{2,1,0:T(8,128)(2,1)S(1)}, u32[]{:S(2)}) copy-start(bf16[4,384,128]{2,1,0:T(8,128)(2,1)S(1)} %collective-permute-done.13.refs_5_.refs_1_) | copy-start | bytes 1179652
  165.8 31.1 %collective-permute-start.16 = (bf16[4,384,128]{2,1,0:T(8,128)(2,1)}, bf16[4,384,128]{2,1,0:T(8,128)(2,1)S(1)}, u32[]{:S(2)}, u32[]{:S(2)}) collective-permute-start(bf16[4,384,128]{2,1,0:T(8,128)(2,1)} %get-tuple-element.57), channel_id=1, source_target_pairs={{0,12},{1,13},{2,14},{3,15},{4,8},{5,9},{6,10},{7,11},{8,4},{9,5},... | collective-permute-start | bytes 1179656 | tf_op jit(solution)/shard_map/ppermute | solution.py:254
  168.5 33.9 %all-to-all-start.3 = ((bf16[16,128,128]{2,1,0:T(8,128)(2,1)}), bf16[16,128,128]{2,1,0:T(8,128)(2,1)S(1)}, u32[]{:S(2)}, u32[]{:S(2)}) async-start(bf16[16,128,128]{2,1,0:T(8,128)(2,1)} %attend.5.refs_4_), calls=%async_computation.3 | async-start | bytes 1048576 | tf_op jit(solution)/shard_map/all_to_all | solution.py:299
  196.9 0.8 copy-start.17
  200.3 8.9 %collective-permute-start.17 = (bf16[4,384,128]{2,1,0:T(8,128)(2,1)}, bf16[4,384,128]{2,1,0:T(8,128)(2,1)S(1)}, u32[]{:S(2)}, u32[]{:S(2)}) collective-permute-start(bf16[4,384,128]{2,1,0:T(8,128)(2,1)} %get-tuple-element.59), channel_id=1, source_target_pairs={{0,1},{1,0},{2,3},{3,2},{4,5},{5,4},{6,7},{7,6},{8,9},{9,8},{10,11... | collective-permute-start | bytes 1179656 | tf_op jit(solution)/shard_map/ppermute | solution.py:254
  200.7 12.2 %collective-permute-start.18 = (bf16[4,384,128]{2,1,0:T(8,128)(2,1)}, bf16[4,384,128]{2,1,0:T(8,128)(2,1)S(1)}, u32[]{:S(2)}, u32[]{:S(2)}) collective-permute-start(bf16[4,384,128]{2,1,0:T(8,128)(2,1)} %get-tuple-element.60), channel_id=1, source_target_pairs={{0,2},{1,3},{2,0},{3,1},{4,6},{5,7},{6,4},{7,5},{8,10},{9,11},{10,... | collective-permute-start | bytes 1179656 | tf_op jit(solution)/shard_map/ppermute | solution.py:254
  202.4 22.5 %collective-permute-start.19 = (bf16[4,384,128]{2,1,0:T(8,128)(2,1)}, bf16[4,384,128]{2,1,0:T(8,128)(2,1)S(1)}, u32[]{:S(2)}, u32[]{:S(2)}) collective-permute-start(bf16[4,384,128]{2,1,0:T(8,128)(2,1)} %get-tuple-element.61), channel_id=1, source_target_pairs={{0,3},{1,2},{2,1},{3,0},{4,7},{5,6},{6,5},{7,4},{8,11},{9,10},{10,... | collective-permute-start | bytes 1179656 | tf_op jit(solution)/shard_map/ppermute | solution.py:254
  202.4 46.4 %copy-start.11 = (bf16[16,128,128]{2,1,0:T(8,128)(2,1)}, bf16[16,128,128]{2,1,0:T(8,128)(2,1)S(1)}, u32[]{:S(2)}) copy-start(bf16[16,128,128]{2,1,0:T(8,128)(2,1)S(1)} %all-to-all-done.3) | copy-start | bytes 1572868
  202.4 38.8 %all-to-all-start.4 = ((bf16[16,128,128]{2,1,0:T(8,128)(2,1)}), bf16[16,128,128]{2,1,0:T(8,128)(2,1)S(1)}, u32[]{:S(2)}, u32[]{:S(2)}) async-start(bf16[16,128,128]{2,1,0:T(8,128)(2,1)} %attend.6.refs_4_), calls=%async_computation.4 | async-start | bytes 1048576 | tf_op jit(solution)/shard_map/all_to_all | solution.py:299
  224.9 1.0 copy-start.10
  241.2 47.7 %copy-start.12 = (bf16[16,128,128]{2,1,0:T(8,128)(2,1)}, bf16[16,128,128]{2,1,0:T(8,128)(2,1)S(1)}, u32[]{:S(2)}) copy-start(bf16[16,128,128]{2,1,0:T(8,128)(2,1)S(1)} %all-to-all-done.4) | copy-start | bytes 1572868
  241.2 21.3 %all-to-all-start.5 = ((bf16[16,128,128]{2,1,0:T(8,128)(2,1)}), bf16[16,128,128]{2,1,0:T(8,128)(2,1)S(1)}, u32[]{:S(2)}, u32[]{:S(2)}) async-start(bf16[16,128,128]{2,1,0:T(8,128)(2,1)} %attend.7), calls=%async_computation.5 | async-start | bytes 1048576 | tf_op jit(solution)/shard_map/all_to_all | solution.py:299
  248.1 36.4 %all-gather.7.cloned.1.call-start = ((), (), s32[]{:S(2)}) async-start(), calls=%async_computation.7 | async-start | bytes 1572864 | tf_op jit(solution)/shard_map/all_gather | solution.py:302
  248.9 40.1 %collective-permute-start.9 = (bf16[1,16,128,128]{3,2,1,0:T(8,128)(2,1)S(1)}, bf16[1,16,128,128]{3,2,1,0:T(8,128)(2,1)S(1)}, u32[]{:S(2)}, u32[]{:S(2)}) collective-permute-start(bf16[1,16,128,128]{3,2,1,0:T(8,128)(2,1)S(1)} %bitcast.17), channel_id=1, source_target_pairs={{0,16},{16,0},{1,17},{17,1},{2,18},{18,2},{3,19},{19,3},{4,20},{20... | collective-permute-start | bytes 1572872 | tf_op jit(solution)/shard_map/ppermute | solution.py:254
  250.5 43.7 %collective-permute-start.14 = (bf16[1,16,128,128]{3,2,1,0:T(8,128)(2,1)S(1)}, bf16[1,16,128,128]{3,2,1,0:T(8,128)(2,1)S(1)}, u32[]{:S(2)}, u32[]{:S(2)}) collective-permute-start(bf16[1,16,128,128]{3,2,1,0:T(8,128)(2,1)S(1)} %bitcast.19), channel_id=1, source_target_pairs={{0,16},{16,0},{1,17},{17,1},{2,18},{18,2},{3,19},{19,3},{4,20},{20... | collective-permute-start | bytes 1572872 | tf_op jit(solution)/shard_map/ppermute | solution.py:254
  262.6 26.4 %copy-start.13 = (bf16[16,128,128]{2,1,0:T(8,128)(2,1)}, bf16[16,128,128]{2,1,0:T(8,128)(2,1)S(1)}, u32[]{:S(2)}) copy-start(bf16[16,128,128]{2,1,0:T(8,128)(2,1)S(1)} %all-to-all-done.5) | copy-start | bytes 1572868
  262.6 36.8 %collective-permute-start.20 = (bf16[1,16,128,128]{3,2,1,0:T(8,128)(2,1)S(1)}, bf16[1,16,128,128]{3,2,1,0:T(8,128)(2,1)S(1)}, u32[]{:S(2)}, u32[]{:S(2)}) collective-permute-start(bf16[1,16,128,128]{3,2,1,0:T(8,128)(2,1)S(1)} %bitcast.21), channel_id=1, source_target_pairs={{0,16},{16,0},{1,17},{17,1},{2,18},{18,2},{3,19},{19,3},{4,20},{20... | collective-permute-start | bytes 1572872 | tf_op jit(solution)/shard_map/ppermute | solution.py:254
  289.0 0.8 copy-start.16
  294.2 0.8 copy-start.15
  299.4 0.8 copy-start.14
Sparse Core Ops, SparseCore 0:
  9.5 59.4 all-gather.4
  250.5 33.9 all-gather.6
